TPU v7x, 32 devices: a whole 2x2x4 slice. The times are simulated.
32 devices in a mesh: expert: 8 (over y, x, core), rep: 4 (over z).
Axes of the slice: x: 2, y: 2, z: 4, core: 2. Of those that a mesh axis runs over, the one named last changes fastest.
Arguments:
- descriptors: bfloat16 [1024, 1024], P(('expert', 'rep')), may hold values from -6 to 6
- expert_ids: int32 [1024, 1], P(('expert', 'rep')), may hold values from 0 to 7; in each aligned block of 32 rows (0 to 31, 32 to 63, ...) at most 12 rows name the same one
- cotangent: bfloat16 [1024], P(('expert', 'rep')), may hold values from -6 to 6
- w1: bfloat16 [8, 1024, 2048], P('expert'), may hold values from -0.1875 to 0.1875
- w2: bfloat16 [8, 2048], P('expert'), may hold values from -0.59765625 to 0.59765625
Outputs:
- energies: bfloat16 [1024], P(('expert', 'rep'))
- descriptor_grad: bfloat16 [1024, 1024], P(('expert', 'rep'))
- w1_grad: bfloat16 [8, 2048, 1024], P('expert', 'rep')
- w2_grad: float32 [8, 2048], P('expert')
Inputs may be any that keep to these rules, and one draw needn't show every extreme that they name: `expert_ids`: within the rows of one device (aligned blocks of 32 atoms) no expert id occurs more than 12 times, and some id occurs exactly 12 times.
All inputs are finite; a program needn't handle non-finite values.
Results may differ from a plain program's by a relative error of at most 0.022.
Values may be sent and summed in bfloat16 or wider, within the bound.
No kernel may reach another device: no remote copies, remote signals or barrier semaphores. Data moves between devices by JAX's collectives and lax.ppermute only.
A program may use at most 128 MiB of HBM per device.

v0:
```python
import jax
import jax.numpy as jnp
from jax import lax
from jax.sharding import PartitionSpec as P

CAP = 12


def on_device(descriptors, expert_ids, cotangent, w1, w2):
    owners = lax.axis_size("expert")
    columns = descriptors.shape[1]
    slot_count = owners * CAP
    targets = expert_ids[:, 0]
    member = (targets[:, None] == jnp.arange(owners, dtype=jnp.int32)[None, :]).astype(jnp.int32)
    slot_rank = jnp.sum((jnp.cumsum(member, axis=0) - 1) * member, axis=1)
    placement = (
        (targets * CAP + slot_rank)[:, None] == jnp.arange(slot_count, dtype=jnp.int32)[None, :]
    ).astype(jnp.bfloat16)
    contract_rows = (((0,), (0,)), ((), ()))
    packed = lax.dot_general(
        placement, descriptors, contract_rows, preferred_element_type=jnp.float32
    ).astype(jnp.bfloat16)
    packed_cot = lax.dot_general(
        placement, cotangent, contract_rows, preferred_element_type=jnp.float32
    ).astype(jnp.bfloat16)
    arrived, arrived_cot = (
        lax.all_to_all(
            packed.reshape(owners, CAP, columns), "expert", split_axis=0, concat_axis=0, tiled=True
        ),
        lax.all_to_all(
            packed_cot.reshape(owners, CAP), "expert", split_axis=0, concat_axis=0, tiled=True
        ),
    )
    slot_rows = arrived.reshape(slot_count, columns)
    slot_cot = arrived_cot.reshape(slot_count).astype(jnp.float32)
    weight = w1[0]
    readout = w2[0].astype(jnp.float32)
    preact = jnp.dot(slot_rows, weight, preferred_element_type=jnp.float32)
    gate_sig = jax.nn.sigmoid(preact)
    activated = preact * gate_sig
    energy = jnp.sum(activated * readout, axis=1).astype(jnp.bfloat16)
    hidden_grad = (
        slot_cot[:, None] * readout * gate_sig * (1.0 + preact * (1.0 - gate_sig))
    ).astype(jnp.bfloat16)
    input_grad = lax.dot_general(
        hidden_grad, weight, (((1,), (1,)), ((), ())), preferred_element_type=jnp.float32
    ).astype(jnp.bfloat16)
    returned, returned_energy = (
        lax.all_to_all(
            input_grad.reshape(owners, CAP, columns),
            "expert",
            split_axis=0,
            concat_axis=0,
            tiled=True,
        ),
        lax.all_to_all(
            energy.reshape(owners, CAP), "expert", split_axis=0, concat_axis=0, tiled=True
        ),
    )
    energies = jnp.dot(
        placement, returned_energy.reshape(slot_count), preferred_element_type=jnp.float32
    ).astype(jnp.bfloat16)
    descriptor_grad = jnp.dot(
        placement, returned.reshape(slot_count, columns), preferred_element_type=jnp.float32
    ).astype(jnp.bfloat16)
    readout_grad = lax.psum(jnp.sum(slot_cot[:, None] * activated, axis=0), "rep")
    weight_band = lax.psum_scatter(
        lax.dot_general(
            hidden_grad, slot_rows, contract_rows, preferred_element_type=jnp.float32
        ).astype(jnp.bfloat16),
        "rep",
        scatter_dimension=0,
        tiled=True,
    )
    w1_grad = weight_band[None]
    w2_grad = readout_grad[None]
    return (energies, descriptor_grad, w1_grad, w2_grad)


def solution(mesh):
    in_specs = (
        P(("expert", "rep"), None),
        P(("expert", "rep"), None),
        P(("expert", "rep")),
        P("expert", None, None),
        P("expert", None),
    )
    out_specs = (
        P(("expert", "rep")),
        P(("expert", "rep"), None),
        P("expert", "rep", None),
        P("expert", None),
    )
    return jax.shard_map(
        on_device, mesh=mesh, in_specs=in_specs, out_specs=out_specs, check_vma=False
    )
```

profile of v0, /device:TPU:0, one launch (start us, length us, event | category | flops | bytes accessed | tf_op | source)
XLA Modules:
  0.0 121.4 jit_solution(2924903781671662333)
XLA Ops:
  7.2 0.0 copy-start
  7.2 0.8 fusion.10
  7.9 0.1 reduce_window_sum.11
  8.0 0.8 select_reduce_fusion
  8.8 0.7 fusion.15
  9.5 0.8 fusion.8
  10.3 0.7 all_to_all.21
  11.0 5.2 %all-to-all-start.2 = ((bf16[8,1,12]{2,1,0:T(2,128)(2,1)}), bf16[8,1,12]{2,1,0:T(2,128)(2,1)S(1)}, u32[]{:S(2)}, u32[]{:S(2)}) async-start(bf16[8,1,12]{2,1,0:T(2,128)(2,1)} %all_to_all.21), calls=%async_computation.2 | async-start | bytes 8192 | tf_op jit(solution)/shard_map/all_to_all | solution.py:30
  16.2 0.0 copy-done
  16.2 0.3 convolution_convert_fusion.1
  16.5 0.7 reshape.53
  17.3 3.5 %all-to-all-done.2 = bf16[8,1,12]{2,1,0:T(2,128)(2,1)S(1)} async-done(((bf16[8,1,12]{2,1,0:T(2,128)(2,1)}), bf16[8,1,12]{2,1,0:T(2,128)(2,1)S(1)}, u32[]{:S(2)}, u32[]{:S(2)}) %all-to-all-start.2) | async-done | bytes 224 | tf_op jit(solution)/shard_map/all_to_all | solution.py:30
  20.8 3.4 %all-to-all-start = ((bf16[8,12,1024]{2,1,0:T(8,128)(2,1)}), bf16[8,12,1024]{2,1,0:T(8,128)(2,1)S(1)}, u32[]{:S(2)}, u32[]{:S(2)}) async-start(bf16[8,12,1024]{2,1,0:T(8,128)(2,1)} %reshape.53), calls=%async_computation | async-start | bytes 524288 | tf_op jit(solution)/shard_map/all_to_all | solution.py:27
  24.2 0.0 reduce-scatter.2.cloned.1.call-start
  24.3 0.7 mul.66
  25.0 0.1 reshape.59
  25.1 6.0 %all-to-all-done = bf16[8,12,1024]{2,1,0:T(8,128)(2,1)S(1)} async-done(((bf16[8,12,1024]{2,1,0:T(8,128)(2,1)}), bf16[8,12,1024]{2,1,0:T(8,128)(2,1)S(1)}, u32[]{:S(2)}, u32[]{:S(2)}) %all-to-all-start) | async-done | bytes 196640 | tf_op jit(solution)/shard_map/all_to_all | solution.py:27
  31.1 3.3 %multiply_reduce_fusion = (f32[2048]{0:T(1024)S(1)}, bf16[96]{0:T(256)(128)(2,1)S(1)}, f32[96,2048]{1,0:T(8,128)S(1)}) fusion(f32[96]{0:T(128)S(1)} %reshape.59, f32[2048]{0:T(1024)S(1)} %bitcast.35, bf16[96,1024]{1,0:T(8,128)(2,1)S(1)} %reshape.54, bf16[1,1024,2048]{2,1,0:T(8,128)(2,1)} %param.8), kind=kOutput, calls=%fused_computation.12 | convolution fusion | flops 404223904 | bytes 5194304 | tf_op jit(solution)/shard_map/dot_general | solution.py:38
  34.4 3.4 %convolution_convert_fusion = bf16[2048,1024]{1,0:T(8,128)(2,1)} fusion(bf16[96,1024]{1,0:T(8,128)(2,1)S(1)} %reshape.54, f32[96,2048]{1,0:T(8,128)S(1)} %get-tuple-element.6, f32[96]{0:T(128)S(1)} %reshape.59, f32[2048]{0:T(1024)S(1)} %bitcast.36), kind=kOutput, calls=%fused_computation.4 | convolution fusion | flops 406716416 | bytes 5185920 | tf_op jit(solution)/shard_map/dot_general | solution.py:68
  37.7 0.0 reduce-scatter.2.cloned.1.call-update
  37.8 0.7 convert_element_type.64
  38.4 3.3 %all-to-all-start.1 = ((bf16[8,1,12]{2,1,0:T(2,128)(2,1)}), bf16[8,1,12]{2,1,0:T(2,128)(2,1)S(1)}, u32[]{:S(2)}, u32[]{:S(2)}) async-start(bf16[8,1,12]{2,1,0:T(2,128)(2,1)} %convert_element_type.64), calls=%async_computation.1 | async-start | bytes 8192 | tf_op jit(solution)/shard_map/all_to_all | solution.py:56
  41.8 4.4 %fusion.4 = bf16[96,1024]{1,0:T(8,128)(2,1)S(1)} fusion(bf16[1,1024,2048]{2,1,0:T(8,128)(2,1)} %param.8, f32[96,2048]{1,0:T(8,128)S(1)} %get-tuple-element.6, f32[96]{0:T(128)S(1)} %reshape.59, f32[2048]{0:T(1024)S(1)} %bitcast.37), kind=kOutput, calls=%fused_computation.6 | convolution fusion | flops 404717568 | bytes 5185920 | tf_op jit(solution)/shard_map/dot_general | solution.py:45
  46.1 13.2 %psum.7 = f32[1,2048]{1,0:T(1,128)} all-reduce(f32[1,2048]{1,0:T(1,128)S(1)} %bitcast.38), channel_id=1, replica_groups=mesh['expert'=8,'rep'=4] {'rep'}, use_global_device_ids=true, to_apply=%region_5.6 | all-reduce | flops 2048 | bytes 16384 | tf_op jit(solution)/shard_map/psum | solution.py:66
  59.3 0.7 reshape.56
  60.0 0.0 all-to-all-done.1
  60.0 4.4 %all-to-all-start.3 = ((bf16[8,12,1024]{2,1,0:T(8,128)(2,1)}), bf16[8,12,1024]{2,1,0:T(8,128)(2,1)S(1)}, u32[]{:S(2)}, u32[]{:S(2)}) async-start(bf16[8,12,1024]{2,1,0:T(8,128)(2,1)} %reshape.56), calls=%async_computation.3 | async-start | bytes 524288 | tf_op jit(solution)/shard_map/all_to_all | solution.py:49
  64.4 0.1 reshape.60
  64.5 0.7 fusion.7
  65.3 6.1 %all-to-all-done.3 = bf16[8,12,1024]{2,1,0:T(8,128)(2,1)S(1)} async-done(((bf16[8,12,1024]{2,1,0:T(8,128)(2,1)}), bf16[8,12,1024]{2,1,0:T(8,128)(2,1)S(1)}, u32[]{:S(2)}, u32[]{:S(2)}) %all-to-all-start.3) | async-done | bytes 196640 | tf_op jit(solution)/shard_map/all_to_all | solution.py:49
  71.4 0.8 convolution_convert_fusion.2
  72.3 42.3 %reduce-scatter.2.cloned.1.call-done = bf16[512,1024]{1,0:T(8,128)(2,1)} async-done(((bf16[2048,1024]{1,0:T(8,128)(2,1)}), bf16[512,1024]{1,0:T(8,128)(2,1)}) %reduce-scatter.2.cloned.1.call-update) | async-done | bytes 1048592 | tf_op jit(solution)/shard_map/reduce_scatter | solution.py:67
  (4 shorter events, 0.1 us)
Async XLA Ops:
  7.2 9.0 %copy-start = (bf16[32,1024]{1,0:T(8,128)(2,1)S(1)}, bf16[32,1024]{1,0:T(8,128)(2,1)}, u32[]{:S(2)}) copy-start(bf16[32,1024]{1,0:T(8,128)(2,1)} %param.5) | copy-start | bytes 196612
  11.0 9.8 %all-to-all-start.2 = ((bf16[8,1,12]{2,1,0:T(2,128)(2,1)}), bf16[8,1,12]{2,1,0:T(2,128)(2,1)S(1)}, u32[]{:S(2)}, u32[]{:S(2)}) async-start(bf16[8,1,12]{2,1,0:T(2,128)(2,1)} %all_to_all.21), calls=%async_computation.2 | async-start | bytes 8192 | tf_op jit(solution)/shard_map/all_to_all | solution.py:30
  20.8 10.3 %all-to-all-start = ((bf16[8,12,1024]{2,1,0:T(8,128)(2,1)}), bf16[8,12,1024]{2,1,0:T(8,128)(2,1)S(1)}, u32[]{:S(2)}, u32[]{:S(2)}) async-start(bf16[8,12,1024]{2,1,0:T(8,128)(2,1)} %reshape.53), calls=%async_computation | async-start | bytes 524288 | tf_op jit(solution)/shard_map/all_to_all | solution.py:27
  24.2 90.4 %reduce-scatter.2.cloned.1.call-start = ((), (), s32[]{:S(2)}) async-start(), calls=%async_computation.5 | async-start | bytes 5242880 | tf_op jit(solution)/shard_map/reduce_scatter | solution.py:67
  38.4 21.6 %all-to-all-start.1 = ((bf16[8,1,12]{2,1,0:T(2,128)(2,1)}), bf16[8,1,12]{2,1,0:T(2,128)(2,1)S(1)}, u32[]{:S(2)}, u32[]{:S(2)}) async-start(bf16[8,1,12]{2,1,0:T(2,128)(2,1)} %convert_element_type.64), calls=%async_computation.1 | async-start | bytes 8192 | tf_op jit(solution)/shard_map/all_to_all | solution.py:56
  60.0 11.4 %all-to-all-start.3 = ((bf16[8,12,1024]{2,1,0:T(8,128)(2,1)}), bf16[8,12,1024]{2,1,0:T(8,128)(2,1)S(1)}, u32[]{:S(2)}, u32[]{:S(2)}) async-start(bf16[8,12,1024]{2,1,0:T(8,128)(2,1)} %reshape.56), calls=%async_computation.3 | async-start | bytes 524288 | tf_op jit(solution)/shard_map/all_to_all | solution.py:49
Sparse Core Ops, SparseCore 0:
  37.9 76.6 reduce-scatter.1
where the time goes:
time: 122 us; the launch traced here: 121 us
  waiting for transfers between devices  57.9 us (47%)
  starting transfers between devices  16.4 us (13%)
  between operations  14.1 us (12%)
  matrix products  13.7 us (11%)
  blocking collectives  13.2 us (11%)
  local copies, waits for them, and re-layouts  3.12 us (3%)
  other arithmetic  3.06 us (3%)
    reduce_scatter x1, waiting for transfers between devices, on_device(): lax.psum_scatter(lax.dot_general(hidden_grad, slot_rows, contract_rows, p...  42.3 us
    psum x1, blocking collectives, on_device(): lax.psum(jnp.sum(slot_cot[:, None] * activated, axis=0), 'rep')  13.2 us
    all_to_all x1, waiting for transfers between devices, on_device(): lax.all_to_all(input_grad.reshape(owners, CAP, columns), 'expert', split_...  6.11 us
    all_to_all x1, waiting for transfers between devices, on_device(): lax.all_to_all(packed.reshape(owners, CAP, columns), 'expert', split_axis...  6 us
    all_to_all x1, starting transfers between devices, on_device(): lax.all_to_all(packed_cot.reshape(owners, CAP), 'expert', split_axis=0, c...  5.17 us
    all_to_all x1, starting transfers between devices, on_device(): lax.all_to_all(input_grad.reshape(owners, CAP, columns), 'expert', split_...  4.42 us
    dot_general x1, matrix products, on_device(): lax.dot_general(hidden_grad, weight, (((1,), (1,)), ((), ())), preferred_...  4.35 us
    all_to_all x1, waiting for transfers between devices, on_device(): lax.all_to_all(packed_cot.reshape(owners, CAP), 'expert', split_axis=0, c...  3.51 us
  transfers between devices with their start and end apart: 5, of which 4 were waited for; matrix products, arithmetic and copies ran while one was open for 8% of the time, Pallas kernels for 0%

commit v1 on v0

v1 whole, which is shorter than its diff:
```python
import functools

import jax
import jax.numpy as jnp
from jax import lax
from jax.experimental import pallas as pl
from jax.experimental.pallas import tpu as pltpu
from jax.sharding import PartitionSpec as P

CAP = 12
LANES = 128
PLANE_ROWS = 512
F32, BF16 = jnp.float32, jnp.bfloat16
VMEM = pl.BlockSpec(memory_space=pltpu.VMEM)
SMEM = pl.BlockSpec(memory_space=pltpu.SMEM)


def call(kernel, out_shape, operands, scratch=(), flops=0, scalars=0):
    moved = sum(x.size * x.dtype.itemsize for x in jax.tree.leaves((out_shape, operands)))
    return pl.pallas_call(
        kernel,
        out_shape=out_shape,
        in_specs=[SMEM] * scalars + [VMEM] * (len(operands) - scalars),
        out_specs=jax.tree.map(lambda _: VMEM, out_shape),
        scratch_shapes=list(scratch),
        cost_estimate=pl.CostEstimate(flops=flops, bytes_accessed=moved, transcendentals=0),
        compiler_params=pltpu.CompilerParams(vmem_limit_bytes=48 << 20),
    )(*operands)


def swap(x, axis, k):
    return lax.ppermute(x, axis, [(i, i ^ k) for i in range(lax.axis_size(axis))])


def iota(shape, dim):
    return lax.broadcasted_iota(jnp.int32, shape, dim)


def dot(a, b, dims=((1,), (0,))):
    return lax.dot_general(a, b, (dims, ((), ())), preferred_element_type=F32)


def label_rows(rows_ref, ids_ref, cot_ref, out_ref):
    rows, width = rows_ref.shape
    eye = iota((rows, rows), 0) == iota((rows, rows), 1)

    def column(line):
        return jnp.sum(jnp.where(eye, jnp.broadcast_to(line, (rows, rows)), 0.0), axis=1, keepdims=True)

    lane = iota((rows, LANES), 1)
    cot = column(cot_ref[...].astype(F32))
    ids = column(ids_ref[...].astype(F32))
    out_ref[:, :width] = rows_ref[...]
    out_ref[:, width:] = jnp.where(lane == 0, cot, jnp.where(lane == 1, ids, 0.0)).astype(BF16)


def gate(preact):
    sig = 1.0 / (1.0 + jnp.exp(-preact))
    return sig, preact * sig


def own_plane(n, where_ref, *refs):
    blocks, (w1_ref, w2_ref), (even_ref, odd_ref, band_ref, readout_ref), (xs, hs) = (
        refs[:n], refs[n:n + 2], refs[n + 2:n + 6], refs[n + 6:])
    rows = blocks[0].shape[0]
    width, hidden = w1_ref.shape
    band = band_ref.shape[1]
    for k in range(n):
        xs[k * rows:(k + 1) * rows, :] = blocks[k][...]
    tags = xs[:, width:].astype(F32)
    mine = tags[:, 1:2] == where_ref[0].astype(F32)
    cot = jnp.where(mine, tags[:, 0:1], 0.0)
    energy = jnp.zeros((n * rows, 1), F32)
    for c in range(0, hidden, band):
        part = slice(c, c + band)
        preact = dot(xs[:, :width], w1_ref[:, part])
        sig, act = gate(preact)
        w2 = w2_ref[:, part].astype(F32)
        energy += jnp.sum(act * w2, axis=1, keepdims=True)
        hs[:, part] = (cot * w2 * sig * (1.0 + preact * (1.0 - sig))).astype(BF16)
        readout_ref[:, part] = jnp.sum(cot * act, axis=0, keepdims=True)
    band_ref[...] = hs[:, pl.ds(pl.multiple_of(where_ref[1] * band, band), band)]
    back = dot(hs[...], w1_ref[...], ((1,), (1,))).astype(BF16)
    tail = jnp.where((iota((n * rows, LANES), 1) == 0) & mine, energy, 0.0).astype(BF16)
    for k in range(n):
        out, at, here = (odd_ref if k % 2 else even_ref), slice(k // 2 * rows, (k // 2 + 1) * rows), slice(k * rows, (k + 1) * rows)
        out[at, :width] = back[here, :]
        out[at, width:] = tail[here, :]


def pick_slots(n, where_ref, *refs):
    blocks, outs, (xs,) = refs[:n], refs[n:-1], refs[-1:]
    rows, wide = blocks[0].shape
    total = n * rows
    width = wide - LANES
    for k in range(n):
        xs[k * rows:(k + 1) * rows, :] = blocks[k][...]
    ids = xs[:, width:].astype(F32)[:, 1:2].astype(jnp.int32)
    i, j = iota((total, total), 0), iota((total, total), 1)
    before = ((j < i) & (j // rows == i // rows)).astype(BF16)
    lane = iota((total, LANES), 1)
    member = ids == (where_ref[0] ^ (2 * lane))
    rank = dot(before, member.astype(BF16))
    slot = jnp.where(member, (iota((total, LANES), 0) // rows) * CAP + rank.astype(jnp.int32), -1)
    for d, out_ref in enumerate(outs):
        size = out_ref.shape[0]
        pick = (slot[:, d:d + 1] == iota((total, size), 1)).astype(BF16)
        out_ref[...] = dot(pick, xs[...], ((0,), (0,))).astype(BF16)


def add_blocks(even_ref, odd_ref, *outs):
    rows = outs[0].shape[0]
    for k, out_ref in enumerate(outs):
        at = slice(k * rows, (k + 1) * rows)
        out_ref[...] = even_ref[at, :] + odd_ref[at, :]


def add_returned(*refs):
    parts, (grad_ref, energy_ref) = refs[:-2], refs[-2:]
    rows, width = grad_ref.shape
    total = parts[0][...].astype(F32)
    for part in parts[1:]:
        total += part[...].astype(F32)
    grad_ref[...] = total[:, :width].astype(BF16)
    eye = iota((rows, rows), 0) == iota((rows, rows), 1)
    line = jnp.sum(jnp.where(eye, total[:, width:width + 1], 0.0), axis=0, keepdims=True)
    energy_ref[...] = line.astype(BF16)


def all_replicas(n, m, where_ref, *refs):
    slots, blocks = refs[:n], refs[n:n + m]
    w1_ref, w2_ref, band_ref, readout_ref, w1_grad_ref, w2_grad_ref, ys, xs = refs[n + m:]
    size, rows = slots[0].shape[0], blocks[0].shape[0]
    width, hidden = w1_ref.shape
    band = w1_grad_ref.shape[0]
    for k in range(n):
        ys[k * size:(k + 1) * size, :] = slots[k][...]
    for k in range(m):
        xs[k * rows:(k + 1) * rows, :] = blocks[k][:, :width]
    cot = ys[:, width:].astype(F32)[:, 0:1]
    bands = hidden // band
    for j in range(bands):
        at = where_ref[1] + j
        at = jnp.where(at >= bands, at - bands, at)
        part = pl.ds(pl.multiple_of(at * band, band), band)
        preact = dot(ys[:, :width], w1_ref[:, part])
        sig, act = gate(preact)
        w2_grad_ref[:, part] = readout_ref[:, part] + jnp.sum(cot * act, axis=0, keepdims=True)
        if j == 0:
            w2 = w2_ref[:, part].astype(F32)
            hidden_grad = (cot * w2 * sig * (1.0 + preact * (1.0 - sig))).astype(BF16)
            grad = dot(hidden_grad, ys[:, :width], ((0,), (0,)))
            grad += dot(band_ref[...], xs[...], ((0,), (0,)))
            w1_grad_ref[...] = grad.astype(BF16)


def by_blocks(descriptors, expert_ids, cotangent, w1, w2):
    owners, replicas = lax.axis_size("expert"), lax.axis_size("rep")
    rows, width = descriptors.shape
    wide = width + LANES
    weight, readout = w1[0], w2
    hidden = weight.shape[1]
    band = hidden // replicas
    where = jnp.stack([lax.axis_index("expert"), lax.axis_index("rep")]).astype(jnp.int32)
    shape = jax.ShapeDtypeStruct

    own = call(
        label_rows, shape((rows, wide), BF16),
        (descriptors, expert_ids.reshape(1, rows), cotangent.reshape(1, rows)),
    )
    far = [swap(own, "rep", k) for k in range(1, replicas)]
    even = [own] + [swap(own, "expert", k) for k in range(2, owners, 2)]
    odd = [swap(block, "expert", 1) for block in even]
    blocks = [block for pair in zip(even, odd) for block in pair]

    total = owners * rows
    even_back, odd_back, band_grad, readout_part = call(
        functools.partial(own_plane, owners),
        (
            shape((total // 2, wide), BF16), shape((total // 2, wide), BF16),
            shape((total, band), BF16), shape((1, hidden), F32),
        ),
        (where, *blocks, weight, readout),
        (pltpu.VMEM((total, wide), BF16), pltpu.VMEM((total, hidden), BF16)),
        flops=4 * total * width * hidden, scalars=1,
    )

    far += [swap(block, "expert", 1) for block in far]
    size = -(-len(far) * CAP // 16) * 16
    slots = call(
        functools.partial(pick_slots, len(far)),
        [shape((size, wide), BF16)] * (owners // 2),
        (where, *far),
        (pltpu.VMEM((len(far) * rows, wide), BF16),),
        flops=owners * size * len(far) * rows * wide, scalars=1,
    )
    slots = [slots[0]] + [swap(slots[k], "expert", 2 * k) for k in range(1, owners // 2)]

    odd_back = swap(odd_back, "expert", 1)
    back = call(add_blocks, [shape((rows, wide), BF16)] * (owners // 2), (even_back, odd_back))
    back = [back[0]] + [swap(back[k], "expert", 2 * k) for k in range(1, owners // 2)]

    w1_grad, w2_grad = call(
        functools.partial(all_replicas, len(slots), owners),
        (shape((band, width), BF16), shape((1, hidden), F32)),
        (where, *slots, *blocks, weight, readout, band_grad, readout_part),
        (pltpu.VMEM((len(slots) * size, wide), BF16), pltpu.VMEM((total, width), BF16)),
        flops=2 * len(slots) * size * width * (hidden + band) + 2 * total * width * band, scalars=1,
    )
    descriptor_grad, energies = call(
        add_returned, (shape((rows, width), BF16), shape((1, rows), BF16)), tuple(back)
    )
    return energies.reshape(rows), descriptor_grad, w1_grad[None], w2_grad


def by_slots(descriptors, expert_ids, cotangent, w1, w2):
    owners = lax.axis_size("expert")
    columns = descriptors.shape[1]
    slot_count = owners * CAP
    targets = expert_ids[:, 0]
    member = (targets[:, None] == jnp.arange(owners, dtype=jnp.int32)[None, :]).astype(jnp.int32)
    slot_rank = jnp.sum((jnp.cumsum(member, axis=0) - 1) * member, axis=1)
    placement = (
        (targets * CAP + slot_rank)[:, None] == jnp.arange(slot_count, dtype=jnp.int32)[None, :]
    ).astype(BF16)
    over_rows = ((0,), (0,))

    def exchange(slots):
        parted = slots.reshape(owners, CAP, *slots.shape[1:])
        moved = lax.all_to_all(parted, "expert", split_axis=0, concat_axis=0, tiled=True)
        return moved.reshape(slots.shape)

    slot_rows = exchange(dot(placement, descriptors, over_rows).astype(BF16))
    slot_cot = exchange(dot(placement, cotangent, over_rows).astype(BF16)).astype(F32)
    weight, readout = w1[0], w2[0].astype(F32)
    preact = dot(slot_rows, weight)
    sig = jax.nn.sigmoid(preact)
    activated = preact * sig
    energy = jnp.sum(activated * readout, axis=1).astype(BF16)
    hidden_grad = (slot_cot[:, None] * readout * sig * (1.0 + preact * (1.0 - sig))).astype(BF16)
    input_grad = dot(hidden_grad, weight, ((1,), (1,))).astype(BF16)
    energies = dot(placement, exchange(energy)).astype(BF16)
    descriptor_grad = dot(placement, exchange(input_grad)).astype(BF16)
    w2_grad = lax.psum(jnp.sum(slot_cot[:, None] * activated, axis=0), "rep")
    w1_grad = lax.psum_scatter(
        dot(hidden_grad, slot_rows, over_rows).astype(BF16), "rep", scatter_dimension=0, tiled=True
    )
    return energies, descriptor_grad, w1_grad[None], w2_grad[None]


def on_device(descriptors, *rest):
    few = descriptors.shape[0] * lax.axis_size("expert") <= PLANE_ROWS
    return (by_blocks if few else by_slots)(descriptors, *rest)


def solution(mesh):
    in_specs = (
        P(("expert", "rep"), None),
        P(("expert", "rep"), None),
        P(("expert", "rep")),
        P("expert", None, None),
        P("expert", None),
    )
    out_specs = (
        P(("expert", "rep")),
        P(("expert", "rep"), None),
        P("expert", "rep", None),
        P("expert", None),
    )
    return jax.shard_map(
        on_device, mesh=mesh, in_specs=in_specs, out_specs=out_specs, check_vma=False
    )
```

time: 122 us -> 43.8 us (0.36)
  waiting for transfers between devices: 57.9 us -> 10.7 us
  matrix products: 13.7 us -> 0 us
  between operations: 14.1 us -> 0.7 us
  blocking collectives: 13.2 us -> 0 us
  Pallas kernels: 0 us -> 9.98 us
  other arithmetic: 3.06 us -> 0.07 us
  local copies, waits for them, and re-layouts: 3.12 us -> 5.03 us
    reduce_scatter x1 -> x0, waiting for transfers between devices: 42.3 us -> none  [on_device(): lax.psum_scatter(lax.dot_general(hidden_grad, slot_rows, contract_rows, p...]
    ppermute x0 -> x20, starting transfers between devices: none -> 17 us  [swap(): lax.ppermute(x, axis, [(i, i ^ k) for i in range(lax.axis_size(axis))])]
    all_to_all x4 -> x0, starting transfers between devices: 16.3 us -> none  [the longest x1 5.17 us: on_device(): lax.all_to_all(packed_cot.reshape(owners, CAP), 'expert', split_axis=0, c...]
    all_to_all x4 -> x0, waiting for transfers between devices: 15.6 us -> none  [the longest x1 6.11 us: on_device(): lax.all_to_all(input_grad.reshape(owners, CAP, columns), 'expert', split_...]
    dot_general x7 -> x0, matrix products: 13.7 us -> none  [the longest x1 4.35 us: on_device(): lax.dot_general(hidden_grad, weight, (((1,), (1,)), ((), ())), preferred_...]
    psum x1 -> x0, blocking collectives: 13.2 us -> none  [on_device(): lax.psum(jnp.sum(slot_cot[:, None] * activated, axis=0), 'rep')]
    ppermute x0 -> x20, waiting for transfers between devices: none -> 10.7 us  [swap(): lax.ppermute(x, axis, [(i, i ^ k) for i in range(lax.axis_size(axis))])]
    pallas_call x0 -> x6, Pallas kernels: none -> 9.98 us  [call(): pl.pallas_call(kernel, out_shape=out_shape, in_specs=[SMEM] * scalars + [...]
  transfers between devices with their start and end apart: 5 -> 20, of which waited for: 4 -> 7; matrix products, arithmetic and copies ran while one was open for 8% -> 0% of each run, Pallas kernels for 0% -> 21%
where the time goes in v1:
time: 43.8 us; the launch traced here: 43.4 us
  starting transfers between devices  17 us (39%)
  waiting for transfers between devices  10.7 us (24%)
  Pallas kernels  9.98 us (23%)
  local copies, waits for them, and re-layouts  5.03 us (11%)
  between operations  0.7 us (2%)
    ppermute x20, starting transfers between devices, swap(): lax.ppermute(x, axis, [(i, i ^ k) for i in range(lax.axis_size(axis))])  17 us
    ppermute x20, waiting for transfers between devices, swap(): lax.ppermute(x, axis, [(i, i ^ k) for i in range(lax.axis_size(axis))])  10.7 us
    pallas_call x6, Pallas kernels, call(): pl.pallas_call(kernel, out_shape=out_shape, in_specs=[SMEM] * scalars + [...  9.98 us
    unnamed x12, local copies, waits for them, and re-layouts  5.03 us
  transfers between devices with their start and end apart: 20, of which 7 were waited for; matrix products, arithmetic and copies ran while one was open for 0% of the time, Pallas kernels for 21%

profile of v1, /device:TPU:0, one launch (start us, length us, event | category | flops | bytes accessed | tf_op | source)
XLA Modules:
  0.0 43.4 jit_solution(12993014198958513967)
XLA Ops:
  0.6 0.8 %copy-done = bf16[32,1024]{1,0:T(8,128)(2,1)S(1)} copy-done((bf16[32,1024]{1,0:T(8,128)(2,1)S(1)}, bf16[32,1024]{1,0:T(8,128)(2,1)}, u32[]{:S(2)}) %copy-start) | copy-done | bytes 65560
  1.5 0.7 %copy-done.1 = s32[32,1]{0,1:T(1,128)S(1)} copy-done((s32[32,1]{0,1:T(1,128)S(1)}, s32[32,1]{0,1:T(1,128)}, u32[]{:S(2)}) %copy-start.1) | copy-done | bytes 152
  2.1 0.7 %copy-done.2 = bf16[32]{0:T(256)(128)(2,1)S(1)} copy-done((bf16[32]{0:T(256)(128)(2,1)S(1)}, bf16[32]{0:T(256)(128)(2,1)}, u32[]{:S(2)}) %copy-start.2) | copy-done | bytes 88
  2.8 0.1 shard_map.84.refs_0_.refs_4_
  2.9 3.0 %collective-permute-start.1 = (bf16[32,1152]{1,0:T(8,128)(2,1)S(1)}, bf16[32,1152]{1,0:T(8,128)(2,1)S(1)}, u32[]{:S(2)}, u32[]{:S(2)}) collective-permute-start(bf16[32,1152]{1,0:T(8,128)(2,1)S(1)} %shard_map.84.refs_0_.refs_4_), channel_id=1, source_target_pairs={{0,8},{4,12},{8,0},{12,4},{16,24},{20,28},{24,16},{28,20},{1,9},{5... | collective-permute-start | bytes 221192 | tf_op jit(solution)/shard_map/ppermute | solution.py:32
  5.8 1.5 %collective-permute-start.3 = (bf16[32,1152]{1,0:T(8,128)(2,1)S(1)}, bf16[32,1152]{1,0:T(8,128)(2,1)S(1)}, u32[]{:S(2)}, u32[]{:S(2)}) collective-permute-start(bf16[32,1152]{1,0:T(8,128)(2,1)S(1)} %shard_map.84.refs_0_.refs_4_), channel_id=1, source_target_pairs={{0,16},{4,20},{8,24},{12,28},{16,0},{20,4},{24,8},{28,12},{1,17},{... | collective-permute-start | bytes 221192 | tf_op jit(solution)/shard_map/ppermute | solution.py:32
  7.4 0.0 collective-permute-start.5
  7.4 0.0 collective-permute-start
  7.4 2.0 %collective-permute-start.11 = (bf16[32,1152]{1,0:T(8,128)(2,1)S(1)}, bf16[32,1152]{1,0:T(8,128)(2,1)S(1)}, u32[]{:S(2)}, u32[]{:S(2)}) collective-permute-start(bf16[32,1152]{1,0:T(8,128)(2,1)S(1)} %shard_map.84.refs_0_.refs_4_), channel_id=1, source_target_pairs={{0,1},{1,0},{2,3},{3,2},{4,5},{5,4},{6,7},{7,6},{8,9},{9,8},{10,11... | collective-permute-start | bytes 221192 | tf_op jit(solution)/shard_map/ppermute | solution.py:32
  9.4 0.0 collective-permute-done.1.refs_2_.refs_6_
  9.4 0.2 collective-permute-start.2
  9.6 0.6 %collective-permute-done.3.refs_4_.refs_8_ = bf16[32,1152]{1,0:T(8,128)(2,1)S(1)} collective-permute-done((bf16[32,1152]{1,0:T(8,128)(2,1)S(1)}, bf16[32,1152]{1,0:T(8,128)(2,1)S(1)}, u32[]{:S(2)}, u32[]{:S(2)}) %collective-permute-start.3) | collective-permute-done | bytes 73760 | tf_op jit(solution)/shard_map/ppermute | solution.py:32
  10.2 0.0 collective-permute-start.4
  10.2 2.4 %collective-permute-done.5.refs_6_.refs_10_ = bf16[32,1152]{1,0:T(8,128)(2,1)S(1)} collective-permute-done((bf16[32,1152]{1,0:T(8,128)(2,1)S(1)}, bf16[32,1152]{1,0:T(8,128)(2,1)S(1)}, u32[]{:S(2)}, u32[]{:S(2)}) %collective-permute-start.5) | collective-permute-done | bytes 73760 | tf_op jit(solution)/shard_map/ppermute | solution.py:32
  12.6 0.0 collective-permute-start.6
  12.6 0.1 pad_add_fusion.where_ref
  12.7 0.0 collective-permute-done.refs_1_.refs_5_
  12.7 2.6 %collective-permute-start.12 = (bf16[32,1152]{1,0:T(8,128)(2,1)S(1)}, bf16[32,1152]{1,0:T(8,128)(2,1)S(1)}, u32[]{:S(2)}, u32[]{:S(2)}) collective-permute-start(bf16[32,1152]{1,0:T(8,128)(2,1)S(1)} %shard_map.84.refs_0_.refs_4_), channel_id=1, source_target_pairs={{0,2},{1,3},{2,0},{3,1},{4,6},{5,7},{6,4},{7,5},{8,10},{9,11},{10,... | collective-permute-start | bytes 221192 | tf_op jit(solution)/shard_map/ppermute | solution.py:32
  15.3 0.0 collective-permute-done.2.refs_3_.refs_7_
  15.3 1.3 %collective-permute-start.13 = (bf16[32,1152]{1,0:T(8,128)(2,1)S(1)}, bf16[32,1152]{1,0:T(8,128)(2,1)S(1)}, u32[]{:S(2)}, u32[]{:S(2)}) collective-permute-start(bf16[32,1152]{1,0:T(8,128)(2,1)S(1)} %shard_map.84.refs_0_.refs_4_), channel_id=1, source_target_pairs={{0,3},{1,2},{2,1},{3,0},{4,7},{5,6},{6,5},{7,4},{8,11},{9,10},{10,... | collective-permute-start | bytes 221192 | tf_op jit(solution)/shard_map/ppermute | solution.py:32
  16.6 0.0 collective-permute-done.4.refs_5_.refs_9_
  16.6 0.0 collective-permute-done.6.refs_7_.refs_11_
  16.7 2.2 %copy-done.3 = bf16[1,1024,2048]{2,1,0:T(8,128)(2,1)S(1)} copy-done((bf16[1,1024,2048]{2,1,0:T(8,128)(2,1)S(1)}, bf16[1,1024,2048]{2,1,0:T(8,128)(2,1)}, u32[]{:S(2)}) %copy-start.3) | copy-done | bytes 4194328
  18.8 0.7 %copy-done.5 = bf16[1,2048]{1,0:T(2,128)(2,1)S(1)} copy-done((bf16[1,2048]{1,0:T(2,128)(2,1)S(1)}, bf16[1,2048]{1,0:T(2,128)(2,1)}, u32[]{:S(2)}) %copy-start.5) | copy-done | bytes 4120
  19.5 3.8 %shard_map.85 = (bf16[128,1152]{1,0:T(8,128)(2,1)S(1)}, bf16[128,1152]{1,0:T(8,128)(2,1)S(1)}, bf16[256,512]{1,0:T(8,128)(2,1)S(1)}, f32[1,2048]{1,0:T(1,128)S(1)}) custom-call(s32[2]{0:T(128)S(1)} %pad_add_fusion.where_ref, bf16[32,1152]{1,0:T(8,128)(2,1)S(1)} %shard_map.84.refs_0_.refs_4_, bf16[32,1152]{1,0:T(8,128)(2,1)S(1)} %collective-permute-done.refs_1_.refs_5_, ...), custom_call_target="tpu_custom_call" | custom-call | flops 2147483648 | bytes 5648392 | tf_op jit(solution)/shard_map/pallas_call | solution.py:20
  23.4 0.1 collective-permute-start.7
  23.4 0.0 collective-permute-done.11.refs_0_
  23.4 0.5 %collective-permute-start.14 = (bf16[32,1152]{1,0:T(8,128)(2,1)S(1)}, bf16[32,1152]{1,0:T(8,128)(2,1)S(1)}, u32[]{:S(2)}, u32[]{:S(2)}) collective-permute-start(bf16[32,1152]{1,0:T(8,128)(2,1)S(1)} %collective-permute-done.11.refs_0_), channel_id=1, source_target_pairs={{0,4},{4,0},{8,12},{12,8},{16,20},{20,16},{24,28},{28,24},{1,5},{5... | collective-permute-start | bytes 221192 | tf_op jit(solution)/shard_map/ppermute | solution.py:32
  23.9 0.0 collective-permute-done.12.refs_1_
  23.9 0.1 collective-permute-start.15
  24.0 0.4 collective-permute-start.16
  24.4 0.7 %collective-permute-done.14.refs_3_ = bf16[32,1152]{1,0:T(8,128)(2,1)S(1)} collective-permute-done((bf16[32,1152]{1,0:T(8,128)(2,1)S(1)}, bf16[32,1152]{1,0:T(8,128)(2,1)S(1)}, u32[]{:S(2)}, u32[]{:S(2)}) %collective-permute-start.14) | collective-permute-done | bytes 73760 | tf_op jit(solution)/shard_map/ppermute | solution.py:32
  25.1 0.1 collective-permute-done.15.refs_4_
  25.2 0.2 collective-permute-done.16.refs_5_
  25.4 1.5 %shard_map.88 = (bf16[80,1152]{1,0:T(8,128)(2,1)S(1)}, bf16[80,1152]{1,0:T(8,128)(2,1)S(1)}, bf16[80,1152]{1,0:T(8,128)(2,1)S(1)}, bf16[80,1152]{1,0:T(8,128)(2,1)S(1)}) custom-call(s32[2]{0:T(128)S(1)} %pad_add_fusion.where_ref, bf16[32,1152]{1,0:T(8,128)(2,1)S(1)} %collective-permute-done.11.refs_0_, bf16[32,1152]{1,0:T(8,128)(2,1)S(1)} %collective-permute-done.12.refs_1_, ...), custom_call_target="tpu_custom_call" | custom-call | flops 141557760 | bytes 1179656 | tf_op jit(solution)/shard_map/pallas_call | solution.py:20
  26.8 0.6 %collective-permute-start.17 = (bf16[80,1152]{1,0:T(8,128)(2,1)S(1)}, bf16[80,1152]{1,0:T(8,128)(2,1)S(1)}, u32[]{:S(2)}, u32[]{:S(2)}) collective-permute-start(bf16[80,1152]{1,0:T(8,128)(2,1)S(1)} %get-tuple-element.29), channel_id=1, source_target_pairs={{0,8},{4,12},{8,0},{12,4},{16,24},{20,28},{24,16},{28,20},{1,9},{5... | collective-permute-start | bytes 552968 | tf_op jit(solution)/shard_map/ppermute | solution.py:32
  27.4 0.5 %collective-permute-start.18 = (bf16[80,1152]{1,0:T(8,128)(2,1)S(1)}, bf16[80,1152]{1,0:T(8,128)(2,1)S(1)}, u32[]{:S(2)}, u32[]{:S(2)}) collective-permute-start(bf16[80,1152]{1,0:T(8,128)(2,1)S(1)} %get-tuple-element.30), channel_id=1, source_target_pairs={{0,16},{4,20},{8,24},{12,28},{16,0},{20,4},{24,8},{28,12},{1,17},{... | collective-permute-start | bytes 552968 | tf_op jit(solution)/shard_map/ppermute | solution.py:32
  28.0 2.4 %collective-permute-start.19 = (bf16[80,1152]{1,0:T(8,128)(2,1)S(1)}, bf16[80,1152]{1,0:T(8,128)(2,1)S(1)}, u32[]{:S(2)}, u32[]{:S(2)}) collective-permute-start(bf16[80,1152]{1,0:T(8,128)(2,1)S(1)} %get-tuple-element.31), channel_id=1, source_target_pairs={{0,24},{4,28},{8,16},{12,20},{16,8},{20,12},{24,0},{28,4},{1,25},{... | collective-permute-start | bytes 552968 | tf_op jit(solution)/shard_map/ppermute | solution.py:32
  30.4 0.0 collective-permute-done.7.odd_ref
  30.5 0.6 %collective-permute-start.8 = (bf16[32,1152]{1,0:T(8,128)(2,1)S(1)}, bf16[32,1152]{1,0:T(8,128)(2,1)S(1)}, u32[]{:S(2)}, u32[]{:S(2)}) collective-permute-start(bf16[32,1152]{1,0:T(8,128)(2,1)S(1)} %get-tuple-element.23), channel_id=1, source_target_pairs={{0,8},{4,12},{8,0},{12,4},{16,24},{20,28},{24,16},{28,20},{1,9},{5... | collective-permute-start | bytes 221192 | tf_op jit(solution)/shard_map/ppermute | solution.py:32
  31.1 0.5 %collective-permute-start.9 = (bf16[32,1152]{1,0:T(8,128)(2,1)S(1)}, bf16[32,1152]{1,0:T(8,128)(2,1)S(1)}, u32[]{:S(2)}, u32[]{:S(2)}) collective-permute-start(bf16[32,1152]{1,0:T(8,128)(2,1)S(1)} %get-tuple-element.24), channel_id=1, source_target_pairs={{0,16},{4,20},{8,24},{12,28},{16,0},{20,4},{24,8},{28,12},{1,17},{... | collective-permute-start | bytes 221192 | tf_op jit(solution)/shard_map/ppermute | solution.py:32
  31.6 2.8 %collective-permute-done.17.refs_1_ = bf16[80,1152]{1,0:T(8,128)(2,1)S(1)} collective-permute-done((bf16[80,1152]{1,0:T(8,128)(2,1)S(1)}, bf16[80,1152]{1,0:T(8,128)(2,1)S(1)}, u32[]{:S(2)}, u32[]{:S(2)}) %collective-permute-start.17) | collective-permute-done | bytes 184352 | tf_op jit(solution)/shard_map/ppermute | solution.py:32
  34.4 0.5 %collective-permute-start.10 = (bf16[32,1152]{1,0:T(8,128)(2,1)S(1)}, bf16[32,1152]{1,0:T(8,128)(2,1)S(1)}, u32[]{:S(2)}, u32[]{:S(2)}) collective-permute-start(bf16[32,1152]{1,0:T(8,128)(2,1)S(1)} %get-tuple-element.25), channel_id=1, source_target_pairs={{0,24},{4,28},{8,16},{12,20},{16,8},{20,12},{24,0},{28,4},{1,25},{... | collective-permute-start | bytes 221192 | tf_op jit(solution)/shard_map/ppermute | solution.py:32
  34.9 4.0 %collective-permute-done.18.refs_2_ = bf16[80,1152]{1,0:T(8,128)(2,1)S(1)} collective-permute-done((bf16[80,1152]{1,0:T(8,128)(2,1)S(1)}, bf16[80,1152]{1,0:T(8,128)(2,1)S(1)}, u32[]{:S(2)}, u32[]{:S(2)}) %collective-permute-start.18) | collective-permute-done | bytes 184352 | tf_op jit(solution)/shard_map/ppermute | solution.py:32
  38.8 0.0 collective-permute-done.19.refs_3_
  38.8 3.9 %shard_map.89 = (bf16[512,1024]{1,0:T(8,128)(2,1)}, f32[1,2048]{1,0:T(1,128)}) custom-call(s32[2]{0:T(128)S(1)} %pad_add_fusion.where_ref, bf16[80,1152]{1,0:T(8,128)(2,1)S(1)} %get-tuple-element.28.refs_0_, bf16[80,1152]{1,0:T(8,128)(2,1)S(1)} %collective-permute-done.17.refs_1_, bf16[80,1152]{1,0:T(8,128)(2,1)S(1)} %collective-permute-done.18.refs_2_, ...), custom_call_target="tpu_custom_call" | custom-call | flops 1946157056 | bytes 6852616 | tf_op jit(solution)/shard_map/pallas_call | solution.py:20
  42.8 0.0 collective-permute-done.10.refs_3_
  42.8 0.7 %shard_map.87 = (bf16[32,1024]{1,0:T(8,128)(2,1)}, bf16[1,32]{1,0:T(2,128)(2,1)}) custom-call(bf16[32,1152]{1,0:T(8,128)(2,1)S(1)} %get-tuple-element.22.refs_0_, bf16[32,1152]{1,0:T(8,128)(2,1)S(1)} %collective-permute-done.8.refs_1_, bf16[32,1152]{1,0:T(8,128)(2,1)S(1)} %collective-permute-done.9.refs_2_, bf16[32,1152]{1,0:T(8,128)(2,1)S(1)} %collective-permute-done.10.refs_3_), custom_call_target="tpu_custom_call" | custom-call | bytes 360512 | tf_op jit(solution)/shard_map/pallas_call | solution.py:20
  (11 shorter events, 0.1 us)
Async XLA Ops:
  0.6 0.8 %copy-start = (bf16[32,1024]{1,0:T(8,128)(2,1)S(1)}, bf16[32,1024]{1,0:T(8,128)(2,1)}, u32[]{:S(2)}) copy-start(bf16[32,1024]{1,0:T(8,128)(2,1)} %rows_ref.1) | copy-start | bytes 196612
  1.5 0.7 %copy-start.1 = (s32[32,1]{0,1:T(1,128)S(1)}, s32[32,1]{0,1:T(1,128)}, u32[]{:S(2)}) copy-start(s32[32,1]{0,1:T(1,128)} %param.6) | copy-start | bytes 388
  2.1 0.7 %copy-start.2 = (bf16[32]{0:T(256)(128)(2,1)S(1)}, bf16[32]{0:T(256)(128)(2,1)}, u32[]{:S(2)}) copy-start(bf16[32]{0:T(256)(128)(2,1)} %param.7) | copy-start | bytes 196
  2.9 6.5 %collective-permute-start.1 = (bf16[32,1152]{1,0:T(8,128)(2,1)S(1)}, bf16[32,1152]{1,0:T(8,128)(2,1)S(1)}, u32[]{:S(2)}, u32[]{:S(2)}) collective-permute-start(bf16[32,1152]{1,0:T(8,128)(2,1)S(1)} %shard_map.84.refs_0_.refs_4_), channel_id=1, source_target_pairs={{0,8},{4,12},{8,0},{12,4},{16,24},{20,28},{24,16},{28,20},{1,9},{5... | collective-permute-start | bytes 221192 | tf_op jit(solution)/shard_map/ppermute | solution.py:32
  5.8 4.4 %collective-permute-start.3 = (bf16[32,1152]{1,0:T(8,128)(2,1)S(1)}, bf16[32,1152]{1,0:T(8,128)(2,1)S(1)}, u32[]{:S(2)}, u32[]{:S(2)}) collective-permute-start(bf16[32,1152]{1,0:T(8,128)(2,1)S(1)} %shard_map.84.refs_0_.refs_4_), channel_id=1, source_target_pairs={{0,16},{4,20},{8,24},{12,28},{16,0},{20,4},{24,8},{28,12},{1,17},{... | collective-permute-start | bytes 221192 | tf_op jit(solution)/shard_map/ppermute | solution.py:32
  7.4 5.3 %collective-permute-start.5 = (bf16[32,1152]{1,0:T(8,128)(2,1)S(1)}, bf16[32,1152]{1,0:T(8,128)(2,1)S(1)}, u32[]{:S(2)}, u32[]{:S(2)}) collective-permute-start(bf16[32,1152]{1,0:T(8,128)(2,1)S(1)} %shard_map.84.refs_0_.refs_4_), channel_id=1, source_target_pairs={{0,24},{4,28},{8,16},{12,20},{16,8},{20,12},{24,0},{28,4},{1,25},{... | collective-permute-start | bytes 221192 | tf_op jit(solution)/shard_map/ppermute | solution.py:32
  7.4 5.3 %collective-permute-start = (bf16[32,1152]{1,0:T(8,128)(2,1)S(1)}, bf16[32,1152]{1,0:T(8,128)(2,1)S(1)}, u32[]{:S(2)}, u32[]{:S(2)}) collective-permute-start(bf16[32,1152]{1,0:T(8,128)(2,1)S(1)} %shard_map.84.refs_0_.refs_4_), channel_id=1, source_target_pairs={{0,4},{4,0},{8,12},{12,8},{16,20},{20,16},{24,28},{28,24},{1,5},{5... | collective-permute-start | bytes 221192 | tf_op jit(solution)/shard_map/ppermute | solution.py:32
  7.4 16.0 %collective-permute-start.11 = (bf16[32,1152]{1,0:T(8,128)(2,1)S(1)}, bf16[32,1152]{1,0:T(8,128)(2,1)S(1)}, u32[]{:S(2)}, u32[]{:S(2)}) collective-permute-start(bf16[32,1152]{1,0:T(8,128)(2,1)S(1)} %shard_map.84.refs_0_.refs_4_), channel_id=1, source_target_pairs={{0,1},{1,0},{2,3},{3,2},{4,5},{5,4},{6,7},{7,6},{8,9},{9,8},{10,11... | collective-permute-start | bytes 221192 | tf_op jit(solution)/shard_map/ppermute | solution.py:32
  9.4 5.9 %collective-permute-start.2 = (bf16[32,1152]{1,0:T(8,128)(2,1)S(1)}, bf16[32,1152]{1,0:T(8,128)(2,1)S(1)}, u32[]{:S(2)}, u32[]{:S(2)}) collective-permute-start(bf16[32,1152]{1,0:T(8,128)(2,1)S(1)} %collective-permute-done.1.refs_2_.refs_6_), channel_id=1, source_target_pairs={{0,4},{4,0},{8,12},{12,8},{16,20},{20,16},{24,28},{28,24},{1,5},{5... | collective-permute-start | bytes 221192 | tf_op jit(solution)/shard_map/ppermute | solution.py:32
  10.2 6.4 %collective-permute-start.4 = (bf16[32,1152]{1,0:T(8,128)(2,1)S(1)}, bf16[32,1152]{1,0:T(8,128)(2,1)S(1)}, u32[]{:S(2)}, u32[]{:S(2)}) collective-permute-start(bf16[32,1152]{1,0:T(8,128)(2,1)S(1)} %collective-permute-done.3.refs_4_.refs_8_), channel_id=1, source_target_pairs={{0,4},{4,0},{8,12},{12,8},{16,20},{20,16},{24,28},{28,24},{1,5},{5... | collective-permute-start | bytes 221192 | tf_op jit(solution)/shard_map/ppermute | solution.py:32
  12.6 4.0 %collective-permute-start.6 = (bf16[32,1152]{1,0:T(8,128)(2,1)S(1)}, bf16[32,1152]{1,0:T(8,128)(2,1)S(1)}, u32[]{:S(2)}, u32[]{:S(2)}) collective-permute-start(bf16[32,1152]{1,0:T(8,128)(2,1)S(1)} %collective-permute-done.5.refs_6_.refs_10_), channel_id=1, source_target_pairs={{0,4},{4,0},{8,12},{12,8},{16,20},{20,16},{24,28},{28,24},{1,5},{5... | collective-permute-start | bytes 221192 | tf_op jit(solution)/shard_map/ppermute | solution.py:32
  12.7 11.2 %collective-permute-start.12 = (bf16[32,1152]{1,0:T(8,128)(2,1)S(1)}, bf16[32,1152]{1,0:T(8,128)(2,1)S(1)}, u32[]{:S(2)}, u32[]{:S(2)}) collective-permute-start(bf16[32,1152]{1,0:T(8,128)(2,1)S(1)} %shard_map.84.refs_0_.refs_4_), channel_id=1, source_target_pairs={{0,2},{1,3},{2,0},{3,1},{4,6},{5,7},{6,4},{7,5},{8,10},{9,11},{10,... | collective-permute-start | bytes 221192 | tf_op jit(solution)/shard_map/ppermute | solution.py:32
  15.3 8.7 %collective-permute-start.13 = (bf16[32,1152]{1,0:T(8,128)(2,1)S(1)}, bf16[32,1152]{1,0:T(8,128)(2,1)S(1)}, u32[]{:S(2)}, u32[]{:S(2)}) collective-permute-start(bf16[32,1152]{1,0:T(8,128)(2,1)S(1)} %shard_map.84.refs_0_.refs_4_), channel_id=1, source_target_pairs={{0,3},{1,2},{2,1},{3,0},{4,7},{5,6},{6,5},{7,4},{8,11},{9,10},{10,... | collective-permute-start | bytes 221192 | tf_op jit(solution)/shard_map/ppermute | solution.py:32
  16.7 2.2 %copy-start.3 = (bf16[1,1024,2048]{2,1,0:T(8,128)(2,1)S(1)}, bf16[1,1024,2048]{2,1,0:T(8,128)(2,1)}, u32[]{:S(2)}) copy-start(bf16[1,1024,2048]{2,1,0:T(8,128)(2,1)} %param.8) | copy-start | bytes 12582916
  18.8 0.7 %copy-start.5 = (bf16[1,2048]{1,0:T(2,128)(2,1)S(1)}, bf16[1,2048]{1,0:T(2,128)(2,1)}, u32[]{:S(2)}) copy-start(bf16[1,2048]{1,0:T(2,128)(2,1)} %refs_13_.1) | copy-start | bytes 12292
  19.5 19.3 %copy-start.4 = (bf16[1,1024,2048]{2,1,0:T(8,128)(2,1)S(1)}, bf16[1,1024,2048]{2,1,0:T(8,128)(2,1)}, u32[]{:S(2)}) copy-start(bf16[1,1024,2048]{2,1,0:T(8,128)(2,1)} %param.8) | copy-start | bytes 12582916
  23.4 7.1 %collective-permute-start.7 = (bf16[128,1152]{1,0:T(8,128)(2,1)S(1)}, bf16[128,1152]{1,0:T(8,128)(2,1)S(1)}, u32[]{:S(2)}, u32[]{:S(2)}) collective-permute-start(bf16[128,1152]{1,0:T(8,128)(2,1)S(1)} %get-tuple-element.21), channel_id=1, source_target_pairs={{0,4},{4,0},{8,12},{12,8},{16,20},{20,16},{24,28},{28,24},{1,5},{5... | collective-permute-start | bytes 884744 | tf_op jit(solution)/shard_map/ppermute | solution.py:32
  23.4 1.7 %collective-permute-start.14 = (bf16[32,1152]{1,0:T(8,128)(2,1)S(1)}, bf16[32,1152]{1,0:T(8,128)(2,1)S(1)}, u32[]{:S(2)}, u32[]{:S(2)}) collective-permute-start(bf16[32,1152]{1,0:T(8,128)(2,1)S(1)} %collective-permute-done.11.refs_0_), channel_id=1, source_target_pairs={{0,4},{4,0},{8,12},{12,8},{16,20},{20,16},{24,28},{28,24},{1,5},{5... | collective-permute-start | bytes 221192 | tf_op jit(solution)/shard_map/ppermute | solution.py:32
  23.9 1.3 %collective-permute-start.15 = (bf16[32,1152]{1,0:T(8,128)(2,1)S(1)}, bf16[32,1152]{1,0:T(8,128)(2,1)S(1)}, u32[]{:S(2)}, u32[]{:S(2)}) collective-permute-start(bf16[32,1152]{1,0:T(8,128)(2,1)S(1)} %collective-permute-done.12.refs_1_), channel_id=1, source_target_pairs={{0,4},{4,0},{8,12},{12,8},{16,20},{20,16},{24,28},{28,24},{1,5},{5... | collective-permute-start | bytes 221192 | tf_op jit(solution)/shard_map/ppermute | solution.py:32
  24.0 1.3 %collective-permute-start.16 = (bf16[32,1152]{1,0:T(8,128)(2,1)S(1)}, bf16[32,1152]{1,0:T(8,128)(2,1)S(1)}, u32[]{:S(2)}, u32[]{:S(2)}) collective-permute-start(bf16[32,1152]{1,0:T(8,128)(2,1)S(1)} %collective-permute-done.13.refs_2_), channel_id=1, source_target_pairs={{0,4},{4,0},{8,12},{12,8},{16,20},{20,16},{24,28},{28,24},{1,5},{5... | collective-permute-start | bytes 221192 | tf_op jit(solution)/shard_map/ppermute | solution.py:32
  26.8 7.5 %collective-permute-start.17 = (bf16[80,1152]{1,0:T(8,128)(2,1)S(1)}, bf16[80,1152]{1,0:T(8,128)(2,1)S(1)}, u32[]{:S(2)}, u32[]{:S(2)}) collective-permute-start(bf16[80,1152]{1,0:T(8,128)(2,1)S(1)} %get-tuple-element.29), channel_id=1, source_target_pairs={{0,8},{4,12},{8,0},{12,4},{16,24},{20,28},{24,16},{28,20},{1,9},{5... | collective-permute-start | bytes 552968 | tf_op jit(solution)/shard_map/ppermute | solution.py:32
  27.4 11.4 %collective-permute-start.18 = (bf16[80,1152]{1,0:T(8,128)(2,1)S(1)}, bf16[80,1152]{1,0:T(8,128)(2,1)S(1)}, u32[]{:S(2)}, u32[]{:S(2)}) collective-permute-start(bf16[80,1152]{1,0:T(8,128)(2,1)S(1)} %get-tuple-element.30), channel_id=1, source_target_pairs={{0,16},{4,20},{8,24},{12,28},{16,0},{20,4},{24,8},{28,12},{1,17},{... | collective-permute-start | bytes 552968 | tf_op jit(solution)/shard_map/ppermute | solution.py:32
  28.0 10.9 %collective-permute-start.19 = (bf16[80,1152]{1,0:T(8,128)(2,1)S(1)}, bf16[80,1152]{1,0:T(8,128)(2,1)S(1)}, u32[]{:S(2)}, u32[]{:S(2)}) collective-permute-start(bf16[80,1152]{1,0:T(8,128)(2,1)S(1)} %get-tuple-element.31), channel_id=1, source_target_pairs={{0,24},{4,28},{8,16},{12,20},{16,8},{20,12},{24,0},{28,4},{1,25},{... | collective-permute-start | bytes 552968 | tf_op jit(solution)/shard_map/ppermute | solution.py:32
  30.5 12.3 %collective-permute-start.8 = (bf16[32,1152]{1,0:T(8,128)(2,1)S(1)}, bf16[32,1152]{1,0:T(8,128)(2,1)S(1)}, u32[]{:S(2)}, u32[]{:S(2)}) collective-permute-start(bf16[32,1152]{1,0:T(8,128)(2,1)S(1)} %get-tuple-element.23), channel_id=1, source_target_pairs={{0,8},{4,12},{8,0},{12,4},{16,24},{20,28},{24,16},{28,20},{1,9},{5... | collective-permute-start | bytes 221192 | tf_op jit(solution)/shard_map/ppermute | solution.py:32
  31.1 11.7 %collective-permute-start.9 = (bf16[32,1152]{1,0:T(8,128)(2,1)S(1)}, bf16[32,1152]{1,0:T(8,128)(2,1)S(1)}, u32[]{:S(2)}, u32[]{:S(2)}) collective-permute-start(bf16[32,1152]{1,0:T(8,128)(2,1)S(1)} %get-tuple-element.24), channel_id=1, source_target_pairs={{0,16},{4,20},{8,24},{12,28},{16,0},{20,4},{24,8},{28,12},{1,17},{... | collective-permute-start | bytes 221192 | tf_op jit(solution)/shard_map/ppermute | solution.py:32
  34.4 8.4 %collective-permute-start.10 = (bf16[32,1152]{1,0:T(8,128)(2,1)S(1)}, bf16[32,1152]{1,0:T(8,128)(2,1)S(1)}, u32[]{:S(2)}, u32[]{:S(2)}) collective-permute-start(bf16[32,1152]{1,0:T(8,128)(2,1)S(1)} %get-tuple-element.25), channel_id=1, source_target_pairs={{0,24},{4,28},{8,16},{12,20},{16,8},{20,12},{24,0},{28,4},{1,25},{... | collective-permute-start | bytes 221192 | tf_op jit(solution)/shard_map/ppermute | solution.py:32

commit v2 on v1

v2 whole, which is shorter than its diff:
```python
import functools

import jax
import jax.numpy as jnp
from jax import lax
from jax.experimental import pallas as pl
from jax.experimental.pallas import tpu as pltpu
from jax.sharding import PartitionSpec as P

CAP = 12
LANES = 128
PLANE_ROWS = 512
WAIT = 5_000_000_000
F32, BF16 = jnp.float32, jnp.bfloat16
VMEM = pl.BlockSpec(memory_space=pltpu.VMEM)
SMEM = pl.BlockSpec(memory_space=pltpu.SMEM)
HBM = pl.BlockSpec(memory_space=pltpu.HBM)
DMA = pltpu.SemaphoreType.DMA


def call(kernel, out_shape, operands, scratch=(), flops=0, scalars=0, from_hbm=0, vmem=24):
    moved = sum(x.size * x.dtype.itemsize for x in jax.tree.leaves((out_shape, operands)))
    return pl.pallas_call(
        kernel,
        out_shape=out_shape,
        in_specs=[SMEM] * scalars + [VMEM] * (len(operands) - scalars - from_hbm) + [HBM] * from_hbm,
        out_specs=jax.tree.map(lambda _: VMEM, out_shape),
        scratch_shapes=list(scratch),
        cost_estimate=pl.CostEstimate(flops=flops, bytes_accessed=moved, transcendentals=0),
        compiler_params=pltpu.CompilerParams(vmem_limit_bytes=vmem << 20),
    )(*operands)


def swap(x, axis, k):
    return lax.ppermute(x, axis, [(i, i ^ k) for i in range(lax.axis_size(axis))])


def iota(shape, dim):
    return lax.broadcasted_iota(jnp.int32, shape, dim)


def dot(a, b, dims=((1,), (0,))):
    return lax.dot_general(a, b, (dims, ((), ())), preferred_element_type=F32)


def label_rows(rows_hbm, ids_hbm, cot_hbm, w2_hbm, out_ref, w2_ref, ids_ref, cot_ref, sems):
    rows, width = rows_hbm.shape
    copies = [
        pltpu.make_async_copy(ids_hbm, ids_ref, sems.at[0]),
        pltpu.make_async_copy(cot_hbm, cot_ref, sems.at[1]),
        pltpu.make_async_copy(rows_hbm, out_ref.at[:, :width], sems.at[2]),
        pltpu.make_async_copy(w2_hbm, w2_ref, sems.at[3]),
    ]
    for copy in copies:
        copy.start()
    eye = iota((rows, rows), 0) == iota((rows, rows), 1)

    def column(line):
        return jnp.sum(jnp.where(eye, jnp.broadcast_to(line, (rows, rows)), 0.0), axis=1, keepdims=True)

    lane = iota((rows, LANES), 1)
    copies[0].wait()
    copies[1].wait()
    cot = column(cot_ref[...].astype(F32))
    ids = column(ids_ref[...].astype(F32))
    out_ref[:, width:] = jnp.where(lane == 0, cot, jnp.where(lane == 1, ids, 0.0)).astype(BF16)
    copies[2].wait()
    copies[3].wait()


def stack_blocks(*refs):
    blocks, out_ref = refs[:-1], refs[-1]
    rows = blocks[0].shape[0]
    for k, block in enumerate(blocks):
        out_ref[k * rows:(k + 1) * rows, :] = block[...]


def gate(preact):
    sig = 1.0 / (1.0 + jnp.exp(-preact))
    return sig, preact * sig


def slots_of(ids, targets, rows, first):
    total = ids.shape[0]
    i, j = iota((total, total), 0), iota((total, total), 1)
    before = jnp.where((j < i) & ((i ^ j) < rows), 1.0, 0.0).astype(BF16)
    member = ids == targets
    rank = dot(before, jnp.where(member, 1.0, 0.0).astype(BF16))
    return jnp.where(member, first + rank.astype(jnp.int32), -1)


def block_of(total, rows):
    return iota((total, LANES), 0) >> rows.bit_length() - 1


def one_hot(slot, size):
    return jnp.where(slot == iota((slot.shape[0], size), 1), 1.0, 0.0).astype(BF16)


def tags_of(block, width):
    return block[:, width:].astype(F32)


def own_plane(chips, rows, where_ref, near_ref, other_ref, w1_ref, w2_ref, after_ref, *refs):
    outs, (band_ref, kept_ref, readout_ref, hs) = refs[:chips], refs[chips:]
    width, hidden = w1_ref.shape
    band = band_ref.shape[1]
    half = chips * rows
    kept = 2 * chips * CAP
    ids = jnp.concatenate([tags_of(ref, width)[:, 1:2] for ref in (near_ref, other_ref)], axis=0)
    block = block_of(2 * half, rows)
    first = jnp.where(block < chips, block * (2 * CAP), (block - chips) * (2 * CAP) + CAP)
    slot = slots_of(ids.astype(jnp.int32), where_ref[0], rows, first)[:, 0:1]
    picked = dot(one_hot(slot[:half], kept), near_ref[...], ((0,), (0,)))
    picked += dot(one_hot(slot[half:], kept), other_ref[...], ((0,), (0,)))
    kept_ref[...] = picked.astype(BF16)
    cot = tags_of(kept_ref, width)[:, 0:1]
    energy = jnp.zeros((kept, 1), F32)
    for c in range(0, hidden, band):
        part = slice(c, c + band)
        preact = dot(kept_ref[:, :width], w1_ref[:, part])
        sig, act = gate(preact)
        w2 = w2_ref[:, part].astype(F32)
        energy += jnp.sum(act * w2, axis=1, keepdims=True)
        hs[:, part] = (cot * w2 * sig * (1.0 + preact * (1.0 - sig))).astype(BF16)
        readout_ref[:, part] = jnp.sum(cot * act, axis=0, keepdims=True)
    band_ref[...] = hs[:, pl.ds(pl.multiple_of(where_ref[1] * band, band), band)]
    back = dot(hs[...], w1_ref[...], ((1,), (1,)))
    tail = jnp.where(iota((kept, LANES), 1) == 0, energy, 0.0)
    for k, out_ref in enumerate(outs):
        here = slice(2 * CAP * k, 2 * CAP * (k + 1))
        out_ref[:, :width] = back[here, :].astype(BF16)
        out_ref[:, width:] = tail[here, :].astype(BF16)


def pick_slots(rows, where_ref, far_ref, other_ref, *outs):
    half, wide = far_ref.shape
    size = outs[0].shape[0]
    ids = jnp.concatenate([tags_of(ref, wide - LANES)[:, 1:2] for ref in (far_ref, other_ref)], axis=0)
    targets = where_ref[0] ^ (2 * iota((2 * half, LANES), 1))
    slot = slots_of(ids.astype(jnp.int32), targets, rows, block_of(2 * half, rows) * CAP)
    for k, out_ref in enumerate(outs):
        pick = one_hot(slot[:, k:k + 1], size)
        rows_of_chip = dot(pick[:half], far_ref[...], ((0,), (0,)))
        rows_of_chip += dot(pick[half:], other_ref[...], ((0,), (0,)))
        out_ref[...] = rows_of_chip.astype(BF16)


def place_rows(n, where_ref, near_ref, other_ref, *refs):
    slots, (mine_ref, theirs_ref) = refs[:n], refs[-2:]
    rows, wide = mine_ref.shape
    ids = jnp.concatenate(
        [tags_of(ref.at[:rows, :], wide - LANES)[:, 1:2] for ref in (near_ref, other_ref)], axis=0
    )
    targets = where_ref[0] ^ (2 * iota((2 * rows, LANES), 1))
    slot = slots_of(ids.astype(jnp.int32), targets, rows, block_of(2 * rows, rows) * CAP)
    total = jnp.zeros((2 * rows, wide), F32)
    for k in range(n):
        total += dot(one_hot(slot[:, k:k + 1], 2 * CAP), slots[k][...])
    mine_ref[...] = total[:rows, :].astype(BF16)
    theirs_ref[...] = total[rows:, :].astype(BF16)


def add_cores(mine_ref, swapped_ref, grad_ref, energy_ref):
    rows, width = grad_ref.shape
    grad_ref[...] = mine_ref[:, :width] + swapped_ref[:, :width]
    column = (tags_of(mine_ref, width) + tags_of(swapped_ref, width))[:, 0:1]
    eye = iota((rows, rows), 0) == iota((rows, rows), 1)
    energy_ref[...] = jnp.sum(jnp.where(eye, column, 0.0), axis=0, keepdims=True).astype(BF16)


def all_replicas(n, where_ref, *refs):
    slots = refs[:n]
    kept_ref, w1_ref, w2_ref, band_ref, readout_ref, w1_grad_ref, w2_grad_ref, token_ref, ys, hs = refs[n:]
    size, kept = slots[0].shape[0], kept_ref.shape[0]
    width, hidden = w1_ref.shape
    band = w1_grad_ref.shape[0]
    new = n * size
    token_ref[...] = jnp.zeros(token_ref.shape, F32)
    for k in range(n):
        ys[k * size:(k + 1) * size, :] = slots[k][...]
    ys[new:, :] = kept_ref[...]
    hs[new:, :] = band_ref[...]
    cot = tags_of(ys, width)[:new, 0:1]
    bands = hidden // band
    for j in range(bands):
        at = where_ref[1] + j
        at = jnp.where(at >= bands, at - bands, at)
        part = pl.ds(pl.multiple_of(at * band, band), band)
        preact = dot(ys[:new, :width], w1_ref[:, part])
        sig, act = gate(preact)
        w2_grad_ref[:, part] = readout_ref[:, part] + jnp.sum(cot * act, axis=0, keepdims=True)
        if j == 0:
            w2 = w2_ref[:, part].astype(F32)
            hs[:new, :] = (cot * w2 * sig * (1.0 + preact * (1.0 - sig))).astype(BF16)
            w1_grad_ref[...] = dot(hs[...], ys[:, :width], ((0,), (0,))).astype(BF16)


def by_blocks(descriptors, expert_ids, cotangent, w1, w2):
    owners, replicas = lax.axis_size("expert"), lax.axis_size("rep")
    rows, width = descriptors.shape
    wide = width + LANES
    hidden = w1.shape[2]
    band = hidden // replicas
    chips = owners // 2
    kept = owners * CAP
    where = jnp.stack([lax.axis_index("expert"), lax.axis_index("rep")]).astype(jnp.int32)

    def shape(*dims, dtype=BF16):
        return jax.ShapeDtypeStruct(dims, dtype)

    def to_chips(blocks):
        return [blocks[0]] + [swap(blocks[k], "expert", 2 * k) for k in range(1, chips)]

    own, readout = call(
        label_rows, (shape(rows, wide), shape(1, hidden)),
        (descriptors, expert_ids.reshape(1, rows), cotangent.reshape(1, rows), w2),
        (pltpu.VMEM((1, rows), jnp.int32), pltpu.VMEM((1, rows), BF16), DMA((4,))),
        from_hbm=4, vmem=60,
    )
    weight = w1[0]
    far = [swap(own, "rep", k) for k in range(1, replicas)]
    near = to_chips([own] * chips)
    far = call(stack_blocks, shape(len(far) * rows, wide), tuple(far), flops=WAIT)
    near = call(stack_blocks, shape(chips * rows, wide), tuple(near), flops=WAIT)
    far_other = swap(far, "expert", 1)
    near_other = swap(near, "expert", 1)

    size = -(-2 * (replicas - 1) * CAP // 16) * 16
    chosen = call(
        functools.partial(pick_slots, rows), [shape(size, wide)] * chips, (where, far, far_other),
        flops=WAIT, scalars=1,
    )
    slots = to_chips(chosen)

    *back, band_grad, kept_rows, readout_part = call(
        functools.partial(own_plane, chips, rows),
        [shape(2 * CAP, wide)] * chips
        + [shape(kept, band), shape(kept, wide), shape(1, hidden, dtype=F32)],
        (where, near, near_other, weight, readout, chosen[0]),
        (pltpu.VMEM((kept, hidden), BF16),),
        flops=4 * kept * width * hidden, scalars=1,
    )
    back = to_chips(back)

    w1_grad, w2_grad, token = call(
        functools.partial(all_replicas, chips),
        (shape(band, width), shape(1, hidden, dtype=F32), shape(1, LANES, dtype=F32)),
        (where, *slots, kept_rows, weight, readout, band_grad, readout_part),
        (pltpu.VMEM((chips * size + kept, wide), BF16), pltpu.VMEM((chips * size + kept, band), BF16)),
        flops=2 * chips * size * width * (hidden + band), scalars=1,
    )

    mine, theirs = call(
        functools.partial(place_rows, chips), (shape(rows, wide), shape(rows, wide)),
        (where, near, near_other, *back, token), scalars=1,
    )
    descriptor_grad, energies = call(
        add_cores, (shape(rows, width), shape(1, rows)), (mine, swap(theirs, "expert", 1))
    )
    return energies.reshape(rows), descriptor_grad, w1_grad[None], w2_grad


def by_slots(descriptors, expert_ids, cotangent, w1, w2):
    owners = lax.axis_size("expert")
    columns = descriptors.shape[1]
    slot_count = owners * CAP
    targets = expert_ids[:, 0]
    member = (targets[:, None] == jnp.arange(owners, dtype=jnp.int32)[None, :]).astype(jnp.int32)
    slot_rank = jnp.sum((jnp.cumsum(member, axis=0) - 1) * member, axis=1)
    placement = (
        (targets * CAP + slot_rank)[:, None] == jnp.arange(slot_count, dtype=jnp.int32)[None, :]
    ).astype(BF16)
    over_rows = ((0,), (0,))

    def exchange(slots):
        parted = slots.reshape(owners, CAP, *slots.shape[1:])
        moved = lax.all_to_all(parted, "expert", split_axis=0, concat_axis=0, tiled=True)
        return moved.reshape(slots.shape)

    slot_rows = exchange(dot(placement, descriptors, over_rows).astype(BF16))
    slot_cot = exchange(dot(placement, cotangent, over_rows).astype(BF16)).astype(F32)
    weight, readout = w1[0], w2[0].astype(F32)
    preact = dot(slot_rows, weight)
    sig = jax.nn.sigmoid(preact)
    activated = preact * sig
    energy = jnp.sum(activated * readout, axis=1).astype(BF16)
    hidden_grad = (slot_cot[:, None] * readout * sig * (1.0 + preact * (1.0 - sig))).astype(BF16)
    input_grad = dot(hidden_grad, weight, ((1,), (1,))).astype(BF16)
    energies = dot(placement, exchange(energy)).astype(BF16)
    descriptor_grad = dot(placement, exchange(input_grad)).astype(BF16)
    w2_grad = lax.psum(jnp.sum(slot_cot[:, None] * activated, axis=0), "rep")
    w1_grad = lax.psum_scatter(
        dot(hidden_grad, slot_rows, over_rows).astype(BF16), "rep", scatter_dimension=0, tiled=True
    )
    return energies, descriptor_grad, w1_grad[None], w2_grad[None]


def on_device(descriptors, *rest):
    few = descriptors.shape[0] * lax.axis_size("expert") <= PLANE_ROWS
    return (by_blocks if few else by_slots)(descriptors, *rest)


def solution(mesh):
    in_specs = (
        P(("expert", "rep"), None),
        P(("expert", "rep"), None),
        P(("expert", "rep")),
        P("expert", None, None),
        P("expert", None),
    )
    out_specs = (
        P(("expert", "rep")),
        P(("expert", "rep"), None),
        P("expert", "rep", None),
        P("expert", None),
    )
    return jax.shard_map(
        on_device, mesh=mesh, in_specs=in_specs, out_specs=out_specs, check_vma=False
    )
```

time: 43.8 us -> 38 us (0.87)
  the two profiles are of different devices: /device:TPU:0 before, /device:TPU:21 now
where the time goes in v2:
time: 38 us; the launch traced here: 37.8 us
  starting transfers between devices  20.7 us (54%)
  Pallas kernels  11.9 us (31%)
  waiting for transfers between devices  4.45 us (12%)
  between operations  0.72 us (2%)
    ppermute x15, starting transfers between devices, swap(): lax.ppermute(x, axis, [(i, i ^ k) for i in range(lax.axis_size(axis))])  20.7 us
    pallas_call x8, Pallas kernels, call(): pl.pallas_call(kernel, out_shape=out_shape, in_specs=[SMEM] * scalars + [...  11.9 us
    ppermute x15, waiting for transfers between devices, swap(): lax.ppermute(x, axis, [(i, i ^ k) for i in range(lax.axis_size(axis))])  4.45 us
  transfers between devices with their start and end apart: 15, of which 4 were waited for; matrix products, arithmetic and copies ran while one was open for 0% of the time, Pallas kernels for 23%

profile of v2, /device:TPU:21, one launch (start us, length us, event | category | flops | bytes accessed | tf_op | source)
XLA Modules:
  0.0 37.8 jit_solution(3961883320622888714)
XLA Ops:
  0.6 1.5 %shard_map.84 = (bf16[32,1152]{1,0:T(8,128)(2,1)}, bf16[1,2048]{1,0:T(2,128)(2,1)}) custom-call(bf16[32,1024]{1,0:T(8,128)(2,1)} %rows_hbm.1, s32[1,32]{1,0:T(1,128)} %bitcast.9, bf16[1,32]{1,0:T(2,128)(2,1)} %bitcast.10, bf16[1,2048]{1,0:T(2,128)(2,1)} %w2_hbm.1), custom_call_target="tpu_custom_call" | custom-call | bytes 147648 | tf_op jit(solution)/shard_map/pallas_call | solution.py:23
  2.2 0.2 collective-permute-start.6
  2.4 3.2 %collective-permute-start.5 = (bf16[32,1152]{1,0:T(8,128)(2,1)}, bf16[32,1152]{1,0:T(8,128)(2,1)S(1)}, u32[]{:S(2)}, u32[]{:S(2)}) collective-permute-start(bf16[32,1152]{1,0:T(8,128)(2,1)} %get-tuple-element.24.refs_0_), channel_id=1, source_target_pairs={{0,2},{1,3},{2,0},{3,1},{4,6},{5,7},{6,4},{7,5},{8,10},{9,11},{10,... | collective-permute-start | bytes 221192 | tf_op jit(solution)/shard_map/ppermute | solution.py:35
  5.6 0.0 collective-permute-start.4
  5.6 1.2 %collective-permute-start.2 = (bf16[32,1152]{1,0:T(8,128)(2,1)}, bf16[32,1152]{1,0:T(8,128)(2,1)S(1)}, u32[]{:S(2)}, u32[]{:S(2)}) collective-permute-start(bf16[32,1152]{1,0:T(8,128)(2,1)} %get-tuple-element.24.refs_0_), channel_id=1, source_target_pairs={{0,24},{4,28},{8,16},{12,20},{16,8},{20,12},{24,0},{28,4},{1,25},{... | collective-permute-start | bytes 221192 | tf_op jit(solution)/shard_map/ppermute | solution.py:35
  6.8 1.2 %collective-permute-start.1 = (bf16[32,1152]{1,0:T(8,128)(2,1)}, bf16[32,1152]{1,0:T(8,128)(2,1)S(1)}, u32[]{:S(2)}, u32[]{:S(2)}) collective-permute-start(bf16[32,1152]{1,0:T(8,128)(2,1)} %get-tuple-element.24.refs_0_), channel_id=1, source_target_pairs={{0,16},{4,20},{8,24},{12,28},{16,0},{20,4},{24,8},{28,12},{1,17},{... | collective-permute-start | bytes 221192 | tf_op jit(solution)/shard_map/ppermute | solution.py:35
  8.0 0.1 pad_add_fusion.where_ref
  8.1 0.0 copy-start.2
  8.1 0.0 collective-permute-done.6.refs_2_
  8.1 0.3 collective-permute-start
  8.4 0.8 %collective-permute-done.5.refs_1_ = bf16[32,1152]{1,0:T(8,128)(2,1)S(1)} collective-permute-done((bf16[32,1152]{1,0:T(8,128)(2,1)}, bf16[32,1152]{1,0:T(8,128)(2,1)S(1)}, u32[]{:S(2)}, u32[]{:S(2)}) %collective-permute-start.5) | collective-permute-done | bytes 73760 | tf_op jit(solution)/shard_map/ppermute | solution.py:35
  9.2 0.2 collective-permute-done.4.refs_0_
  9.4 3.2 %collective-permute-start.7 = (bf16[96,1152]{1,0:T(8,128)(2,1)S(1)}, bf16[96,1152]{1,0:T(8,128)(2,1)S(1)}, u32[]{:S(2)}, u32[]{:S(2)}) collective-permute-start(bf16[96,1152]{1,0:T(8,128)(2,1)S(1)} %shard_map.86.far_ref), channel_id=1, source_target_pairs={{0,4},{4,0},{8,12},{12,8},{16,20},{20,16},{24,28},{28,24},{1,5},{5... | collective-permute-start | bytes 663560 | tf_op jit(solution)/shard_map/ppermute | solution.py:35
  12.6 0.0 collective-permute-done.2.refs_3_
  12.6 0.0 collective-permute-done.1.refs_2_
  12.6 0.0 collective-permute-done.refs_1_
  12.6 0.0 copy-done.2
  12.6 0.0 copy-start
  12.6 0.0 copy-start.1
  12.7 3.0 %collective-permute-start.3 = (bf16[128,1152]{1,0:T(8,128)(2,1)S(1)}, bf16[128,1152]{1,0:T(8,128)(2,1)S(1)}, u32[]{:S(2)}, u32[]{:S(2)}) collective-permute-start(bf16[128,1152]{1,0:T(8,128)(2,1)S(1)} %shard_map.85.near_ref), channel_id=1, source_target_pairs={{0,4},{4,0},{8,12},{12,8},{16,20},{20,16},{24,28},{28,24},{1,5},{5... | collective-permute-start | bytes 884744 | tf_op jit(solution)/shard_map/ppermute | solution.py:35
  15.7 0.0 collective-permute-done.7.other_ref
  15.7 1.5 %shard_map.87 = (bf16[80,1152]{1,0:T(8,128)(2,1)S(1)}, bf16[80,1152]{1,0:T(8,128)(2,1)S(1)}, bf16[80,1152]{1,0:T(8,128)(2,1)S(1)}, bf16[80,1152]{1,0:T(8,128)(2,1)S(1)}) custom-call(s32[2]{0:T(128)S(1)} %pad_add_fusion.where_ref, bf16[96,1152]{1,0:T(8,128)(2,1)S(1)} %shard_map.86.far_ref, bf16[96,1152]{1,0:T(8,128)(2,1)S(1)} %collective-permute-done.7.other_ref), custom_call_target="tpu_custom_call" | custom-call | flops 5000000000 | bytes 1179656 | tf_op jit(solution)/shard_map/pallas_call | solution.py:23
  17.2 1.3 %collective-permute-start.11 = (bf16[80,1152]{1,0:T(8,128)(2,1)S(1)}, bf16[80,1152]{1,0:T(8,128)(2,1)S(1)}, u32[]{:S(2)}, u32[]{:S(2)}) collective-permute-start(bf16[80,1152]{1,0:T(8,128)(2,1)S(1)} %get-tuple-element.31), channel_id=1, source_target_pairs={{0,8},{4,12},{8,0},{12,4},{16,24},{20,28},{24,16},{28,20},{1,9},{5... | collective-permute-start | bytes 552968 | tf_op jit(solution)/shard_map/ppermute | solution.py:35
  18.4 0.2 collective-permute-start.12
  18.7 1.2 %collective-permute-start.13 = (bf16[80,1152]{1,0:T(8,128)(2,1)S(1)}, bf16[80,1152]{1,0:T(8,128)(2,1)S(1)}, u32[]{:S(2)}, u32[]{:S(2)}) collective-permute-start(bf16[80,1152]{1,0:T(8,128)(2,1)S(1)} %get-tuple-element.33), channel_id=1, source_target_pairs={{0,24},{4,28},{8,16},{12,20},{16,8},{20,12},{24,0},{28,4},{1,25},{... | collective-permute-start | bytes 552968 | tf_op jit(solution)/shard_map/ppermute | solution.py:35
  19.9 0.0 collective-permute-done.3.other_ref
  19.9 0.0 copy-done
  19.9 0.0 copy-done.1
  19.9 3.2 %shard_map.88 = (bf16[24,1152]{1,0:T(8,128)(2,1)S(1)}, bf16[24,1152]{1,0:T(8,128)(2,1)S(1)}, bf16[24,1152]{1,0:T(8,128)(2,1)S(1)}, bf16[24,1152]{1,0:T(8,128)(2,...) custom-call(s32[2]{0:T(128)S(1)} %pad_add_fusion.where_ref, ...), custom_call_target="tpu_custom_call" | custom-call | flops 805306368 | bytes 5521416 | tf_op jit(solution)/shard_map/pallas_call | solution.py:23
  23.1 1.3 %collective-permute-start.8 = (bf16[24,1152]{1,0:T(8,128)(2,1)S(1)}, bf16[24,1152]{1,0:T(8,128)(2,1)S(1)}, u32[]{:S(2)}, u32[]{:S(2)}) collective-permute-start(bf16[24,1152]{1,0:T(8,128)(2,1)S(1)} %get-tuple-element.28), channel_id=1, source_target_pairs={{0,8},{4,12},{8,0},{12,4},{16,24},{20,28},{24,16},{28,20},{1,9},{5... | collective-permute-start | bytes 165896 | tf_op jit(solution)/shard_map/ppermute | solution.py:35
  24.3 0.2 collective-permute-start.9
  24.6 0.0 collective-permute-done.11.refs_1_
  24.6 1.2 %collective-permute-start.10 = (bf16[24,1152]{1,0:T(8,128)(2,1)S(1)}, bf16[24,1152]{1,0:T(8,128)(2,1)S(1)}, u32[]{:S(2)}, u32[]{:S(2)}) collective-permute-start(bf16[24,1152]{1,0:T(8,128)(2,1)S(1)} %get-tuple-element.30), channel_id=1, source_target_pairs={{0,24},{4,28},{8,16},{12,20},{16,8},{20,12},{24,0},{28,4},{1,25},{... | collective-permute-start | bytes 165896 | tf_op jit(solution)/shard_map/ppermute | solution.py:35
  25.8 2.5 %collective-permute-done.12.refs_2_ = bf16[80,1152]{1,0:T(8,128)(2,1)S(1)} collective-permute-done((bf16[80,1152]{1,0:T(8,128)(2,1)S(1)}, bf16[80,1152]{1,0:T(8,128)(2,1)S(1)}, u32[]{:S(2)}, u32[]{:S(2)}) %collective-permute-start.12) | collective-permute-done | bytes 184352 | tf_op jit(solution)/shard_map/ppermute | solution.py:35
  28.3 0.0 collective-permute-done.13.refs_3_
  28.3 3.9 %shard_map.89 = (bf16[512,1024]{1,0:T(8,128)(2,1)}, f32[1,2048]{1,0:T(1,128)}, f32[1,128]{1,0:T(1,128)S(1)}) custom-call(s32[2]{0:T(128)S(1)} %pad_add_fusion.where_ref, bf16[80,1152]{1,0:T(8,128)(2,1)S(1)} %get-tuple-element.26.after_ref.refs_0_, bf16[80,1152]{1,0:T(8,128)(2,1)S(1)} %collective-permute-done.11.refs_1_, ...), custom_call_target="tpu_custom_call" | custom-call | flops 1677721600 | bytes 6320648 | tf_op jit(solution)/shard_map/pallas_call | solution.py:23
  32.2 0.0 collective-permute-done.8.refs_1_
  32.2 0.0 collective-permute-done.9.refs_2_
  32.2 0.0 collective-permute-done.10.refs_3_
  32.2 1.1 %shard_map.90 = (bf16[32,1152]{1,0:T(8,128)(2,1)S(1)}, bf16[32,1152]{1,0:T(8,128)(2,1)S(1)}) custom-call(s32[2]{0:T(128)S(1)} %pad_add_fusion.where_ref, bf16[128,1152]{1,0:T(8,128)(2,1)S(1)} %shard_map.85.near_ref, bf16[128,1152]{1,0:T(8,128)(2,1)S(1)} %collective-permute-done.3.other_ref, bf16[24,1152]{1,0:T(8,128)(2,1)S(1)} %get-tuple-element.27.refs_0_, ...), custom_call_target="tpu_custom_call" | custom-call | bytes 958984 | tf_op jit(solution)/shard_map/pallas_call | solution.py:23
  33.3 3.0 %collective-permute-start.14 = (bf16[32,1152]{1,0:T(8,128)(2,1)S(1)}, bf16[32,1152]{1,0:T(8,128)(2,1)S(1)}, u32[]{:S(2)}, u32[]{:S(2)}) collective-permute-start(bf16[32,1152]{1,0:T(8,128)(2,1)S(1)} %get-tuple-element.39), channel_id=1, source_target_pairs={{0,4},{4,0},{8,12},{12,8},{16,20},{20,16},{24,28},{28,24},{1,5},{5... | collective-permute-start | bytes 221192 | tf_op jit(solution)/shard_map/ppermute | solution.py:35
  36.3 0.9 %collective-permute-done.14.swapped_ref = bf16[32,1152]{1,0:T(8,128)(2,1)S(1)} collective-permute-done((bf16[32,1152]{1,0:T(8,128)(2,1)S(1)}, bf16[32,1152]{1,0:T(8,128)(2,1)S(1)}, u32[]{:S(2)}, u32[]{:S(2)}) %collective-permute-start.14) | collective-permute-done | bytes 73760 | tf_op jit(solution)/shard_map/ppermute | solution.py:35
  37.2 0.6 %shard_map.91 = (bf16[32,1024]{1,0:T(8,128)(2,1)}, bf16[1,32]{1,0:T(2,128)(2,1)}) custom-call(bf16[32,1152]{1,0:T(8,128)(2,1)S(1)} %get-tuple-element.38.mine_ref, bf16[32,1152]{1,0:T(8,128)(2,1)S(1)} %collective-permute-done.14.swapped_ref), custom_call_target="tpu_custom_call" | custom-call | bytes 213056 | tf_op jit(solution)/shard_map/pallas_call | solution.py:23
  (2 shorter events, 0.0 us)
Async XLA Ops:
  2.2 5.9 %collective-permute-start.6 = (bf16[32,1152]{1,0:T(8,128)(2,1)}, bf16[32,1152]{1,0:T(8,128)(2,1)S(1)}, u32[]{:S(2)}, u32[]{:S(2)}) collective-permute-start(bf16[32,1152]{1,0:T(8,128)(2,1)} %get-tuple-element.24.refs_0_), channel_id=1, source_target_pairs={{0,3},{1,2},{2,1},{3,0},{4,7},{5,6},{6,5},{7,4},{8,11},{9,10},{10,... | collective-permute-start | bytes 221192 | tf_op jit(solution)/shard_map/ppermute | solution.py:35
  2.4 6.7 %collective-permute-start.5 = (bf16[32,1152]{1,0:T(8,128)(2,1)}, bf16[32,1152]{1,0:T(8,128)(2,1)S(1)}, u32[]{:S(2)}, u32[]{:S(2)}) collective-permute-start(bf16[32,1152]{1,0:T(8,128)(2,1)} %get-tuple-element.24.refs_0_), channel_id=1, source_target_pairs={{0,2},{1,3},{2,0},{3,1},{4,6},{5,7},{6,4},{7,5},{8,10},{9,11},{10,... | collective-permute-start | bytes 221192 | tf_op jit(solution)/shard_map/ppermute | solution.py:35
  5.6 3.7 %collective-permute-start.4 = (bf16[32,1152]{1,0:T(8,128)(2,1)}, bf16[32,1152]{1,0:T(8,128)(2,1)S(1)}, u32[]{:S(2)}, u32[]{:S(2)}) collective-permute-start(bf16[32,1152]{1,0:T(8,128)(2,1)} %get-tuple-element.24.refs_0_), channel_id=1, source_target_pairs={{0,1},{1,0},{2,3},{3,2},{4,5},{5,4},{6,7},{7,6},{8,9},{9,8},{10,11... | collective-permute-start | bytes 221192 | tf_op jit(solution)/shard_map/ppermute | solution.py:35
  5.6 7.0 %collective-permute-start.2 = (bf16[32,1152]{1,0:T(8,128)(2,1)}, bf16[32,1152]{1,0:T(8,128)(2,1)S(1)}, u32[]{:S(2)}, u32[]{:S(2)}) collective-permute-start(bf16[32,1152]{1,0:T(8,128)(2,1)} %get-tuple-element.24.refs_0_), channel_id=1, source_target_pairs={{0,24},{4,28},{8,16},{12,20},{16,8},{20,12},{24,0},{28,4},{1,25},{... | collective-permute-start | bytes 221192 | tf_op jit(solution)/shard_map/ppermute | solution.py:35
  6.8 5.8 %collective-permute-start.1 = (bf16[32,1152]{1,0:T(8,128)(2,1)}, bf16[32,1152]{1,0:T(8,128)(2,1)S(1)}, u32[]{:S(2)}, u32[]{:S(2)}) collective-permute-start(bf16[32,1152]{1,0:T(8,128)(2,1)} %get-tuple-element.24.refs_0_), channel_id=1, source_target_pairs={{0,16},{4,20},{8,24},{12,28},{16,0},{20,4},{24,8},{28,12},{1,17},{... | collective-permute-start | bytes 221192 | tf_op jit(solution)/shard_map/ppermute | solution.py:35
  8.1 4.5 %copy-start.2 = (bf16[32,1152]{1,0:T(8,128)(2,1)S(1)}, bf16[32,1152]{1,0:T(8,128)(2,1)}, u32[]{:S(2)}) copy-start(bf16[32,1152]{1,0:T(8,128)(2,1)} %get-tuple-element.24.refs_0_) | copy-start | bytes 221188
  8.1 4.5 %collective-permute-start = (bf16[32,1152]{1,0:T(8,128)(2,1)}, bf16[32,1152]{1,0:T(8,128)(2,1)S(1)}, u32[]{:S(2)}, u32[]{:S(2)}) collective-permute-start(bf16[32,1152]{1,0:T(8,128)(2,1)} %get-tuple-element.24.refs_0_), channel_id=1, source_target_pairs={{0,8},{4,12},{8,0},{12,4},{16,24},{20,28},{24,16},{28,20},{1,9},{5... | collective-permute-start | bytes 221192 | tf_op jit(solution)/shard_map/ppermute | solution.py:35
  9.4 6.3 %collective-permute-start.7 = (bf16[96,1152]{1,0:T(8,128)(2,1)S(1)}, bf16[96,1152]{1,0:T(8,128)(2,1)S(1)}, u32[]{:S(2)}, u32[]{:S(2)}) collective-permute-start(bf16[96,1152]{1,0:T(8,128)(2,1)S(1)} %shard_map.86.far_ref), channel_id=1, source_target_pairs={{0,4},{4,0},{8,12},{12,8},{16,20},{20,16},{24,28},{28,24},{1,5},{5... | collective-permute-start | bytes 663560 | tf_op jit(solution)/shard_map/ppermute | solution.py:35
  12.6 7.2 %copy-start = (bf16[1,1024,2048]{2,1,0:T(8,128)(2,1)S(1)}, bf16[1,1024,2048]{2,1,0:T(8,128)(2,1)}, u32[]{:S(2)}) copy-start(bf16[1,1024,2048]{2,1,0:T(8,128)(2,1)} %param.8) | copy-start | bytes 12582916
  12.6 7.2 %copy-start.1 = (bf16[1,2048]{1,0:T(2,128)(2,1)S(1)}, bf16[1,2048]{1,0:T(2,128)(2,1)}, u32[]{:S(2)}) copy-start(bf16[1,2048]{1,0:T(2,128)(2,1)} %get-tuple-element.25.w2_ref.refs_6_) | copy-start | bytes 12292
  12.7 7.2 %collective-permute-start.3 = (bf16[128,1152]{1,0:T(8,128)(2,1)S(1)}, bf16[128,1152]{1,0:T(8,128)(2,1)S(1)}, u32[]{:S(2)}, u32[]{:S(2)}) collective-permute-start(bf16[128,1152]{1,0:T(8,128)(2,1)S(1)} %shard_map.85.near_ref), channel_id=1, source_target_pairs={{0,4},{4,0},{8,12},{12,8},{16,20},{20,16},{24,28},{28,24},{1,5},{5... | collective-permute-start | bytes 884744 | tf_op jit(solution)/shard_map/ppermute | solution.py:35
  17.2 7.4 %collective-permute-start.11 = (bf16[80,1152]{1,0:T(8,128)(2,1)S(1)}, bf16[80,1152]{1,0:T(8,128)(2,1)S(1)}, u32[]{:S(2)}, u32[]{:S(2)}) collective-permute-start(bf16[80,1152]{1,0:T(8,128)(2,1)S(1)} %get-tuple-element.31), channel_id=1, source_target_pairs={{0,8},{4,12},{8,0},{12,4},{16,24},{20,28},{24,16},{28,20},{1,9},{5... | collective-permute-start | bytes 552968 | tf_op jit(solution)/shard_map/ppermute | solution.py:35
  18.4 9.9 %collective-permute-start.12 = (bf16[80,1152]{1,0:T(8,128)(2,1)S(1)}, bf16[80,1152]{1,0:T(8,128)(2,1)S(1)}, u32[]{:S(2)}, u32[]{:S(2)}) collective-permute-start(bf16[80,1152]{1,0:T(8,128)(2,1)S(1)} %get-tuple-element.32), channel_id=1, source_target_pairs={{0,16},{4,20},{8,24},{12,28},{16,0},{20,4},{24,8},{28,12},{1,17},{... | collective-permute-start | bytes 552968 | tf_op jit(solution)/shard_map/ppermute | solution.py:35
  18.7 9.7 %collective-permute-start.13 = (bf16[80,1152]{1,0:T(8,128)(2,1)S(1)}, bf16[80,1152]{1,0:T(8,128)(2,1)S(1)}, u32[]{:S(2)}, u32[]{:S(2)}) collective-permute-start(bf16[80,1152]{1,0:T(8,128)(2,1)S(1)} %get-tuple-element.33), channel_id=1, source_target_pairs={{0,24},{4,28},{8,16},{12,20},{16,8},{20,12},{24,0},{28,4},{1,25},{... | collective-permute-start | bytes 552968 | tf_op jit(solution)/shard_map/ppermute | solution.py:35
  23.1 9.1 %collective-permute-start.8 = (bf16[24,1152]{1,0:T(8,128)(2,1)S(1)}, bf16[24,1152]{1,0:T(8,128)(2,1)S(1)}, u32[]{:S(2)}, u32[]{:S(2)}) collective-permute-start(bf16[24,1152]{1,0:T(8,128)(2,1)S(1)} %get-tuple-element.28), channel_id=1, source_target_pairs={{0,8},{4,12},{8,0},{12,4},{16,24},{20,28},{24,16},{28,20},{1,9},{5... | collective-permute-start | bytes 165896 | tf_op jit(solution)/shard_map/ppermute | solution.py:35
  24.3 7.9 %collective-permute-start.9 = (bf16[24,1152]{1,0:T(8,128)(2,1)S(1)}, bf16[24,1152]{1,0:T(8,128)(2,1)S(1)}, u32[]{:S(2)}, u32[]{:S(2)}) collective-permute-start(bf16[24,1152]{1,0:T(8,128)(2,1)S(1)} %get-tuple-element.29), channel_id=1, source_target_pairs={{0,16},{4,20},{8,24},{12,28},{16,0},{20,4},{24,8},{28,12},{1,17},{... | collective-permute-start | bytes 165896 | tf_op jit(solution)/shard_map/ppermute | solution.py:35
  24.6 7.6 %collective-permute-start.10 = (bf16[24,1152]{1,0:T(8,128)(2,1)S(1)}, bf16[24,1152]{1,0:T(8,128)(2,1)S(1)}, u32[]{:S(2)}, u32[]{:S(2)}) collective-permute-start(bf16[24,1152]{1,0:T(8,128)(2,1)S(1)} %get-tuple-element.30), channel_id=1, source_target_pairs={{0,24},{4,28},{8,16},{12,20},{16,8},{20,12},{24,0},{28,4},{1,25},{... | collective-permute-start | bytes 165896 | tf_op jit(solution)/shard_map/ppermute | solution.py:35
  33.3 3.9 %collective-permute-start.14 = (bf16[32,1152]{1,0:T(8,128)(2,1)S(1)}, bf16[32,1152]{1,0:T(8,128)(2,1)S(1)}, u32[]{:S(2)}, u32[]{:S(2)}) collective-permute-start(bf16[32,1152]{1,0:T(8,128)(2,1)S(1)} %get-tuple-element.39), channel_id=1, source_target_pairs={{0,4},{4,0},{8,12},{12,8},{16,20},{20,16},{24,28},{28,24},{1,5},{5... | collective-permute-start | bytes 221192 | tf_op jit(solution)/shard_map/ppermute | solution.py:35

commit v3 on v2

--- a/solution.py
+++ b/solution.py
@@ -101,16 +101,17 @@
     return block[:, width:].astype(F32)
 
 
-def own_plane(chips, rows, where_ref, near_ref, other_ref, w1_ref, w2_ref, after_ref, *refs):
-    outs, (band_ref, kept_ref, readout_ref, hs) = refs[:chips], refs[chips:]
+def own_plane(
+    chips, rows, where_ref, near_ref, other_ref, w1_ref, w2_ref, after_ref,
+    keep_ref, give_ref, band_ref, kept_ref, readout_ref, hs,
+):
     width, hidden = w1_ref.shape
     band = band_ref.shape[1]
     half = chips * rows
     kept = 2 * chips * CAP
     ids = jnp.concatenate([tags_of(ref, width)[:, 1:2] for ref in (near_ref, other_ref)], axis=0)
     block = block_of(2 * half, rows)
-    first = jnp.where(block < chips, block * (2 * CAP), (block - chips) * (2 * CAP) + CAP)
-    slot = slots_of(ids.astype(jnp.int32), where_ref[0], rows, first)[:, 0:1]
+    slot = slots_of(ids.astype(jnp.int32), where_ref[0], rows, block_of(2 * half, rows) * CAP)[:, 0:1]
     picked = dot(one_hot(slot[:half], kept), near_ref[...], ((0,), (0,)))
     picked += dot(one_hot(slot[half:], kept), other_ref[...], ((0,), (0,)))
     kept_ref[...] = picked.astype(BF16)
@@ -127,10 +128,16 @@
     band_ref[...] = hs[:, pl.ds(pl.multiple_of(where_ref[1] * band, band), band)]
     back = dot(hs[...], w1_ref[...], ((1,), (1,)))
     tail = jnp.where(iota((kept, LANES), 1) == 0, energy, 0.0)
+    for out_ref, part in ((keep_ref, slice(0, kept // 2)), (give_ref, slice(kept // 2, kept))):
+        out_ref[:, :width] = back[part, :].astype(BF16)
+        out_ref[:, width:] = tail[part, :].astype(BF16)
+
+
+def join_cores(keep_ref, got_ref, *outs):
+    keep, got = keep_ref[...].astype(F32), got_ref[...].astype(F32)
     for k, out_ref in enumerate(outs):
-        here = slice(2 * CAP * k, 2 * CAP * (k + 1))
-        out_ref[:, :width] = back[here, :].astype(BF16)
-        out_ref[:, width:] = tail[here, :].astype(BF16)
+        part = slice(CAP * k, CAP * (k + 1))
+        out_ref[...] = jnp.concatenate([keep[part, :], got[part, :]], axis=0).astype(BF16)
 
 
 def pick_slots(rows, where_ref, far_ref, other_ref, *outs):
@@ -146,27 +153,20 @@
         out_ref[...] = rows_of_chip.astype(BF16)
 
 
-def place_rows(n, where_ref, near_ref, other_ref, *refs):
-    slots, (mine_ref, theirs_ref) = refs[:n], refs[-2:]
-    rows, wide = mine_ref.shape
-    ids = jnp.concatenate(
-        [tags_of(ref.at[:rows, :], wide - LANES)[:, 1:2] for ref in (near_ref, other_ref)], axis=0
-    )
-    targets = where_ref[0] ^ (2 * iota((2 * rows, LANES), 1))
-    slot = slots_of(ids.astype(jnp.int32), targets, rows, block_of(2 * rows, rows) * CAP)
-    total = jnp.zeros((2 * rows, wide), F32)
+def place_rows(n, where_ref, own_ref, *refs):
+    slots, (grad_ref, energy_ref) = refs[:n], refs[-2:]
+    rows, width = grad_ref.shape
+    ids = tags_of(own_ref, width)[:, 1:2].astype(jnp.int32)
+    lane = iota((rows, LANES), 1)
+    slot = slots_of(ids, where_ref[0] ^ lane, rows, jnp.where(lane & 1 == 0, 0, CAP))
+    total = jnp.zeros(own_ref.shape, F32)
     for k in range(n):
-        total += dot(one_hot(slot[:, k:k + 1], 2 * CAP), slots[k][...])
-    mine_ref[...] = total[:rows, :].astype(BF16)
-    theirs_ref[...] = total[rows:, :].astype(BF16)
-
-
-def add_cores(mine_ref, swapped_ref, grad_ref, energy_ref):
-    rows, width = grad_ref.shape
-    grad_ref[...] = mine_ref[:, :width] + swapped_ref[:, :width]
-    column = (tags_of(mine_ref, width) + tags_of(swapped_ref, width))[:, 0:1]
+        pick = one_hot(slot[:, 2 * k:2 * k + 1], 2 * CAP) + one_hot(slot[:, 2 * k + 1:2 * k + 2], 2 * CAP)
+        total += dot(pick, slots[k][...])
+    grad_ref[...] = total[:, :width].astype(BF16)
     eye = iota((rows, rows), 0) == iota((rows, rows), 1)
-    energy_ref[...] = jnp.sum(jnp.where(eye, column, 0.0), axis=0, keepdims=True).astype(BF16)
+    line = jnp.sum(jnp.where(eye, total[:, width:width + 1], 0.0), axis=0, keepdims=True)
+    energy_ref[...] = line.astype(BF16)
 
 
 def all_replicas(n, where_ref, *refs):
@@ -220,43 +220,40 @@
     )
     weight = w1[0]
     far = [swap(own, "rep", k) for k in range(1, replicas)]
+    far = call(stack_blocks, shape(len(far) * rows, wide), tuple(far), flops=WAIT)
+    far_other = swap(far, "expert", 1)
     near = to_chips([own] * chips)
-    far = call(stack_blocks, shape(len(far) * rows, wide), tuple(far), flops=WAIT)
     near = call(stack_blocks, shape(chips * rows, wide), tuple(near), flops=WAIT)
-    far_other = swap(far, "expert", 1)
     near_other = swap(near, "expert", 1)
 
-    size = -(-2 * (replicas - 1) * CAP // 16) * 16
+    size = 2 * (replicas - 1) * CAP
     chosen = call(
         functools.partial(pick_slots, rows), [shape(size, wide)] * chips, (where, far, far_other),
         flops=WAIT, scalars=1,
     )
     slots = to_chips(chosen)
 
-    *back, band_grad, kept_rows, readout_part = call(
+    keep, give, band_grad, kept_rows, readout_part = call(
         functools.partial(own_plane, chips, rows),
-        [shape(2 * CAP, wide)] * chips
-        + [shape(kept, band), shape(kept, wide), shape(1, hidden, dtype=F32)],
+        [shape(kept // 2, wide), shape(kept // 2, wide), shape(kept, band), shape(kept, wide), shape(1, hidden, dtype=F32)],
         (where, near, near_other, weight, readout, chosen[0]),
         (pltpu.VMEM((kept, hidden), BF16),),
         flops=4 * kept * width * hidden, scalars=1,
     )
-    back = to_chips(back)
+    got = swap(give, "expert", 1)
+    back = to_chips(call(join_cores, [shape(2 * CAP, wide)] * chips, (keep, got)))
 
     w1_grad, w2_grad, token = call(
         functools.partial(all_replicas, chips),
         (shape(band, width), shape(1, hidden, dtype=F32), shape(1, LANES, dtype=F32)),
         (where, *slots, kept_rows, weight, readout, band_grad, readout_part),
         (pltpu.VMEM((chips * size + kept, wide), BF16), pltpu.VMEM((chips * size + kept, band), BF16)),
-        flops=2 * chips * size * width * (hidden + band), scalars=1,
-    )
-
-    mine, theirs = call(
-        functools.partial(place_rows, chips), (shape(rows, wide), shape(rows, wide)),
-        (where, near, near_other, *back, token), scalars=1,
-    )
+        flops=4 * WAIT, scalars=1,
+    )
+
     descriptor_grad, energies = call(
-        add_cores, (shape(rows, width), shape(1, rows)), (mine, swap(theirs, "expert", 1))
+        functools.partial(place_rows, chips), (shape(rows, width), shape(1, rows)),
+        (where, own, *back, token), scalars=1,
     )
     return energies.reshape(rows), descriptor_grad, w1_grad[None], w2_grad
 

time: 38 us -> 35 us (0.921)
  the two profiles are of different devices: /device:TPU:21 before, /device:TPU:0 now
where the time goes in v3:
time: 35 us; the launch traced here: 34.8 us
  starting transfers between devices  17.2 us (49%)
  Pallas kernels  11.7 us (33%)
  waiting for transfers between devices  5.1 us (15%)
  between operations  0.74 us (2%)
    ppermute x15, starting transfers between devices, swap(): lax.ppermute(x, axis, [(i, i ^ k) for i in range(lax.axis_size(axis))])  17.2 us
    pallas_call x8, Pallas kernels, call(): pl.pallas_call(kernel, out_shape=out_shape, in_specs=[SMEM] * scalars + [...  11.7 us
    ppermute x15, waiting for transfers between devices, swap(): lax.ppermute(x, axis, [(i, i ^ k) for i in range(lax.axis_size(axis))])  5.1 us
  transfers between devices with their start and end apart: 15, of which 5 were waited for; matrix products, arithmetic and copies ran while one was open for 0% of the time, Pallas kernels for 24%

profile of v3, /device:TPU:0, one launch (start us, length us, event | category | flops | bytes accessed | tf_op | source)
XLA Modules:
  0.0 34.8 jit_solution(15515934923129191587)
XLA Ops:
  0.6 1.5 %shard_map.84 = (bf16[32,1152]{1,0:T(8,128)(2,1)}, bf16[1,2048]{1,0:T(2,128)(2,1)}) custom-call(bf16[32,1024]{1,0:T(8,128)(2,1)} %rows_hbm.1, s32[1,32]{1,0:T(1,128)} %bitcast.9, bf16[1,32]{1,0:T(2,128)(2,1)} %bitcast.10, bf16[1,2048]{1,0:T(2,128)(2,1)} %w2_hbm.1), custom_call_target="tpu_custom_call" | custom-call | bytes 147648 | tf_op jit(solution)/shard_map/pallas_call | solution.py:23
  2.2 5.1 %collective-permute-start.6 = (bf16[32,1152]{1,0:T(8,128)(2,1)}, bf16[32,1152]{1,0:T(8,128)(2,1)S(1)}, u32[]{:S(2)}, u32[]{:S(2)}) collective-permute-start(bf16[32,1152]{1,0:T(8,128)(2,1)} %get-tuple-element.24.refs_0_.own_ref), channel_id=1, source_target_pairs={{0,3},{1,2},{2,1},{3,0},{4,7},{5,6},{6,5},{7,4},{8,11},{9,10},{10,... | collective-permute-start | bytes 221192 | tf_op jit(solution)/shard_map/ppermute | solution.py:35
  7.3 0.0 collective-permute-start.5
  7.3 0.6 %collective-permute-start.4 = (bf16[32,1152]{1,0:T(8,128)(2,1)}, bf16[32,1152]{1,0:T(8,128)(2,1)S(1)}, u32[]{:S(2)}, u32[]{:S(2)}) collective-permute-start(bf16[32,1152]{1,0:T(8,128)(2,1)} %get-tuple-element.24.refs_0_.own_ref), channel_id=1, source_target_pairs={{0,1},{1,0},{2,3},{3,2},{4,5},{5,4},{6,7},{7,6},{8,9},{9,8},{10,11... | collective-permute-start | bytes 221192 | tf_op jit(solution)/shard_map/ppermute | solution.py:35
  7.9 2.6 %collective-permute-start.2 = (bf16[32,1152]{1,0:T(8,128)(2,1)}, bf16[32,1152]{1,0:T(8,128)(2,1)S(1)}, u32[]{:S(2)}, u32[]{:S(2)}) collective-permute-start(bf16[32,1152]{1,0:T(8,128)(2,1)} %get-tuple-element.24.refs_0_.own_ref), channel_id=1, source_target_pairs={{0,24},{4,28},{8,16},{12,20},{16,8},{20,12},{24,0},{28,4},{1,25},{... | collective-permute-start | bytes 221192 | tf_op jit(solution)/shard_map/ppermute | solution.py:35
  10.5 0.5 %collective-permute-start.1 = (bf16[32,1152]{1,0:T(8,128)(2,1)}, bf16[32,1152]{1,0:T(8,128)(2,1)S(1)}, u32[]{:S(2)}, u32[]{:S(2)}) collective-permute-start(bf16[32,1152]{1,0:T(8,128)(2,1)} %get-tuple-element.24.refs_0_.own_ref), channel_id=1, source_target_pairs={{0,16},{4,20},{8,24},{12,28},{16,0},{20,4},{24,8},{28,12},{1,17},{... | collective-permute-start | bytes 221192 | tf_op jit(solution)/shard_map/ppermute | solution.py:35
  11.0 0.1 pad_add_fusion.where_ref
  11.1 0.0 copy-start.1
  11.1 0.0 collective-permute-done.6.refs_2_
  11.1 1.0 %collective-permute-start = (bf16[32,1152]{1,0:T(8,128)(2,1)}, bf16[32,1152]{1,0:T(8,128)(2,1)S(1)}, u32[]{:S(2)}, u32[]{:S(2)}) collective-permute-start(bf16[32,1152]{1,0:T(8,128)(2,1)} %get-tuple-element.24.refs_0_.own_ref), channel_id=1, source_target_pairs={{0,8},{4,12},{8,0},{12,4},{16,24},{20,28},{24,16},{28,20},{1,9},{5... | collective-permute-start | bytes 221192 | tf_op jit(solution)/shard_map/ppermute | solution.py:35
  12.1 1.6 %collective-permute-done.5.refs_1_ = bf16[32,1152]{1,0:T(8,128)(2,1)S(1)} collective-permute-done((bf16[32,1152]{1,0:T(8,128)(2,1)}, bf16[32,1152]{1,0:T(8,128)(2,1)S(1)}, u32[]{:S(2)}, u32[]{:S(2)}) %collective-permute-start.5) | collective-permute-done | bytes 73760 | tf_op jit(solution)/shard_map/ppermute | solution.py:35
  13.7 0.0 collective-permute-done.4.refs_0_
  13.7 0.1 collective-permute-start.7
  13.8 0.0 collective-permute-done.2.refs_3_
  13.8 1.3 %collective-permute-done.1.refs_2_ = bf16[32,1152]{1,0:T(8,128)(2,1)S(1)} collective-permute-done((bf16[32,1152]{1,0:T(8,128)(2,1)}, bf16[32,1152]{1,0:T(8,128)(2,1)S(1)}, u32[]{:S(2)}, u32[]{:S(2)}) %collective-permute-start.1) | collective-permute-done | bytes 73760 | tf_op jit(solution)/shard_map/ppermute | solution.py:35
  15.1 0.6 %collective-permute-done.refs_1_ = bf16[32,1152]{1,0:T(8,128)(2,1)S(1)} collective-permute-done((bf16[32,1152]{1,0:T(8,128)(2,1)}, bf16[32,1152]{1,0:T(8,128)(2,1)S(1)}, u32[]{:S(2)}, u32[]{:S(2)}) %collective-permute-start) | collective-permute-done | bytes 73760 | tf_op jit(solution)/shard_map/ppermute | solution.py:35
  15.7 0.0 copy-done.1
  15.7 0.0 copy-start
  15.7 0.0 copy-start.2
  15.7 0.1 collective-permute-start.3
  15.8 0.0 collective-permute-done.7.other_ref
  15.8 1.5 %shard_map.87 = (bf16[72,1152]{1,0:T(8,128)(2,1)S(1)}, bf16[72,1152]{1,0:T(8,128)(2,1)S(1)}, bf16[72,1152]{1,0:T(8,128)(2,1)S(1)}, bf16[72,1152]{1,0:T(8,128)(2,1)S(1)}) custom-call(s32[2]{0:T(128)S(1)} %pad_add_fusion.where_ref, bf16[96,1152]{1,0:T(8,128)(2,1)S(1)} %shard_map.86.far_ref, bf16[96,1152]{1,0:T(8,128)(2,1)S(1)} %collective-permute-done.7.other_ref), custom_call_target="tpu_custom_call" | custom-call | flops 5000000000 | bytes 1105928 | tf_op jit(solution)/shard_map/pallas_call | solution.py:23
  17.3 1.0 %collective-permute-start.12 = (bf16[72,1152]{1,0:T(8,128)(2,1)S(1)}, bf16[72,1152]{1,0:T(8,128)(2,1)S(1)}, u32[]{:S(2)}, u32[]{:S(2)}) collective-permute-start(bf16[72,1152]{1,0:T(8,128)(2,1)S(1)} %get-tuple-element.33), channel_id=1, source_target_pairs={{0,8},{4,12},{8,0},{12,4},{16,24},{20,28},{24,16},{28,20},{1,9},{5... | collective-permute-start | bytes 497672 | tf_op jit(solution)/shard_map/ppermute | solution.py:35
  18.4 1.5 %collective-permute-start.13 = (bf16[72,1152]{1,0:T(8,128)(2,1)S(1)}, bf16[72,1152]{1,0:T(8,128)(2,1)S(1)}, u32[]{:S(2)}, u32[]{:S(2)}) collective-permute-start(bf16[72,1152]{1,0:T(8,128)(2,1)S(1)} %get-tuple-element.34), channel_id=1, source_target_pairs={{0,16},{4,20},{8,24},{12,28},{16,0},{20,4},{24,8},{28,12},{1,17},{... | collective-permute-start | bytes 497672 | tf_op jit(solution)/shard_map/ppermute | solution.py:35
  19.9 1.0 %collective-permute-start.14 = (bf16[72,1152]{1,0:T(8,128)(2,1)S(1)}, bf16[72,1152]{1,0:T(8,128)(2,1)S(1)}, u32[]{:S(2)}, u32[]{:S(2)}) collective-permute-start(bf16[72,1152]{1,0:T(8,128)(2,1)S(1)} %get-tuple-element.35), channel_id=1, source_target_pairs={{0,24},{4,28},{8,16},{12,20},{16,8},{20,12},{24,0},{28,4},{1,25},{... | collective-permute-start | bytes 497672 | tf_op jit(solution)/shard_map/ppermute | solution.py:35
  20.9 0.0 collective-permute-done.3.other_ref
  20.9 0.0 copy-done
  20.9 0.0 copy-done.2
  20.9 3.2 %shard_map.88 = (bf16[48,1152]{1,0:T(8,128)(2,1)S(1)}, bf16[48,1152]{1,0:T(8,128)(2,1)S(1)}, bf16[96,512]{1,0:T(8,128)(2,1)S(1)}, bf16[96,1152]{1,0:T(8,128)(2,1)S(1)}, f32[1,2048]{1,0:T(1,128)S(1)}) custom-call(s32[2]{0:T(128)S(1)} %pad_add_fusion.where_ref, bf16[128,1152]{1,0:T(8,128)(2,1)S(1)} %shard_map.85.near_ref, ...), custom_call_target="tpu_custom_call" | custom-call | flops 805306368 | bytes 5502984 | tf_op jit(solution)/shard_map/pallas_call | solution.py:23
  24.1 0.1 collective-permute-start.8
  24.2 1.3 %collective-permute-done.8.got_ref = bf16[48,1152]{1,0:T(8,128)(2,1)S(1)} collective-permute-done((bf16[48,1152]{1,0:T(8,128)(2,1)S(1)}, bf16[48,1152]{1,0:T(8,128)(2,1)S(1)}, u32[]{:S(2)}, u32[]{:S(2)}) %collective-permute-start.8) | collective-permute-done | bytes 110624 | tf_op jit(solution)/shard_map/ppermute | solution.py:35
  25.5 1.0 %collective-permute-start.9 = (bf16[24,1152]{1,0:T(8,128)(2,1)S(1)}, bf16[24,1152]{1,0:T(8,128)(2,1)S(1)}, u32[]{:S(2)}, u32[]{:S(2)}) collective-permute-start(bf16[24,1152]{1,0:T(8,128)(2,1)S(1)} %get-tuple-element.30), channel_id=1, source_target_pairs={{0,8},{4,12},{8,0},{12,4},{16,24},{20,28},{24,16},{28,20},{1,9},{5... | collective-permute-start | bytes 165896 | tf_op jit(solution)/shard_map/ppermute | solution.py:35
  26.6 1.5 %collective-permute-start.10 = (bf16[24,1152]{1,0:T(8,128)(2,1)S(1)}, bf16[24,1152]{1,0:T(8,128)(2,1)S(1)}, u32[]{:S(2)}, u32[]{:S(2)}) collective-permute-start(bf16[24,1152]{1,0:T(8,128)(2,1)S(1)} %get-tuple-element.31), channel_id=1, source_target_pairs={{0,16},{4,20},{8,24},{12,28},{16,0},{20,4},{24,8},{28,12},{1,17},{... | collective-permute-start | bytes 165896 | tf_op jit(solution)/shard_map/ppermute | solution.py:35
  28.1 0.0 collective-permute-done.12.refs_1_
  28.1 1.0 %collective-permute-start.11 = (bf16[24,1152]{1,0:T(8,128)(2,1)S(1)}, bf16[24,1152]{1,0:T(8,128)(2,1)S(1)}, u32[]{:S(2)}, u32[]{:S(2)}) collective-permute-start(bf16[24,1152]{1,0:T(8,128)(2,1)S(1)} %get-tuple-element.32), channel_id=1, source_target_pairs={{0,24},{4,28},{8,16},{12,20},{16,8},{20,12},{24,0},{28,4},{1,25},{... | collective-permute-start | bytes 165896 | tf_op jit(solution)/shard_map/ppermute | solution.py:35
  29.1 0.0 collective-permute-done.13.refs_2_
  29.1 0.0 collective-permute-done.14.refs_3_
  29.1 3.7 %shard_map.90 = (bf16[512,1024]{1,0:T(8,128)(2,1)}, f32[1,2048]{1,0:T(1,128)}, f32[1,128]{1,0:T(1,128)S(1)}) custom-call(s32[2]{0:T(128)S(1)} %pad_add_fusion.where_ref, bf16[72,1152]{1,0:T(8,128)(2,1)S(1)} %get-tuple-element.26.after_ref.refs_0_, bf16[72,1152]{1,0:T(8,128)(2,1)S(1)} %collective-permute-done.12.refs_1_, ...), custom_call_target="tpu_custom_call" | custom-call | flops 20000000000 | bytes 6246920 | tf_op jit(solution)/shard_map/pallas_call | solution.py:23
  32.8 0.0 collective-permute-done.9.refs_1_
  32.9 0.0 collective-permute-done.10.refs_2_
  32.9 0.3 collective-permute-done.11.refs_3_
  33.2 1.7 %shard_map.91 = (bf16[32,1024]{1,0:T(8,128)(2,1)}, bf16[1,32]{1,0:T(2,128)(2,1)}) custom-call(s32[2]{0:T(128)S(1)} %pad_add_fusion.where_ref, bf16[32,1152]{1,0:T(8,128)(2,1)S(1)} %copy-done.1, bf16[24,1152]{1,0:T(8,128)(2,1)S(1)} %get-tuple-element.29.refs_0_, bf16[24,1152]{1,0:T(8,128)(2,1)S(1)} %collective-permute-done.9.refs_1_, ...), custom_call_target="tpu_custom_call" | custom-call | bytes 361032 | tf_op jit(solution)/shard_map/pallas_call | solution.py:23
  (3 shorter events, 0.1 us)
Async XLA Ops:
  2.2 8.9 %collective-permute-start.6 = (bf16[32,1152]{1,0:T(8,128)(2,1)}, bf16[32,1152]{1,0:T(8,128)(2,1)S(1)}, u32[]{:S(2)}, u32[]{:S(2)}) collective-permute-start(bf16[32,1152]{1,0:T(8,128)(2,1)} %get-tuple-element.24.refs_0_.own_ref), channel_id=1, source_target_pairs={{0,3},{1,2},{2,1},{3,0},{4,7},{5,6},{6,5},{7,4},{8,11},{9,10},{10,... | collective-permute-start | bytes 221192 | tf_op jit(solution)/shard_map/ppermute | solution.py:35
  7.3 6.4 %collective-permute-start.5 = (bf16[32,1152]{1,0:T(8,128)(2,1)}, bf16[32,1152]{1,0:T(8,128)(2,1)S(1)}, u32[]{:S(2)}, u32[]{:S(2)}) collective-permute-start(bf16[32,1152]{1,0:T(8,128)(2,1)} %get-tuple-element.24.refs_0_.own_ref), channel_id=1, source_target_pairs={{0,2},{1,3},{2,0},{3,1},{4,6},{5,7},{6,4},{7,5},{8,10},{9,11},{10,... | collective-permute-start | bytes 221192 | tf_op jit(solution)/shard_map/ppermute | solution.py:35
  7.3 6.4 %collective-permute-start.4 = (bf16[32,1152]{1,0:T(8,128)(2,1)}, bf16[32,1152]{1,0:T(8,128)(2,1)S(1)}, u32[]{:S(2)}, u32[]{:S(2)}) collective-permute-start(bf16[32,1152]{1,0:T(8,128)(2,1)} %get-tuple-element.24.refs_0_.own_ref), channel_id=1, source_target_pairs={{0,1},{1,0},{2,3},{3,2},{4,5},{5,4},{6,7},{7,6},{8,9},{9,8},{10,11... | collective-permute-start | bytes 221192 | tf_op jit(solution)/shard_map/ppermute | solution.py:35
  7.9 5.9 %collective-permute-start.2 = (bf16[32,1152]{1,0:T(8,128)(2,1)}, bf16[32,1152]{1,0:T(8,128)(2,1)S(1)}, u32[]{:S(2)}, u32[]{:S(2)}) collective-permute-start(bf16[32,1152]{1,0:T(8,128)(2,1)} %get-tuple-element.24.refs_0_.own_ref), channel_id=1, source_target_pairs={{0,24},{4,28},{8,16},{12,20},{16,8},{20,12},{24,0},{28,4},{1,25},{... | collective-permute-start | bytes 221192 | tf_op jit(solution)/shard_map/ppermute | solution.py:35
  10.5 4.6 %collective-permute-start.1 = (bf16[32,1152]{1,0:T(8,128)(2,1)}, bf16[32,1152]{1,0:T(8,128)(2,1)S(1)}, u32[]{:S(2)}, u32[]{:S(2)}) collective-permute-start(bf16[32,1152]{1,0:T(8,128)(2,1)} %get-tuple-element.24.refs_0_.own_ref), channel_id=1, source_target_pairs={{0,16},{4,20},{8,24},{12,28},{16,0},{20,4},{24,8},{28,12},{1,17},{... | collective-permute-start | bytes 221192 | tf_op jit(solution)/shard_map/ppermute | solution.py:35
  11.1 4.6 %copy-start.1 = (bf16[32,1152]{1,0:T(8,128)(2,1)S(1)}, bf16[32,1152]{1,0:T(8,128)(2,1)}, u32[]{:S(2)}) copy-start(bf16[32,1152]{1,0:T(8,128)(2,1)} %get-tuple-element.24.refs_0_.own_ref) | copy-start | bytes 221188
  11.1 4.6 %collective-permute-start = (bf16[32,1152]{1,0:T(8,128)(2,1)}, bf16[32,1152]{1,0:T(8,128)(2,1)S(1)}, u32[]{:S(2)}, u32[]{:S(2)}) collective-permute-start(bf16[32,1152]{1,0:T(8,128)(2,1)} %get-tuple-element.24.refs_0_.own_ref), channel_id=1, source_target_pairs={{0,8},{4,12},{8,0},{12,4},{16,24},{20,28},{24,16},{28,20},{1,9},{5... | collective-permute-start | bytes 221192 | tf_op jit(solution)/shard_map/ppermute | solution.py:35
  13.7 2.1 %collective-permute-start.7 = (bf16[96,1152]{1,0:T(8,128)(2,1)S(1)}, bf16[96,1152]{1,0:T(8,128)(2,1)S(1)}, u32[]{:S(2)}, u32[]{:S(2)}) collective-permute-start(bf16[96,1152]{1,0:T(8,128)(2,1)S(1)} %shard_map.86.far_ref), channel_id=1, source_target_pairs={{0,4},{4,0},{8,12},{12,8},{16,20},{20,16},{24,28},{28,24},{1,5},{5... | collective-permute-start | bytes 663560 | tf_op jit(solution)/shard_map/ppermute | solution.py:35
  15.7 5.2 %copy-start = (bf16[1,1024,2048]{2,1,0:T(8,128)(2,1)S(1)}, bf16[1,1024,2048]{2,1,0:T(8,128)(2,1)}, u32[]{:S(2)}) copy-start(bf16[1,1024,2048]{2,1,0:T(8,128)(2,1)} %param.8) | copy-start | bytes 12582916
  15.7 5.1 %copy-start.2 = (bf16[1,2048]{1,0:T(2,128)(2,1)S(1)}, bf16[1,2048]{1,0:T(2,128)(2,1)}, u32[]{:S(2)}) copy-start(bf16[1,2048]{1,0:T(2,128)(2,1)} %get-tuple-element.25.w2_ref.refs_6_) | copy-start | bytes 12292
  15.7 5.1 %collective-permute-start.3 = (bf16[128,1152]{1,0:T(8,128)(2,1)S(1)}, bf16[128,1152]{1,0:T(8,128)(2,1)S(1)}, u32[]{:S(2)}, u32[]{:S(2)}) collective-permute-start(bf16[128,1152]{1,0:T(8,128)(2,1)S(1)} %shard_map.85.near_ref), channel_id=1, source_target_pairs={{0,4},{4,0},{8,12},{12,8},{16,20},{20,16},{24,28},{28,24},{1,5},{5... | collective-permute-start | bytes 884744 | tf_op jit(solution)/shard_map/ppermute | solution.py:35
  17.3 10.8 %collective-permute-start.12 = (bf16[72,1152]{1,0:T(8,128)(2,1)S(1)}, bf16[72,1152]{1,0:T(8,128)(2,1)S(1)}, u32[]{:S(2)}, u32[]{:S(2)}) collective-permute-start(bf16[72,1152]{1,0:T(8,128)(2,1)S(1)} %get-tuple-element.33), channel_id=1, source_target_pairs={{0,8},{4,12},{8,0},{12,4},{16,24},{20,28},{24,16},{28,20},{1,9},{5... | collective-permute-start | bytes 497672 | tf_op jit(solution)/shard_map/ppermute | solution.py:35
  18.4 10.7 %collective-permute-start.13 = (bf16[72,1152]{1,0:T(8,128)(2,1)S(1)}, bf16[72,1152]{1,0:T(8,128)(2,1)S(1)}, u32[]{:S(2)}, u32[]{:S(2)}) collective-permute-start(bf16[72,1152]{1,0:T(8,128)(2,1)S(1)} %get-tuple-element.34), channel_id=1, source_target_pairs={{0,16},{4,20},{8,24},{12,28},{16,0},{20,4},{24,8},{28,12},{1,17},{... | collective-permute-start | bytes 497672 | tf_op jit(solution)/shard_map/ppermute | solution.py:35
  19.9 9.2 %collective-permute-start.14 = (bf16[72,1152]{1,0:T(8,128)(2,1)S(1)}, bf16[72,1152]{1,0:T(8,128)(2,1)S(1)}, u32[]{:S(2)}, u32[]{:S(2)}) collective-permute-start(bf16[72,1152]{1,0:T(8,128)(2,1)S(1)} %get-tuple-element.35), channel_id=1, source_target_pairs={{0,24},{4,28},{8,16},{12,20},{16,8},{20,12},{24,0},{28,4},{1,25},{... | collective-permute-start | bytes 497672 | tf_op jit(solution)/shard_map/ppermute | solution.py:35
  24.1 1.4 %collective-permute-start.8 = (bf16[48,1152]{1,0:T(8,128)(2,1)S(1)}, bf16[48,1152]{1,0:T(8,128)(2,1)S(1)}, u32[]{:S(2)}, u32[]{:S(2)}) collective-permute-start(bf16[48,1152]{1,0:T(8,128)(2,1)S(1)} %get-tuple-element.28), channel_id=1, source_target_pairs={{0,4},{4,0},{8,12},{12,8},{16,20},{20,16},{24,28},{28,24},{1,5},{5... | collective-permute-start | bytes 331784 | tf_op jit(solution)/shard_map/ppermute | solution.py:35
  25.5 7.3 %collective-permute-start.9 = (bf16[24,1152]{1,0:T(8,128)(2,1)S(1)}, bf16[24,1152]{1,0:T(8,128)(2,1)S(1)}, u32[]{:S(2)}, u32[]{:S(2)}) collective-permute-start(bf16[24,1152]{1,0:T(8,128)(2,1)S(1)} %get-tuple-element.30), channel_id=1, source_target_pairs={{0,8},{4,12},{8,0},{12,4},{16,24},{20,28},{24,16},{28,20},{1,9},{5... | collective-permute-start | bytes 165896 | tf_op jit(solution)/shard_map/ppermute | solution.py:35
  26.6 6.3 %collective-permute-start.10 = (bf16[24,1152]{1,0:T(8,128)(2,1)S(1)}, bf16[24,1152]{1,0:T(8,128)(2,1)S(1)}, u32[]{:S(2)}, u32[]{:S(2)}) collective-permute-start(bf16[24,1152]{1,0:T(8,128)(2,1)S(1)} %get-tuple-element.31), channel_id=1, source_target_pairs={{0,16},{4,20},{8,24},{12,28},{16,0},{20,4},{24,8},{28,12},{1,17},{... | collective-permute-start | bytes 165896 | tf_op jit(solution)/shard_map/ppermute | solution.py:35
  28.1 5.1 %collective-permute-start.11 = (bf16[24,1152]{1,0:T(8,128)(2,1)S(1)}, bf16[24,1152]{1,0:T(8,128)(2,1)S(1)}, u32[]{:S(2)}, u32[]{:S(2)}) collective-permute-start(bf16[24,1152]{1,0:T(8,128)(2,1)S(1)} %get-tuple-element.32), channel_id=1, source_target_pairs={{0,24},{4,28},{8,16},{12,20},{16,8},{20,12},{24,0},{28,4},{1,25},{... | collective-permute-start | bytes 165896 | tf_op jit(solution)/shard_map/ppermute | solution.py:35

commit v4 on v3

--- a/solution.py
+++ b/solution.py
@@ -18,16 +18,18 @@
 DMA = pltpu.SemaphoreType.DMA
 
 
-def call(kernel, out_shape, operands, scratch=(), flops=0, scalars=0, from_hbm=0, vmem=24):
+def call(kernel, out_shape, operands, scratch=(), flops=0, scalars=0, hbm_outs=0):
+    outs = jax.tree.leaves(out_shape)
+    specs = [HBM] * hbm_outs + [VMEM] * (len(outs) - hbm_outs)
     moved = sum(x.size * x.dtype.itemsize for x in jax.tree.leaves((out_shape, operands)))
     return pl.pallas_call(
         kernel,
         out_shape=out_shape,
-        in_specs=[SMEM] * scalars + [VMEM] * (len(operands) - scalars - from_hbm) + [HBM] * from_hbm,
-        out_specs=jax.tree.map(lambda _: VMEM, out_shape),
+        in_specs=[SMEM] * scalars + [VMEM] * (len(operands) - scalars),
+        out_specs=jax.tree.unflatten(jax.tree.structure(out_shape), specs),
         scratch_shapes=list(scratch),
         cost_estimate=pl.CostEstimate(flops=flops, bytes_accessed=moved, transcendentals=0),
-        compiler_params=pltpu.CompilerParams(vmem_limit_bytes=vmem << 20),
+        compiler_params=pltpu.CompilerParams(vmem_limit_bytes=24 << 20),
     )(*operands)
 
 
@@ -43,29 +45,26 @@
     return lax.dot_general(a, b, (dims, ((), ())), preferred_element_type=F32)
 
 
-def label_rows(rows_hbm, ids_hbm, cot_hbm, w2_hbm, out_ref, w2_ref, ids_ref, cot_ref, sems):
-    rows, width = rows_hbm.shape
-    copies = [
-        pltpu.make_async_copy(ids_hbm, ids_ref, sems.at[0]),
-        pltpu.make_async_copy(cot_hbm, cot_ref, sems.at[1]),
-        pltpu.make_async_copy(rows_hbm, out_ref.at[:, :width], sems.at[2]),
-        pltpu.make_async_copy(w2_hbm, w2_ref, sems.at[3]),
-    ]
-    for copy in copies:
-        copy.start()
-    eye = iota((rows, rows), 0) == iota((rows, rows), 1)
-
-    def column(line):
-        return jnp.sum(jnp.where(eye, jnp.broadcast_to(line, (rows, rows)), 0.0), axis=1, keepdims=True)
-
+def begin(where_ref, token_ref):
+    token_ref[...] = jnp.zeros(token_ref.shape, F32)
+
+
+def label_rows(rows_ref, ids_ref, cot_ref, after_ref, out_ref):
+    rows, width = rows_ref.shape
+    i, j = iota((rows, rows), 0), iota((rows, rows), 1)
+
+    def column(square):
+        return jnp.sum(square, axis=1, keepdims=True)
+
+    ids_line = jnp.broadcast_to(ids_ref[...].astype(F32), (rows, rows))
+    cot_line = jnp.broadcast_to(cot_ref[...].astype(F32), (rows, rows))
+    ids = column(jnp.where(i == j, ids_line, 0.0))
+    cot = column(jnp.where(i == j, cot_line, 0.0))
+    rank = column(jnp.where((j < i) & (ids_line == ids), 1.0, 0.0))
     lane = iota((rows, LANES), 1)
-    copies[0].wait()
-    copies[1].wait()
-    cot = column(cot_ref[...].astype(F32))
-    ids = column(ids_ref[...].astype(F32))
-    out_ref[:, width:] = jnp.where(lane == 0, cot, jnp.where(lane == 1, ids, 0.0)).astype(BF16)
-    copies[2].wait()
-    copies[3].wait()
+    tags = jnp.where(lane == 0, cot, jnp.where(lane == 1, ids, jnp.where(lane == 2, rank, 0.0)))
+    out_ref[:, :width] = rows_ref[...]
+    out_ref[:, width:] = tags.astype(BF16)
 
 
 def stack_blocks(*refs):
@@ -80,25 +79,18 @@
     return sig, preact * sig
 
 
-def slots_of(ids, targets, rows, first):
-    total = ids.shape[0]
-    i, j = iota((total, total), 0), iota((total, total), 1)
-    before = jnp.where((j < i) & ((i ^ j) < rows), 1.0, 0.0).astype(BF16)
-    member = ids == targets
-    rank = dot(before, jnp.where(member, 1.0, 0.0).astype(BF16))
-    return jnp.where(member, first + rank.astype(jnp.int32), -1)
-
-
-def block_of(total, rows):
-    return iota((total, LANES), 0) >> rows.bit_length() - 1
+def ids_and_ranks(*refs):
+    tags = [ref[:, ref.shape[1] - LANES:].astype(F32)[:, 1:3] for ref in refs]
+    tags = (tags[0] if len(tags) == 1 else jnp.concatenate(tags, axis=0)).astype(jnp.int32)
+    return tags[:, 0:1], tags[:, 1:2]
+
+
+def first_slot(total, rows):
+    return (iota((total, 1), 0) >> rows.bit_length() - 1) * CAP
 
 
 def one_hot(slot, size):
     return jnp.where(slot == iota((slot.shape[0], size), 1), 1.0, 0.0).astype(BF16)
-
-
-def tags_of(block, width):
-    return block[:, width:].astype(F32)
 
 
 def own_plane(
@@ -109,13 +101,12 @@
     band = band_ref.shape[1]
     half = chips * rows
     kept = 2 * chips * CAP
-    ids = jnp.concatenate([tags_of(ref, width)[:, 1:2] for ref in (near_ref, other_ref)], axis=0)
-    block = block_of(2 * half, rows)
-    slot = slots_of(ids.astype(jnp.int32), where_ref[0], rows, block_of(2 * half, rows) * CAP)[:, 0:1]
+    ids, ranks = ids_and_ranks(near_ref, other_ref)
+    slot = jnp.where(ids == where_ref[0], first_slot(2 * half, rows) + ranks, -1)
     picked = dot(one_hot(slot[:half], kept), near_ref[...], ((0,), (0,)))
     picked += dot(one_hot(slot[half:], kept), other_ref[...], ((0,), (0,)))
     kept_ref[...] = picked.astype(BF16)
-    cot = tags_of(kept_ref, width)[:, 0:1]
+    cot = kept_ref[:, width:].astype(F32)[:, 0:1]
     energy = jnp.zeros((kept, 1), F32)
     for c in range(0, hidden, band):
         part = slice(c, c + band)
@@ -141,28 +132,28 @@
 
 
 def pick_slots(rows, where_ref, far_ref, other_ref, *outs):
-    half, wide = far_ref.shape
+    half = far_ref.shape[0]
     size = outs[0].shape[0]
-    ids = jnp.concatenate([tags_of(ref, wide - LANES)[:, 1:2] for ref in (far_ref, other_ref)], axis=0)
-    targets = where_ref[0] ^ (2 * iota((2 * half, LANES), 1))
-    slot = slots_of(ids.astype(jnp.int32), targets, rows, block_of(2 * half, rows) * CAP)
+    ids, ranks = ids_and_ranks(far_ref, other_ref)
+    apart = ids ^ where_ref[0]
+    slot = jnp.where(apart & 1 == 0, (apart >> 1) * size + first_slot(2 * half, rows) + ranks, -1)
+    pick = one_hot(slot, len(outs) * size)
+    picked = dot(pick[:half], far_ref[...], ((0,), (0,)))
+    picked += dot(pick[half:], other_ref[...], ((0,), (0,)))
     for k, out_ref in enumerate(outs):
-        pick = one_hot(slot[:, k:k + 1], size)
-        rows_of_chip = dot(pick[:half], far_ref[...], ((0,), (0,)))
-        rows_of_chip += dot(pick[half:], other_ref[...], ((0,), (0,)))
-        out_ref[...] = rows_of_chip.astype(BF16)
+        out_ref[...] = picked[k * size:(k + 1) * size, :].astype(BF16)
 
 
 def place_rows(n, where_ref, own_ref, *refs):
     slots, (grad_ref, energy_ref) = refs[:n], refs[-2:]
     rows, width = grad_ref.shape
-    ids = tags_of(own_ref, width)[:, 1:2].astype(jnp.int32)
-    lane = iota((rows, LANES), 1)
-    slot = slots_of(ids, where_ref[0] ^ lane, rows, jnp.where(lane & 1 == 0, 0, CAP))
-    total = jnp.zeros(own_ref.shape, F32)
-    for k in range(n):
-        pick = one_hot(slot[:, 2 * k:2 * k + 1], 2 * CAP) + one_hot(slot[:, 2 * k + 1:2 * k + 2], 2 * CAP)
-        total += dot(pick, slots[k][...])
+    size = slots[0].shape[0]
+    ids, ranks = ids_and_ranks(own_ref)
+    apart = ids ^ where_ref[0]
+    slot = (apart >> 1) * size + (apart & 1) * CAP + ranks
+    total = dot(one_hot(slot, size), slots[0][...])
+    for k in range(1, n):
+        total += dot(one_hot(slot - k * size, size), slots[k][...])
     grad_ref[...] = total[:, :width].astype(BF16)
     eye = iota((rows, rows), 0) == iota((rows, rows), 1)
     line = jnp.sum(jnp.where(eye, total[:, width:width + 1], 0.0), axis=0, keepdims=True)
@@ -171,17 +162,18 @@
 
 def all_replicas(n, where_ref, *refs):
     slots = refs[:n]
-    kept_ref, w1_ref, w2_ref, band_ref, readout_ref, w1_grad_ref, w2_grad_ref, token_ref, ys, hs = refs[n:]
+    kept_ref, w1_ref, w2_ref, band_ref, readout_ref, w1_grad_hbm, w2_grad_ref, token_ref = refs[n:n + 8]
+    ys, hs, w1_grad_ref, sem = refs[n + 8:]
     size, kept = slots[0].shape[0], kept_ref.shape[0]
     width, hidden = w1_ref.shape
-    band = w1_grad_ref.shape[0]
+    band = band_ref.shape[1]
     new = n * size
     token_ref[...] = jnp.zeros(token_ref.shape, F32)
     for k in range(n):
         ys[k * size:(k + 1) * size, :] = slots[k][...]
     ys[new:, :] = kept_ref[...]
     hs[new:, :] = band_ref[...]
-    cot = tags_of(ys, width)[:new, 0:1]
+    cot = ys[:new, width:].astype(F32)[:, 0:1]
     bands = hidden // band
     for j in range(bands):
         at = where_ref[1] + j
@@ -194,6 +186,9 @@
             w2 = w2_ref[:, part].astype(F32)
             hs[:new, :] = (cot * w2 * sig * (1.0 + preact * (1.0 - sig))).astype(BF16)
             w1_grad_ref[...] = dot(hs[...], ys[:, :width], ((0,), (0,))).astype(BF16)
+            copy = pltpu.make_async_copy(w1_grad_ref, w1_grad_hbm, sem)
+            copy.start()
+    copy.wait()
 
 
 def by_blocks(descriptors, expert_ids, cotangent, w1, w2):
@@ -212,12 +207,12 @@
     def to_chips(blocks):
         return [blocks[0]] + [swap(blocks[k], "expert", 2 * k) for k in range(1, chips)]
 
-    own, readout = call(
-        label_rows, (shape(rows, wide), shape(1, hidden)),
-        (descriptors, expert_ids.reshape(1, rows), cotangent.reshape(1, rows), w2),
-        (pltpu.VMEM((1, rows), jnp.int32), pltpu.VMEM((1, rows), BF16), DMA((4,))),
-        from_hbm=4, vmem=60,
-    )
+    begun = call(begin, shape(1, LANES, dtype=F32), (where,), flops=WAIT, scalars=1)
+    own = call(
+        label_rows, shape(rows, wide),
+        (descriptors, expert_ids.reshape(1, rows), cotangent.reshape(1, rows), begun),
+    )
+    readout = w2
     weight = w1[0]
     far = [swap(own, "rep", k) for k in range(1, replicas)]
     far = call(stack_blocks, shape(len(far) * rows, wide), tuple(far), flops=WAIT)
@@ -247,8 +242,11 @@
         functools.partial(all_replicas, chips),
         (shape(band, width), shape(1, hidden, dtype=F32), shape(1, LANES, dtype=F32)),
         (where, *slots, kept_rows, weight, readout, band_grad, readout_part),
-        (pltpu.VMEM((chips * size + kept, wide), BF16), pltpu.VMEM((chips * size + kept, band), BF16)),
-        flops=4 * WAIT, scalars=1,
+        (
+            pltpu.VMEM((chips * size + kept, wide), BF16), pltpu.VMEM((chips * size + kept, band), BF16),
+            pltpu.VMEM((band, width), BF16), DMA,
+        ),
+        flops=4 * WAIT, scalars=1, hbm_outs=1,
     )
 
     descriptor_grad, energies = call(

time: 35 us -> 33.9 us (0.969)
  Pallas kernels: 11.7 us -> 10.6 us
    pallas_call x8 -> x9, Pallas kernels: 11.7 us -> 10.6 us  [call(): pl.pallas_call(kernel, out_shape=out_shape, in_specs=[SMEM] * scalars + [...]
  transfers between devices with their start and end apart: 15 -> 15, of which waited for: 5 -> 5; matrix products, arithmetic and copies ran while one was open for 0% -> 0% of each run, Pallas kernels for 24% -> 25%
where the time goes in v4:
time: 33.9 us; the launch traced here: 33.7 us
  starting transfers between devices  17 us (50%)
  Pallas kernels  10.6 us (31%)
  waiting for transfers between devices  5.04 us (15%)
  between operations  0.77 us (2%)
    ppermute x15, starting transfers between devices, swap(): lax.ppermute(x, axis, [(i, i ^ k) for i in range(lax.axis_size(axis))])  17 us
    pallas_call x9, Pallas kernels, call(): pl.pallas_call(kernel, out_shape=out_shape, in_specs=[SMEM] * scalars + [...  10.6 us
    ppermute x15, waiting for transfers between devices, swap(): lax.ppermute(x, axis, [(i, i ^ k) for i in range(lax.axis_size(axis))])  5.04 us
  transfers between devices with their start and end apart: 15, of which 5 were waited for; matrix products, arithmetic and copies ran while one was open for 0% of the time, Pallas kernels for 25%

profile of v4, /device:TPU:0, one launch (start us, length us, event | category | flops | bytes accessed | tf_op | source)
XLA Modules:
  0.0 33.7 jit_solution(12913759953792065276)
XLA Ops:
  0.6 0.1 pad_add_fusion.where_ref
  0.7 0.0 copy-start.1
  0.7 0.0 copy-start.3
  0.7 0.0 copy-start.4
  0.7 0.5 %shard_map.84.after_ref = f32[1,128]{1,0:T(1,128)S(1)} custom-call(s32[2]{0:T(128)S(1)} %pad_add_fusion.where_ref), custom_call_target="tpu_custom_call" | custom-call | flops 5000000000 | bytes 520 | tf_op jit(solution)/shard_map/pallas_call | solution.py:25
  1.3 0.3 copy-done.1
  1.6 0.0 copy-done.3
  1.6 0.0 copy-done.4
  1.6 0.2 shard_map.85.refs_0_.own_ref
  1.7 5.1 %collective-permute-start.6 = (bf16[32,1152]{1,0:T(8,128)(2,1)S(1)}, bf16[32,1152]{1,0:T(8,128)(2,1)S(1)}, u32[]{:S(2)}, u32[]{:S(2)}) collective-permute-start(bf16[32,1152]{1,0:T(8,128)(2,1)S(1)} %shard_map.85.refs_0_.own_ref), channel_id=1, source_target_pairs={{0,3},{1,2},{2,1},{3,0},{4,7},{5,6},{6,5},{7,4},{8,11},{9,10},{10,... | collective-permute-start | bytes 221192 | tf_op jit(solution)/shard_map/ppermute | solution.py:37
  6.8 0.0 collective-permute-start.5
  6.8 0.6 %collective-permute-start.4 = (bf16[32,1152]{1,0:T(8,128)(2,1)S(1)}, bf16[32,1152]{1,0:T(8,128)(2,1)S(1)}, u32[]{:S(2)}, u32[]{:S(2)}) collective-permute-start(bf16[32,1152]{1,0:T(8,128)(2,1)S(1)} %shard_map.85.refs_0_.own_ref), channel_id=1, source_target_pairs={{0,1},{1,0},{2,3},{3,2},{4,5},{5,4},{6,7},{7,6},{8,9},{9,8},{10,11... | collective-permute-start | bytes 221192 | tf_op jit(solution)/shard_map/ppermute | solution.py:37
  7.4 2.6 %collective-permute-start.2 = (bf16[32,1152]{1,0:T(8,128)(2,1)S(1)}, bf16[32,1152]{1,0:T(8,128)(2,1)S(1)}, u32[]{:S(2)}, u32[]{:S(2)}) collective-permute-start(bf16[32,1152]{1,0:T(8,128)(2,1)S(1)} %shard_map.85.refs_0_.own_ref), channel_id=1, source_target_pairs={{0,24},{4,28},{8,16},{12,20},{16,8},{20,12},{24,0},{28,4},{1,25},{... | collective-permute-start | bytes 221192 | tf_op jit(solution)/shard_map/ppermute | solution.py:37
  10.0 0.5 %collective-permute-start.1 = (bf16[32,1152]{1,0:T(8,128)(2,1)S(1)}, bf16[32,1152]{1,0:T(8,128)(2,1)S(1)}, u32[]{:S(2)}, u32[]{:S(2)}) collective-permute-start(bf16[32,1152]{1,0:T(8,128)(2,1)S(1)} %shard_map.85.refs_0_.own_ref), channel_id=1, source_target_pairs={{0,16},{4,20},{8,24},{12,28},{16,0},{20,4},{24,8},{28,12},{1,17},{... | collective-permute-start | bytes 221192 | tf_op jit(solution)/shard_map/ppermute | solution.py:37
  10.5 0.0 collective-permute-done.6.refs_2_
  10.5 0.9 %collective-permute-start = (bf16[32,1152]{1,0:T(8,128)(2,1)S(1)}, bf16[32,1152]{1,0:T(8,128)(2,1)S(1)}, u32[]{:S(2)}, u32[]{:S(2)}) collective-permute-start(bf16[32,1152]{1,0:T(8,128)(2,1)S(1)} %shard_map.85.refs_0_.own_ref), channel_id=1, source_target_pairs={{0,8},{4,12},{8,0},{12,4},{16,24},{20,28},{24,16},{28,20},{1,9},{5... | collective-permute-start | bytes 221192 | tf_op jit(solution)/shard_map/ppermute | solution.py:37
  11.4 1.6 %collective-permute-done.5.refs_1_ = bf16[32,1152]{1,0:T(8,128)(2,1)S(1)} collective-permute-done((bf16[32,1152]{1,0:T(8,128)(2,1)S(1)}, bf16[32,1152]{1,0:T(8,128)(2,1)S(1)}, u32[]{:S(2)}, u32[]{:S(2)}) %collective-permute-start.5) | collective-permute-done | bytes 73760 | tf_op jit(solution)/shard_map/ppermute | solution.py:37
  13.0 0.0 collective-permute-done.4.refs_0_
  13.0 0.1 collective-permute-start.7
  13.1 0.0 collective-permute-done.2.refs_3_
  13.1 1.3 %collective-permute-done.1.refs_2_ = bf16[32,1152]{1,0:T(8,128)(2,1)S(1)} collective-permute-done((bf16[32,1152]{1,0:T(8,128)(2,1)S(1)}, bf16[32,1152]{1,0:T(8,128)(2,1)S(1)}, u32[]{:S(2)}, u32[]{:S(2)}) %collective-permute-start.1) | collective-permute-done | bytes 73760 | tf_op jit(solution)/shard_map/ppermute | solution.py:37
  14.4 0.5 %collective-permute-done.refs_1_ = bf16[32,1152]{1,0:T(8,128)(2,1)S(1)} collective-permute-done((bf16[32,1152]{1,0:T(8,128)(2,1)S(1)}, bf16[32,1152]{1,0:T(8,128)(2,1)S(1)}, u32[]{:S(2)}, u32[]{:S(2)}) %collective-permute-start) | collective-permute-done | bytes 73760 | tf_op jit(solution)/shard_map/ppermute | solution.py:37
  14.9 0.0 copy-start
  14.9 0.0 copy-start.2
  14.9 0.1 collective-permute-start.3
  15.0 0.0 collective-permute-done.7.other_ref
  15.0 1.2 %shard_map.88 = (bf16[72,1152]{1,0:T(8,128)(2,1)S(1)}, bf16[72,1152]{1,0:T(8,128)(2,1)S(1)}, bf16[72,1152]{1,0:T(8,128)(2,1)S(1)}, bf16[72,1152]{1,0:T(8,128)(2,1)S(1)}) custom-call(s32[2]{0:T(128)S(1)} %pad_add_fusion.where_ref, bf16[96,1152]{1,0:T(8,128)(2,1)S(1)} %shard_map.87.far_ref, bf16[96,1152]{1,0:T(8,128)(2,1)S(1)} %collective-permute-done.7.other_ref), custom_call_target="tpu_custom_call" | custom-call | flops 5000000000 | bytes 1105928 | tf_op jit(solution)/shard_map/pallas_call | solution.py:25
  16.3 1.1 %collective-permute-start.12 = (bf16[72,1152]{1,0:T(8,128)(2,1)S(1)}, bf16[72,1152]{1,0:T(8,128)(2,1)S(1)}, u32[]{:S(2)}, u32[]{:S(2)}) collective-permute-start(bf16[72,1152]{1,0:T(8,128)(2,1)S(1)} %get-tuple-element.29), channel_id=1, source_target_pairs={{0,8},{4,12},{8,0},{12,4},{16,24},{20,28},{24,16},{28,20},{1,9},{5... | collective-permute-start | bytes 497672 | tf_op jit(solution)/shard_map/ppermute | solution.py:37
  17.4 1.5 %collective-permute-start.13 = (bf16[72,1152]{1,0:T(8,128)(2,1)S(1)}, bf16[72,1152]{1,0:T(8,128)(2,1)S(1)}, u32[]{:S(2)}, u32[]{:S(2)}) collective-permute-start(bf16[72,1152]{1,0:T(8,128)(2,1)S(1)} %get-tuple-element.30), channel_id=1, source_target_pairs={{0,16},{4,20},{8,24},{12,28},{16,0},{20,4},{24,8},{28,12},{1,17},{... | collective-permute-start | bytes 497672 | tf_op jit(solution)/shard_map/ppermute | solution.py:37
  18.9 0.9 %collective-permute-start.14 = (bf16[72,1152]{1,0:T(8,128)(2,1)S(1)}, bf16[72,1152]{1,0:T(8,128)(2,1)S(1)}, u32[]{:S(2)}, u32[]{:S(2)}) collective-permute-start(bf16[72,1152]{1,0:T(8,128)(2,1)S(1)} %get-tuple-element.31), channel_id=1, source_target_pairs={{0,24},{4,28},{8,16},{12,20},{16,8},{20,12},{24,0},{28,4},{1,25},{... | collective-permute-start | bytes 497672 | tf_op jit(solution)/shard_map/ppermute | solution.py:37
  19.8 0.0 collective-permute-done.3.other_ref
  19.8 0.0 copy-done
  19.8 0.0 copy-done.2
  19.8 3.3 %shard_map.89 = (bf16[48,1152]{1,0:T(8,128)(2,1)S(1)}, bf16[48,1152]{1,0:T(8,128)(2,1)S(1)}, bf16[96,512]{1,0:T(8,128)(2,1)S(1)}, bf16[96,1152]{1,0:T(8,128)(2,1)S(1)}, f32[1,2048]{1,0:T(1,128)S(1)}) custom-call(s32[2]{0:T(128)S(1)} %pad_add_fusion.where_ref, bf16[128,1152]{1,0:T(8,128)(2,1)S(1)} %shard_map.86.near_ref, ...), custom_call_target="tpu_custom_call" | custom-call | flops 805306368 | bytes 5502984 | tf_op jit(solution)/shard_map/pallas_call | solution.py:25
  23.1 0.1 collective-permute-start.8
  23.2 1.3 %collective-permute-done.8.got_ref = bf16[48,1152]{1,0:T(8,128)(2,1)S(1)} collective-permute-done((bf16[48,1152]{1,0:T(8,128)(2,1)S(1)}, bf16[48,1152]{1,0:T(8,128)(2,1)S(1)}, u32[]{:S(2)}, u32[]{:S(2)}) %collective-permute-start.8) | collective-permute-done | bytes 110624 | tf_op jit(solution)/shard_map/ppermute | solution.py:37
  24.5 1.1 %collective-permute-start.9 = (bf16[24,1152]{1,0:T(8,128)(2,1)S(1)}, bf16[24,1152]{1,0:T(8,128)(2,1)S(1)}, u32[]{:S(2)}, u32[]{:S(2)}) collective-permute-start(bf16[24,1152]{1,0:T(8,128)(2,1)S(1)} %get-tuple-element.26), channel_id=1, source_target_pairs={{0,8},{4,12},{8,0},{12,4},{16,24},{20,28},{24,16},{28,20},{1,9},{5... | collective-permute-start | bytes 165896 | tf_op jit(solution)/shard_map/ppermute | solution.py:37
  25.6 1.5 %collective-permute-start.10 = (bf16[24,1152]{1,0:T(8,128)(2,1)S(1)}, bf16[24,1152]{1,0:T(8,128)(2,1)S(1)}, u32[]{:S(2)}, u32[]{:S(2)}) collective-permute-start(bf16[24,1152]{1,0:T(8,128)(2,1)S(1)} %get-tuple-element.27), channel_id=1, source_target_pairs={{0,16},{4,20},{8,24},{12,28},{16,0},{20,4},{24,8},{28,12},{1,17},{... | collective-permute-start | bytes 165896 | tf_op jit(solution)/shard_map/ppermute | solution.py:37
  27.2 0.0 collective-permute-done.12.refs_1_
  27.2 0.9 %collective-permute-start.11 = (bf16[24,1152]{1,0:T(8,128)(2,1)S(1)}, bf16[24,1152]{1,0:T(8,128)(2,1)S(1)}, u32[]{:S(2)}, u32[]{:S(2)}) collective-permute-start(bf16[24,1152]{1,0:T(8,128)(2,1)S(1)} %get-tuple-element.28), channel_id=1, source_target_pairs={{0,24},{4,28},{8,16},{12,20},{16,8},{20,12},{24,0},{28,4},{1,25},{... | collective-permute-start | bytes 165896 | tf_op jit(solution)/shard_map/ppermute | solution.py:37
  28.1 0.0 collective-permute-done.13.refs_2_
  28.1 0.0 collective-permute-done.14.refs_3_
  28.1 3.8 %shard_map.91 = (bf16[512,1024]{1,0:T(8,128)(2,1)}, f32[1,2048]{1,0:T(1,128)}, f32[1,128]{1,0:T(1,128)S(1)}) custom-call(s32[2]{0:T(128)S(1)} %pad_add_fusion.where_ref, bf16[72,1152]{1,0:T(8,128)(2,1)S(1)} %get-tuple-element.22.after_ref.refs_0_, bf16[72,1152]{1,0:T(8,128)(2,1)S(1)} %collective-permute-done.12.refs_1_, ...), custom_call_target="tpu_custom_call" | custom-call | flops 20000000000 | bytes 6246920 | tf_op jit(solution)/shard_map/pallas_call | solution.py:25
  31.9 0.0 collective-permute-done.9.refs_1_
  31.9 0.0 collective-permute-done.10.refs_2_
  31.9 0.3 collective-permute-done.11.refs_3_
  32.2 1.5 %shard_map.92 = (bf16[32,1024]{1,0:T(8,128)(2,1)}, bf16[1,32]{1,0:T(2,128)(2,1)}) custom-call(s32[2]{0:T(128)S(1)} %pad_add_fusion.where_ref, bf16[32,1152]{1,0:T(8,128)(2,1)S(1)} %shard_map.85.refs_0_.own_ref, bf16[24,1152]{1,0:T(8,128)(2,1)S(1)} %get-tuple-element.25.refs_0_, bf16[24,1152]{1,0:T(8,128)(2,1)S(1)} %collective-permute-done.9.refs_1_, ...), custom_call_target="tpu_custom_call" | custom-call | bytes 361032 | tf_op jit(solution)/shard_map/pallas_call | solution.py:25
  (3 shorter events, 0.1 us)
Async XLA Ops:
  0.7 0.8 %copy-start.1 = (bf16[32,1024]{1,0:T(8,128)(2,1)S(1)}, bf16[32,1024]{1,0:T(8,128)(2,1)}, u32[]{:S(2)}) copy-start(bf16[32,1024]{1,0:T(8,128)(2,1)} %rows_ref.1) | copy-start | bytes 196612
  0.7 0.8 %copy-start.3 = (s32[32,1]{0,1:T(1,128)S(1)}, s32[32,1]{0,1:T(1,128)}, u32[]{:S(2)}) copy-start(s32[32,1]{0,1:T(1,128)} %param.6) | copy-start | bytes 388
  0.7 0.8 %copy-start.4 = (bf16[32]{0:T(256)(128)(2,1)S(1)}, bf16[32]{0:T(256)(128)(2,1)}, u32[]{:S(2)}) copy-start(bf16[32]{0:T(256)(128)(2,1)} %param.7) | copy-start | bytes 196
  1.7 8.8 %collective-permute-start.6 = (bf16[32,1152]{1,0:T(8,128)(2,1)S(1)}, bf16[32,1152]{1,0:T(8,128)(2,1)S(1)}, u32[]{:S(2)}, u32[]{:S(2)}) collective-permute-start(bf16[32,1152]{1,0:T(8,128)(2,1)S(1)} %shard_map.85.refs_0_.own_ref), channel_id=1, source_target_pairs={{0,3},{1,2},{2,1},{3,0},{4,7},{5,6},{6,5},{7,4},{8,11},{9,10},{10,... | collective-permute-start | bytes 221192 | tf_op jit(solution)/shard_map/ppermute | solution.py:37
  6.8 6.2 %collective-permute-start.5 = (bf16[32,1152]{1,0:T(8,128)(2,1)S(1)}, bf16[32,1152]{1,0:T(8,128)(2,1)S(1)}, u32[]{:S(2)}, u32[]{:S(2)}) collective-permute-start(bf16[32,1152]{1,0:T(8,128)(2,1)S(1)} %shard_map.85.refs_0_.own_ref), channel_id=1, source_target_pairs={{0,2},{1,3},{2,0},{3,1},{4,6},{5,7},{6,4},{7,5},{8,10},{9,11},{10,... | collective-permute-start | bytes 221192 | tf_op jit(solution)/shard_map/ppermute | solution.py:37
  6.8 6.2 %collective-permute-start.4 = (bf16[32,1152]{1,0:T(8,128)(2,1)S(1)}, bf16[32,1152]{1,0:T(8,128)(2,1)S(1)}, u32[]{:S(2)}, u32[]{:S(2)}) collective-permute-start(bf16[32,1152]{1,0:T(8,128)(2,1)S(1)} %shard_map.85.refs_0_.own_ref), channel_id=1, source_target_pairs={{0,1},{1,0},{2,3},{3,2},{4,5},{5,4},{6,7},{7,6},{8,9},{9,8},{10,11... | collective-permute-start | bytes 221192 | tf_op jit(solution)/shard_map/ppermute | solution.py:37
  7.4 5.7 %collective-permute-start.2 = (bf16[32,1152]{1,0:T(8,128)(2,1)S(1)}, bf16[32,1152]{1,0:T(8,128)(2,1)S(1)}, u32[]{:S(2)}, u32[]{:S(2)}) collective-permute-start(bf16[32,1152]{1,0:T(8,128)(2,1)S(1)} %shard_map.85.refs_0_.own_ref), channel_id=1, source_target_pairs={{0,24},{4,28},{8,16},{12,20},{16,8},{20,12},{24,0},{28,4},{1,25},{... | collective-permute-start | bytes 221192 | tf_op jit(solution)/shard_map/ppermute | solution.py:37
  10.0 4.4 %collective-permute-start.1 = (bf16[32,1152]{1,0:T(8,128)(2,1)S(1)}, bf16[32,1152]{1,0:T(8,128)(2,1)S(1)}, u32[]{:S(2)}, u32[]{:S(2)}) collective-permute-start(bf16[32,1152]{1,0:T(8,128)(2,1)S(1)} %shard_map.85.refs_0_.own_ref), channel_id=1, source_target_pairs={{0,16},{4,20},{8,24},{12,28},{16,0},{20,4},{24,8},{28,12},{1,17},{... | collective-permute-start | bytes 221192 | tf_op jit(solution)/shard_map/ppermute | solution.py:37
  10.5 4.4 %collective-permute-start = (bf16[32,1152]{1,0:T(8,128)(2,1)S(1)}, bf16[32,1152]{1,0:T(8,128)(2,1)S(1)}, u32[]{:S(2)}, u32[]{:S(2)}) collective-permute-start(bf16[32,1152]{1,0:T(8,128)(2,1)S(1)} %shard_map.85.refs_0_.own_ref), channel_id=1, source_target_pairs={{0,8},{4,12},{8,0},{12,4},{16,24},{20,28},{24,16},{28,20},{1,9},{5... | collective-permute-start | bytes 221192 | tf_op jit(solution)/shard_map/ppermute | solution.py:37
  13.0 2.0 %collective-permute-start.7 = (bf16[96,1152]{1,0:T(8,128)(2,1)S(1)}, bf16[96,1152]{1,0:T(8,128)(2,1)S(1)}, u32[]{:S(2)}, u32[]{:S(2)}) collective-permute-start(bf16[96,1152]{1,0:T(8,128)(2,1)S(1)} %shard_map.87.far_ref), channel_id=1, source_target_pairs={{0,4},{4,0},{8,12},{12,8},{16,20},{20,16},{24,28},{28,24},{1,5},{5... | collective-permute-start | bytes 663560 | tf_op jit(solution)/shard_map/ppermute | solution.py:37
  14.9 4.9 %copy-start = (bf16[1,1024,2048]{2,1,0:T(8,128)(2,1)S(1)}, bf16[1,1024,2048]{2,1,0:T(8,128)(2,1)}, u32[]{:S(2)}) copy-start(bf16[1,1024,2048]{2,1,0:T(8,128)(2,1)} %param.8) | copy-start | bytes 12582916
  14.9 4.9 %copy-start.2 = (bf16[1,2048]{1,0:T(2,128)(2,1)S(1)}, bf16[1,2048]{1,0:T(2,128)(2,1)}, u32[]{:S(2)}) copy-start(bf16[1,2048]{1,0:T(2,128)(2,1)} %refs_6_.1) | copy-start | bytes 12292
  14.9 4.9 %collective-permute-start.3 = (bf16[128,1152]{1,0:T(8,128)(2,1)S(1)}, bf16[128,1152]{1,0:T(8,128)(2,1)S(1)}, u32[]{:S(2)}, u32[]{:S(2)}) collective-permute-start(bf16[128,1152]{1,0:T(8,128)(2,1)S(1)} %shard_map.86.near_ref), channel_id=1, source_target_pairs={{0,4},{4,0},{8,12},{12,8},{16,20},{20,16},{24,28},{28,24},{1,5},{5... | collective-permute-start | bytes 884744 | tf_op jit(solution)/shard_map/ppermute | solution.py:37
  16.3 10.9 %collective-permute-start.12 = (bf16[72,1152]{1,0:T(8,128)(2,1)S(1)}, bf16[72,1152]{1,0:T(8,128)(2,1)S(1)}, u32[]{:S(2)}, u32[]{:S(2)}) collective-permute-start(bf16[72,1152]{1,0:T(8,128)(2,1)S(1)} %get-tuple-element.29), channel_id=1, source_target_pairs={{0,8},{4,12},{8,0},{12,4},{16,24},{20,28},{24,16},{28,20},{1,9},{5... | collective-permute-start | bytes 497672 | tf_op jit(solution)/shard_map/ppermute | solution.py:37
  17.4 10.7 %collective-permute-start.13 = (bf16[72,1152]{1,0:T(8,128)(2,1)S(1)}, bf16[72,1152]{1,0:T(8,128)(2,1)S(1)}, u32[]{:S(2)}, u32[]{:S(2)}) collective-permute-start(bf16[72,1152]{1,0:T(8,128)(2,1)S(1)} %get-tuple-element.30), channel_id=1, source_target_pairs={{0,16},{4,20},{8,24},{12,28},{16,0},{20,4},{24,8},{28,12},{1,17},{... | collective-permute-start | bytes 497672 | tf_op jit(solution)/shard_map/ppermute | solution.py:37
  18.9 9.2 %collective-permute-start.14 = (bf16[72,1152]{1,0:T(8,128)(2,1)S(1)}, bf16[72,1152]{1,0:T(8,128)(2,1)S(1)}, u32[]{:S(2)}, u32[]{:S(2)}) collective-permute-start(bf16[72,1152]{1,0:T(8,128)(2,1)S(1)} %get-tuple-element.31), channel_id=1, source_target_pairs={{0,24},{4,28},{8,16},{12,20},{16,8},{20,12},{24,0},{28,4},{1,25},{... | collective-permute-start | bytes 497672 | tf_op jit(solution)/shard_map/ppermute | solution.py:37
  23.1 1.4 %collective-permute-start.8 = (bf16[48,1152]{1,0:T(8,128)(2,1)S(1)}, bf16[48,1152]{1,0:T(8,128)(2,1)S(1)}, u32[]{:S(2)}, u32[]{:S(2)}) collective-permute-start(bf16[48,1152]{1,0:T(8,128)(2,1)S(1)} %get-tuple-element.24), channel_id=1, source_target_pairs={{0,4},{4,0},{8,12},{12,8},{16,20},{20,16},{24,28},{28,24},{1,5},{5... | collective-permute-start | bytes 331784 | tf_op jit(solution)/shard_map/ppermute | solution.py:37
  24.5 7.3 %collective-permute-start.9 = (bf16[24,1152]{1,0:T(8,128)(2,1)S(1)}, bf16[24,1152]{1,0:T(8,128)(2,1)S(1)}, u32[]{:S(2)}, u32[]{:S(2)}) collective-permute-start(bf16[24,1152]{1,0:T(8,128)(2,1)S(1)} %get-tuple-element.26), channel_id=1, source_target_pairs={{0,8},{4,12},{8,0},{12,4},{16,24},{20,28},{24,16},{28,20},{1,9},{5... | collective-permute-start | bytes 165896 | tf_op jit(solution)/shard_map/ppermute | solution.py:37
  25.6 6.2 %collective-permute-start.10 = (bf16[24,1152]{1,0:T(8,128)(2,1)S(1)}, bf16[24,1152]{1,0:T(8,128)(2,1)S(1)}, u32[]{:S(2)}, u32[]{:S(2)}) collective-permute-start(bf16[24,1152]{1,0:T(8,128)(2,1)S(1)} %get-tuple-element.27), channel_id=1, source_target_pairs={{0,16},{4,20},{8,24},{12,28},{16,0},{20,4},{24,8},{28,12},{1,17},{... | collective-permute-start | bytes 165896 | tf_op jit(solution)/shard_map/ppermute | solution.py:37
  27.2 5.1 %collective-permute-start.11 = (bf16[24,1152]{1,0:T(8,128)(2,1)S(1)}, bf16[24,1152]{1,0:T(8,128)(2,1)S(1)}, u32[]{:S(2)}, u32[]{:S(2)}) collective-permute-start(bf16[24,1152]{1,0:T(8,128)(2,1)S(1)} %get-tuple-element.28), channel_id=1, source_target_pairs={{0,24},{4,28},{8,16},{12,20},{16,8},{20,12},{24,0},{28,4},{1,25},{... | collective-permute-start | bytes 165896 | tf_op jit(solution)/shard_map/ppermute | solution.py:37

commit v5 on v4

--- a/solution.py
+++ b/solution.py
@@ -75,7 +75,7 @@
 
 
 def gate(preact):
-    sig = 1.0 / (1.0 + jnp.exp(-preact))
+    sig = 0.5 * jnp.tanh(0.5 * preact) + 0.5
     return sig, preact * sig
 
 
@@ -95,7 +95,7 @@
 
 def own_plane(
     chips, rows, where_ref, near_ref, other_ref, w1_ref, w2_ref, after_ref,
-    keep_ref, give_ref, band_ref, kept_ref, readout_ref, hs,
+    keep_ref, give_ref, band_ref, kept_ref, readout_ref, spread_ref, xs, hs,
 ):
     width, hidden = w1_ref.shape
     band = band_ref.shape[1]
@@ -103,9 +103,11 @@
     kept = 2 * chips * CAP
     ids, ranks = ids_and_ranks(near_ref, other_ref)
     slot = jnp.where(ids == where_ref[0], first_slot(2 * half, rows) + ranks, -1)
-    picked = dot(one_hot(slot[:half], kept), near_ref[...], ((0,), (0,)))
-    picked += dot(one_hot(slot[half:], kept), other_ref[...], ((0,), (0,)))
-    kept_ref[...] = picked.astype(BF16)
+    apart = ids[:rows] ^ where_ref[0]
+    spread_ref[...] = one_hot((apart >> 1) * (2 * CAP) + (apart & 1) * CAP + ranks[:rows], kept)
+    xs[:half, :] = near_ref[...]
+    xs[half:, :] = other_ref[...]
+    kept_ref[...] = dot(one_hot(slot, kept), xs[...], ((0,), (0,))).astype(BF16)
     cot = kept_ref[:, width:].astype(F32)[:, 0:1]
     energy = jnp.zeros((kept, 1), F32)
     for c in range(0, hidden, band):
@@ -131,44 +133,41 @@
         out_ref[...] = jnp.concatenate([keep[part, :], got[part, :]], axis=0).astype(BF16)
 
 
-def pick_slots(rows, where_ref, far_ref, other_ref, *outs):
+def pick_slots(rows, where_ref, far_ref, other_ref, *refs):
+    outs, xs = refs[:-1], refs[-1]
     half = far_ref.shape[0]
     size = outs[0].shape[0]
     ids, ranks = ids_and_ranks(far_ref, other_ref)
     apart = ids ^ where_ref[0]
     slot = jnp.where(apart & 1 == 0, (apart >> 1) * size + first_slot(2 * half, rows) + ranks, -1)
-    pick = one_hot(slot, len(outs) * size)
-    picked = dot(pick[:half], far_ref[...], ((0,), (0,)))
-    picked += dot(pick[half:], other_ref[...], ((0,), (0,)))
+    xs[:half, :] = far_ref[...]
+    xs[half:, :] = other_ref[...]
+    picked = dot(one_hot(slot, len(outs) * size), xs[...], ((0,), (0,)))
     for k, out_ref in enumerate(outs):
         out_ref[...] = picked[k * size:(k + 1) * size, :].astype(BF16)
 
 
-def place_rows(n, where_ref, own_ref, *refs):
-    slots, (grad_ref, energy_ref) = refs[:n], refs[-2:]
-    rows, width = grad_ref.shape
+def place_rows(n, spread_ref, w2_grad_ref, *refs):
+    slots, (w2_grad_hbm, grad_ref, energy_ref, ys, sem) = refs[:n], refs[n:]
+    copy = pltpu.make_async_copy(w2_grad_ref, w2_grad_hbm, sem)
+    copy.start()
+    width = grad_ref.shape[1]
     size = slots[0].shape[0]
-    ids, ranks = ids_and_ranks(own_ref)
-    apart = ids ^ where_ref[0]
-    slot = (apart >> 1) * size + (apart & 1) * CAP + ranks
-    total = dot(one_hot(slot, size), slots[0][...])
-    for k in range(1, n):
-        total += dot(one_hot(slot - k * size, size), slots[k][...])
-    grad_ref[...] = total[:, :width].astype(BF16)
-    eye = iota((rows, rows), 0) == iota((rows, rows), 1)
-    line = jnp.sum(jnp.where(eye, total[:, width:width + 1], 0.0), axis=0, keepdims=True)
-    energy_ref[...] = line.astype(BF16)
+    for k in range(n):
+        ys[k * size:(k + 1) * size, :] = slots[k][...]
+    grad_ref[...] = dot(spread_ref[...], ys[:, :width]).astype(BF16)
+    energy_ref[...] = dot(ys[:, width:], spread_ref[...], ((0,), (1,)))[:1, :].astype(BF16)
+    copy.wait()
 
 
 def all_replicas(n, where_ref, *refs):
     slots = refs[:n]
-    kept_ref, w1_ref, w2_ref, band_ref, readout_ref, w1_grad_hbm, w2_grad_ref, token_ref = refs[n:n + 8]
-    ys, hs, w1_grad_ref, sem = refs[n + 8:]
+    kept_ref, w1_ref, w2_ref, band_ref, readout_ref, w1_grad_hbm, w2_grad_ref = refs[n:n + 7]
+    ys, hs, w1_grad_ref, sem = refs[n + 7:]
     size, kept = slots[0].shape[0], kept_ref.shape[0]
     width, hidden = w1_ref.shape
     band = band_ref.shape[1]
     new = n * size
-    token_ref[...] = jnp.zeros(token_ref.shape, F32)
     for k in range(n):
         ys[k * size:(k + 1) * size, :] = slots[k][...]
     ys[new:, :] = kept_ref[...]
@@ -224,23 +223,27 @@
     size = 2 * (replicas - 1) * CAP
     chosen = call(
         functools.partial(pick_slots, rows), [shape(size, wide)] * chips, (where, far, far_other),
+        (pltpu.VMEM((2 * far.shape[0], wide), BF16),),
         flops=WAIT, scalars=1,
     )
     slots = to_chips(chosen)
 
-    keep, give, band_grad, kept_rows, readout_part = call(
+    keep, give, band_grad, kept_rows, readout_part, spread = call(
         functools.partial(own_plane, chips, rows),
-        [shape(kept // 2, wide), shape(kept // 2, wide), shape(kept, band), shape(kept, wide), shape(1, hidden, dtype=F32)],
+        [
+            shape(kept // 2, wide), shape(kept // 2, wide), shape(kept, band), shape(kept, wide),
+            shape(1, hidden, dtype=F32), shape(rows, kept),
+        ],
         (where, near, near_other, weight, readout, chosen[0]),
-        (pltpu.VMEM((kept, hidden), BF16),),
+        (pltpu.VMEM((owners * rows, wide), BF16), pltpu.VMEM((kept, hidden), BF16)),
         flops=4 * kept * width * hidden, scalars=1,
     )
     got = swap(give, "expert", 1)
     back = to_chips(call(join_cores, [shape(2 * CAP, wide)] * chips, (keep, got)))
 
-    w1_grad, w2_grad, token = call(
+    w1_grad, w2_grad = call(
         functools.partial(all_replicas, chips),
-        (shape(band, width), shape(1, hidden, dtype=F32), shape(1, LANES, dtype=F32)),
+        (shape(band, width), shape(1, hidden, dtype=F32)),
         (where, *slots, kept_rows, weight, readout, band_grad, readout_part),
         (
             pltpu.VMEM((chips * size + kept, wide), BF16), pltpu.VMEM((chips * size + kept, band), BF16),
@@ -249,9 +252,10 @@
         flops=4 * WAIT, scalars=1, hbm_outs=1,
     )
 
-    descriptor_grad, energies = call(
-        functools.partial(place_rows, chips), (shape(rows, width), shape(1, rows)),
-        (where, own, *back, token), scalars=1,
+    w2_grad, descriptor_grad, energies = call(
+        functools.partial(place_rows, chips),
+        (shape(1, hidden, dtype=F32), shape(rows, width), shape(1, rows)),
+        (spread, w2_grad, *back), (pltpu.VMEM((kept, wide), BF16), DMA), hbm_outs=1,
     )
     return energies.reshape(rows), descriptor_grad, w1_grad[None], w2_grad
 

time: 33.9 us -> 33.4 us (0.985)
  Pallas kernels: 10.6 us -> 9.37 us
  waiting for transfers between devices: 5.04 us -> 5.7 us
    pallas_call x9, Pallas kernels: 10.6 us -> 9.37 us  [call(): pl.pallas_call(kernel, out_shape=out_shape, in_specs=[SMEM] * scalars + [...]
    ppermute x15, waiting for transfers between devices: 5.04 us -> 5.7 us  [swap(): lax.ppermute(x, axis, [(i, i ^ k) for i in range(lax.axis_size(axis))])]
  transfers between devices with their start and end apart: 15 -> 15, of which waited for: 5 -> 5; matrix products, arithmetic and copies ran while one was open for 0% -> 0% of each run, Pallas kernels for 25% -> 22%
where the time goes in v5:
time: 33.4 us; the launch traced here: 33.2 us
  starting transfers between devices  17 us (51%)
  Pallas kernels  9.37 us (28%)
  waiting for transfers between devices  5.7 us (17%)
  between operations  0.77 us (2%)
    ppermute x15, starting transfers between devices, swap(): lax.ppermute(x, axis, [(i, i ^ k) for i in range(lax.axis_size(axis))])  17 us
    pallas_call x9, Pallas kernels, call(): pl.pallas_call(kernel, out_shape=out_shape, in_specs=[SMEM] * scalars + [...  9.37 us
    ppermute x15, waiting for transfers between devices, swap(): lax.ppermute(x, axis, [(i, i ^ k) for i in range(lax.axis_size(axis))])  5.7 us
  transfers between devices with their start and end apart: 15, of which 5 were waited for; matrix products, arithmetic and copies ran while one was open for 0% of the time, Pallas kernels for 22%

profile of v5, /device:TPU:0, one launch (start us, length us, event | category | flops | bytes accessed | tf_op | source)
XLA Modules:
  0.0 33.2 jit_solution(12563536106902499555)
XLA Ops:
  0.6 0.1 pad_add_fusion.where_ref
  0.7 0.0 copy-start.1
  0.7 0.0 copy-start.3
  0.7 0.0 copy-start.4
  0.7 0.5 %shard_map.84.after_ref = f32[1,128]{1,0:T(1,128)S(1)} custom-call(s32[2]{0:T(128)S(1)} %pad_add_fusion.where_ref), custom_call_target="tpu_custom_call" | custom-call | flops 5000000000 | bytes 520 | tf_op jit(solution)/shard_map/pallas_call | solution.py:25
  1.3 0.3 copy-done.1
  1.6 0.0 copy-done.3
  1.6 0.0 copy-done.4
  1.6 0.2 shard_map.85.refs_0_
  1.7 5.1 %collective-permute-start.6 = (bf16[32,1152]{1,0:T(8,128)(2,1)S(1)}, bf16[32,1152]{1,0:T(8,128)(2,1)S(1)}, u32[]{:S(2)}, u32[]{:S(2)}) collective-permute-start(bf16[32,1152]{1,0:T(8,128)(2,1)S(1)} %shard_map.85.refs_0_), channel_id=1, source_target_pairs={{0,3},{1,2},{2,1},{3,0},{4,7},{5,6},{6,5},{7,4},{8,11},{9,10},{10,... | collective-permute-start | bytes 221192 | tf_op jit(solution)/shard_map/ppermute | solution.py:37
  6.8 0.0 collective-permute-start.5
  6.8 0.6 %collective-permute-start.4 = (bf16[32,1152]{1,0:T(8,128)(2,1)S(1)}, bf16[32,1152]{1,0:T(8,128)(2,1)S(1)}, u32[]{:S(2)}, u32[]{:S(2)}) collective-permute-start(bf16[32,1152]{1,0:T(8,128)(2,1)S(1)} %shard_map.85.refs_0_), channel_id=1, source_target_pairs={{0,1},{1,0},{2,3},{3,2},{4,5},{5,4},{6,7},{7,6},{8,9},{9,8},{10,11... | collective-permute-start | bytes 221192 | tf_op jit(solution)/shard_map/ppermute | solution.py:37
  7.4 2.6 %collective-permute-start.2 = (bf16[32,1152]{1,0:T(8,128)(2,1)S(1)}, bf16[32,1152]{1,0:T(8,128)(2,1)S(1)}, u32[]{:S(2)}, u32[]{:S(2)}) collective-permute-start(bf16[32,1152]{1,0:T(8,128)(2,1)S(1)} %shard_map.85.refs_0_), channel_id=1, source_target_pairs={{0,24},{4,28},{8,16},{12,20},{16,8},{20,12},{24,0},{28,4},{1,25},{... | collective-permute-start | bytes 221192 | tf_op jit(solution)/shard_map/ppermute | solution.py:37
  10.0 0.5 %collective-permute-start.1 = (bf16[32,1152]{1,0:T(8,128)(2,1)S(1)}, bf16[32,1152]{1,0:T(8,128)(2,1)S(1)}, u32[]{:S(2)}, u32[]{:S(2)}) collective-permute-start(bf16[32,1152]{1,0:T(8,128)(2,1)S(1)} %shard_map.85.refs_0_), channel_id=1, source_target_pairs={{0,16},{4,20},{8,24},{12,28},{16,0},{20,4},{24,8},{28,12},{1,17},{... | collective-permute-start | bytes 221192 | tf_op jit(solution)/shard_map/ppermute | solution.py:37
  10.5 0.0 collective-permute-done.6.refs_2_
  10.5 0.9 %collective-permute-start = (bf16[32,1152]{1,0:T(8,128)(2,1)S(1)}, bf16[32,1152]{1,0:T(8,128)(2,1)S(1)}, u32[]{:S(2)}, u32[]{:S(2)}) collective-permute-start(bf16[32,1152]{1,0:T(8,128)(2,1)S(1)} %shard_map.85.refs_0_), channel_id=1, source_target_pairs={{0,8},{4,12},{8,0},{12,4},{16,24},{20,28},{24,16},{28,20},{1,9},{5... | collective-permute-start | bytes 221192 | tf_op jit(solution)/shard_map/ppermute | solution.py:37
  11.4 1.6 %collective-permute-done.5.refs_1_ = bf16[32,1152]{1,0:T(8,128)(2,1)S(1)} collective-permute-done((bf16[32,1152]{1,0:T(8,128)(2,1)S(1)}, bf16[32,1152]{1,0:T(8,128)(2,1)S(1)}, u32[]{:S(2)}, u32[]{:S(2)}) %collective-permute-start.5) | collective-permute-done | bytes 73760 | tf_op jit(solution)/shard_map/ppermute | solution.py:37
  13.0 0.0 collective-permute-done.4.refs_0_
  13.0 0.1 collective-permute-start.7
  13.1 0.0 collective-permute-done.2.refs_3_
  13.1 1.3 %collective-permute-done.1.refs_2_ = bf16[32,1152]{1,0:T(8,128)(2,1)S(1)} collective-permute-done((bf16[32,1152]{1,0:T(8,128)(2,1)S(1)}, bf16[32,1152]{1,0:T(8,128)(2,1)S(1)}, u32[]{:S(2)}, u32[]{:S(2)}) %collective-permute-start.1) | collective-permute-done | bytes 73760 | tf_op jit(solution)/shard_map/ppermute | solution.py:37
  14.4 0.5 %collective-permute-done.refs_1_ = bf16[32,1152]{1,0:T(8,128)(2,1)S(1)} collective-permute-done((bf16[32,1152]{1,0:T(8,128)(2,1)S(1)}, bf16[32,1152]{1,0:T(8,128)(2,1)S(1)}, u32[]{:S(2)}, u32[]{:S(2)}) %collective-permute-start) | collective-permute-done | bytes 73760 | tf_op jit(solution)/shard_map/ppermute | solution.py:37
  14.9 0.0 copy-start
  14.9 0.0 copy-start.2
  14.9 0.1 collective-permute-start.3
  15.0 0.0 collective-permute-done.7.other_ref
  15.0 1.1 %shard_map.88 = (bf16[72,1152]{1,0:T(8,128)(2,1)S(1)}, bf16[72,1152]{1,0:T(8,128)(2,1)S(1)}, bf16[72,1152]{1,0:T(8,128)(2,1)S(1)}, bf16[72,1152]{1,0:T(8,128)(2,1)S(1)}) custom-call(s32[2]{0:T(128)S(1)} %pad_add_fusion.where_ref, bf16[96,1152]{1,0:T(8,128)(2,1)S(1)} %shard_map.87.far_ref, bf16[96,1152]{1,0:T(8,128)(2,1)S(1)} %collective-permute-done.7.other_ref), custom_call_target="tpu_custom_call" | custom-call | flops 5000000000 | bytes 1105928 | tf_op jit(solution)/shard_map/pallas_call | solution.py:25
  16.1 1.1 %collective-permute-start.8 = (bf16[72,1152]{1,0:T(8,128)(2,1)S(1)}, bf16[72,1152]{1,0:T(8,128)(2,1)S(1)}, u32[]{:S(2)}, u32[]{:S(2)}) collective-permute-start(bf16[72,1152]{1,0:T(8,128)(2,1)S(1)} %get-tuple-element.25), channel_id=1, source_target_pairs={{0,8},{4,12},{8,0},{12,4},{16,24},{20,28},{24,16},{28,20},{1,9},{5... | collective-permute-start | bytes 497672 | tf_op jit(solution)/shard_map/ppermute | solution.py:37
  17.2 1.5 %collective-permute-start.9 = (bf16[72,1152]{1,0:T(8,128)(2,1)S(1)}, bf16[72,1152]{1,0:T(8,128)(2,1)S(1)}, u32[]{:S(2)}, u32[]{:S(2)}) collective-permute-start(bf16[72,1152]{1,0:T(8,128)(2,1)S(1)} %get-tuple-element.26), channel_id=1, source_target_pairs={{0,16},{4,20},{8,24},{12,28},{16,0},{20,4},{24,8},{28,12},{1,17},{... | collective-permute-start | bytes 497672 | tf_op jit(solution)/shard_map/ppermute | solution.py:37
  18.7 0.9 %collective-permute-start.10 = (bf16[72,1152]{1,0:T(8,128)(2,1)S(1)}, bf16[72,1152]{1,0:T(8,128)(2,1)S(1)}, u32[]{:S(2)}, u32[]{:S(2)}) collective-permute-start(bf16[72,1152]{1,0:T(8,128)(2,1)S(1)} %get-tuple-element.27), channel_id=1, source_target_pairs={{0,24},{4,28},{8,16},{12,20},{16,8},{20,12},{24,0},{28,4},{1,25},{... | collective-permute-start | bytes 497672 | tf_op jit(solution)/shard_map/ppermute | solution.py:37
  19.7 0.0 collective-permute-done.3.other_ref
  19.7 0.0 copy-done
  19.7 0.0 copy-done.2
  19.7 3.2 %shard_map.89 = (bf16[48,1152]{1,0:T(8,128)(2,1)S(1)}, bf16[48,1152]{1,0:T(8,128)(2,1)S(1)}, bf16[96,512]{1,0:T(8,128)(2,1)S(1)}, bf16[96,1152]{1,0:T(8,128)(2,1...) custom-call(s32[2]{0:T(128)S(1)} %pad_add_fusion.where_ref, bf16[128,1152]{1,0:T(8,128)(2,1)S(1)} %shard_map.86.near_ref, ...), custom_call_target="tpu_custom_call" | custom-call | flops 805306368 | bytes 5509128 | tf_op jit(solution)/shard_map/pallas_call | solution.py:25
  22.8 0.1 collective-permute-start.11
  22.9 1.3 %collective-permute-done.11.got_ref = bf16[48,1152]{1,0:T(8,128)(2,1)S(1)} collective-permute-done((bf16[48,1152]{1,0:T(8,128)(2,1)S(1)}, bf16[48,1152]{1,0:T(8,128)(2,1)S(1)}, u32[]{:S(2)}, u32[]{:S(2)}) %collective-permute-start.11) | collective-permute-done | bytes 110624 | tf_op jit(solution)/shard_map/ppermute | solution.py:37
  24.3 1.1 %collective-permute-start.12 = (bf16[24,1152]{1,0:T(8,128)(2,1)S(1)}, bf16[24,1152]{1,0:T(8,128)(2,1)S(1)}, u32[]{:S(2)}, u32[]{:S(2)}) collective-permute-start(bf16[24,1152]{1,0:T(8,128)(2,1)S(1)} %get-tuple-element.35), channel_id=1, source_target_pairs={{0,8},{4,12},{8,0},{12,4},{16,24},{20,28},{24,16},{28,20},{1,9},{5... | collective-permute-start | bytes 165896 | tf_op jit(solution)/shard_map/ppermute | solution.py:37
  25.4 1.5 %collective-permute-start.13 = (bf16[24,1152]{1,0:T(8,128)(2,1)S(1)}, bf16[24,1152]{1,0:T(8,128)(2,1)S(1)}, u32[]{:S(2)}, u32[]{:S(2)}) collective-permute-start(bf16[24,1152]{1,0:T(8,128)(2,1)S(1)} %get-tuple-element.36), channel_id=1, source_target_pairs={{0,16},{4,20},{8,24},{12,28},{16,0},{20,4},{24,8},{28,12},{1,17},{... | collective-permute-start | bytes 165896 | tf_op jit(solution)/shard_map/ppermute | solution.py:37
  26.9 0.0 collective-permute-done.8.refs_1_
  26.9 0.9 %collective-permute-start.14 = (bf16[24,1152]{1,0:T(8,128)(2,1)S(1)}, bf16[24,1152]{1,0:T(8,128)(2,1)S(1)}, u32[]{:S(2)}, u32[]{:S(2)}) collective-permute-start(bf16[24,1152]{1,0:T(8,128)(2,1)S(1)} %get-tuple-element.37), channel_id=1, source_target_pairs={{0,24},{4,28},{8,16},{12,20},{16,8},{20,12},{24,0},{28,4},{1,25},{... | collective-permute-start | bytes 165896 | tf_op jit(solution)/shard_map/ppermute | solution.py:37
  27.8 0.0 collective-permute-done.9.refs_2_
  27.8 0.0 collective-permute-done.10.refs_3_
  27.8 3.1 %shard_map.90 = (bf16[512,1024]{1,0:T(8,128)(2,1)}, f32[1,2048]{1,0:T(1,128)S(1)}) custom-call(s32[2]{0:T(128)S(1)} %pad_add_fusion.where_ref, bf16[72,1152]{1,0:T(8,128)(2,1)S(1)} %get-tuple-element.23.after_ref.refs_0_, bf16[72,1152]{1,0:T(8,128)(2,1)S(1)} %collective-permute-done.8.refs_1_, bf16[72,1152]{1,0:T(8,128)(2,1)S(1)} %collective-permute-done.9.refs_2_, ...), custom_call_target="tpu_custom_call" | custom-call | flops 20000000000 | bytes 6246408 | tf_op jit(solution)/shard_map/pallas_call | solution.py:25
  30.9 0.0 collective-permute-done.12.refs_1_
  30.9 0.0 collective-permute-done.13.refs_2_
  30.9 1.0 %collective-permute-done.14.refs_3_ = bf16[24,1152]{1,0:T(8,128)(2,1)S(1)} collective-permute-done((bf16[24,1152]{1,0:T(8,128)(2,1)S(1)}, bf16[24,1152]{1,0:T(8,128)(2,1)S(1)}, u32[]{:S(2)}, u32[]{:S(2)}) %collective-permute-start.14) | collective-permute-done | bytes 55328 | tf_op jit(solution)/shard_map/ppermute | solution.py:37
  31.9 1.3 %shard_map.92 = (f32[1,2048]{1,0:T(1,128)}, bf16[32,1024]{1,0:T(8,128)(2,1)}, bf16[1,32]{1,0:T(2,128)(2,1)}) custom-call(bf16[32,96]{1,0:T(8,128)(2,1)S(1)} %get-tuple-element.24.spread_ref, f32[1,2048]{1,0:T(1,128)S(1)} %get-tuple-element.31.w2_grad_ref, bf16[24,1152]{1,0:T(8,128)(2,1)S(1)} %get-tuple-element.34.refs_0_, ...), custom_call_target="tpu_custom_call" | custom-call | bytes 309312 | tf_op jit(solution)/shard_map/pallas_call | solution.py:25
  (3 shorter events, 0.1 us)
Async XLA Ops:
  0.7 0.8 %copy-start.1 = (bf16[32,1024]{1,0:T(8,128)(2,1)S(1)}, bf16[32,1024]{1,0:T(8,128)(2,1)}, u32[]{:S(2)}) copy-start(bf16[32,1024]{1,0:T(8,128)(2,1)} %rows_ref.1) | copy-start | bytes 196612
  0.7 0.8 %copy-start.3 = (s32[32,1]{0,1:T(1,128)S(1)}, s32[32,1]{0,1:T(1,128)}, u32[]{:S(2)}) copy-start(s32[32,1]{0,1:T(1,128)} %param.6) | copy-start | bytes 388
  0.7 0.8 %copy-start.4 = (bf16[32]{0:T(256)(128)(2,1)S(1)}, bf16[32]{0:T(256)(128)(2,1)}, u32[]{:S(2)}) copy-start(bf16[32]{0:T(256)(128)(2,1)} %param.7) | copy-start | bytes 196
  1.7 8.8 %collective-permute-start.6 = (bf16[32,1152]{1,0:T(8,128)(2,1)S(1)}, bf16[32,1152]{1,0:T(8,128)(2,1)S(1)}, u32[]{:S(2)}, u32[]{:S(2)}) collective-permute-start(bf16[32,1152]{1,0:T(8,128)(2,1)S(1)} %shard_map.85.refs_0_), channel_id=1, source_target_pairs={{0,3},{1,2},{2,1},{3,0},{4,7},{5,6},{6,5},{7,4},{8,11},{9,10},{10,... | collective-permute-start | bytes 221192 | tf_op jit(solution)/shard_map/ppermute | solution.py:37
  6.8 6.2 %collective-permute-start.5 = (bf16[32,1152]{1,0:T(8,128)(2,1)S(1)}, bf16[32,1152]{1,0:T(8,128)(2,1)S(1)}, u32[]{:S(2)}, u32[]{:S(2)}) collective-permute-start(bf16[32,1152]{1,0:T(8,128)(2,1)S(1)} %shard_map.85.refs_0_), channel_id=1, source_target_pairs={{0,2},{1,3},{2,0},{3,1},{4,6},{5,7},{6,4},{7,5},{8,10},{9,11},{10,... | collective-permute-start | bytes 221192 | tf_op jit(solution)/shard_map/ppermute | solution.py:37
  6.8 6.2 %collective-permute-start.4 = (bf16[32,1152]{1,0:T(8,128)(2,1)S(1)}, bf16[32,1152]{1,0:T(8,128)(2,1)S(1)}, u32[]{:S(2)}, u32[]{:S(2)}) collective-permute-start(bf16[32,1152]{1,0:T(8,128)(2,1)S(1)} %shard_map.85.refs_0_), channel_id=1, source_target_pairs={{0,1},{1,0},{2,3},{3,2},{4,5},{5,4},{6,7},{7,6},{8,9},{9,8},{10,11... | collective-permute-start | bytes 221192 | tf_op jit(solution)/shard_map/ppermute | solution.py:37
  7.4 5.7 %collective-permute-start.2 = (bf16[32,1152]{1,0:T(8,128)(2,1)S(1)}, bf16[32,1152]{1,0:T(8,128)(2,1)S(1)}, u32[]{:S(2)}, u32[]{:S(2)}) collective-permute-start(bf16[32,1152]{1,0:T(8,128)(2,1)S(1)} %shard_map.85.refs_0_), channel_id=1, source_target_pairs={{0,24},{4,28},{8,16},{12,20},{16,8},{20,12},{24,0},{28,4},{1,25},{... | collective-permute-start | bytes 221192 | tf_op jit(solution)/shard_map/ppermute | solution.py:37
  10.0 4.4 %collective-permute-start.1 = (bf16[32,1152]{1,0:T(8,128)(2,1)S(1)}, bf16[32,1152]{1,0:T(8,128)(2,1)S(1)}, u32[]{:S(2)}, u32[]{:S(2)}) collective-permute-start(bf16[32,1152]{1,0:T(8,128)(2,1)S(1)} %shard_map.85.refs_0_), channel_id=1, source_target_pairs={{0,16},{4,20},{8,24},{12,28},{16,0},{20,4},{24,8},{28,12},{1,17},{... | collective-permute-start | bytes 221192 | tf_op jit(solution)/shard_map/ppermute | solution.py:37
  10.5 4.4 %collective-permute-start = (bf16[32,1152]{1,0:T(8,128)(2,1)S(1)}, bf16[32,1152]{1,0:T(8,128)(2,1)S(1)}, u32[]{:S(2)}, u32[]{:S(2)}) collective-permute-start(bf16[32,1152]{1,0:T(8,128)(2,1)S(1)} %shard_map.85.refs_0_), channel_id=1, source_target_pairs={{0,8},{4,12},{8,0},{12,4},{16,24},{20,28},{24,16},{28,20},{1,9},{5... | collective-permute-start | bytes 221192 | tf_op jit(solution)/shard_map/ppermute | solution.py:37
  13.0 2.0 %collective-permute-start.7 = (bf16[96,1152]{1,0:T(8,128)(2,1)S(1)}, bf16[96,1152]{1,0:T(8,128)(2,1)S(1)}, u32[]{:S(2)}, u32[]{:S(2)}) collective-permute-start(bf16[96,1152]{1,0:T(8,128)(2,1)S(1)} %shard_map.87.far_ref), channel_id=1, source_target_pairs={{0,4},{4,0},{8,12},{12,8},{16,20},{20,16},{24,28},{28,24},{1,5},{5... | collective-permute-start | bytes 663560 | tf_op jit(solution)/shard_map/ppermute | solution.py:37
  14.9 4.8 %copy-start = (bf16[1,1024,2048]{2,1,0:T(8,128)(2,1)S(1)}, bf16[1,1024,2048]{2,1,0:T(8,128)(2,1)}, u32[]{:S(2)}) copy-start(bf16[1,1024,2048]{2,1,0:T(8,128)(2,1)} %param.8) | copy-start | bytes 12582916
  14.9 4.7 %copy-start.2 = (bf16[1,2048]{1,0:T(2,128)(2,1)S(1)}, bf16[1,2048]{1,0:T(2,128)(2,1)}, u32[]{:S(2)}) copy-start(bf16[1,2048]{1,0:T(2,128)(2,1)} %refs_6_.1) | copy-start | bytes 12292
  14.9 4.7 %collective-permute-start.3 = (bf16[128,1152]{1,0:T(8,128)(2,1)S(1)}, bf16[128,1152]{1,0:T(8,128)(2,1)S(1)}, u32[]{:S(2)}, u32[]{:S(2)}) collective-permute-start(bf16[128,1152]{1,0:T(8,128)(2,1)S(1)} %shard_map.86.near_ref), channel_id=1, source_target_pairs={{0,4},{4,0},{8,12},{12,8},{16,20},{20,16},{24,28},{28,24},{1,5},{5... | collective-permute-start | bytes 884744 | tf_op jit(solution)/shard_map/ppermute | solution.py:37
  16.1 10.8 %collective-permute-start.8 = (bf16[72,1152]{1,0:T(8,128)(2,1)S(1)}, bf16[72,1152]{1,0:T(8,128)(2,1)S(1)}, u32[]{:S(2)}, u32[]{:S(2)}) collective-permute-start(bf16[72,1152]{1,0:T(8,128)(2,1)S(1)} %get-tuple-element.25), channel_id=1, source_target_pairs={{0,8},{4,12},{8,0},{12,4},{16,24},{20,28},{24,16},{28,20},{1,9},{5... | collective-permute-start | bytes 497672 | tf_op jit(solution)/shard_map/ppermute | solution.py:37
  17.2 10.6 %collective-permute-start.9 = (bf16[72,1152]{1,0:T(8,128)(2,1)S(1)}, bf16[72,1152]{1,0:T(8,128)(2,1)S(1)}, u32[]{:S(2)}, u32[]{:S(2)}) collective-permute-start(bf16[72,1152]{1,0:T(8,128)(2,1)S(1)} %get-tuple-element.26), channel_id=1, source_target_pairs={{0,16},{4,20},{8,24},{12,28},{16,0},{20,4},{24,8},{28,12},{1,17},{... | collective-permute-start | bytes 497672 | tf_op jit(solution)/shard_map/ppermute | solution.py:37
  18.7 9.1 %collective-permute-start.10 = (bf16[72,1152]{1,0:T(8,128)(2,1)S(1)}, bf16[72,1152]{1,0:T(8,128)(2,1)S(1)}, u32[]{:S(2)}, u32[]{:S(2)}) collective-permute-start(bf16[72,1152]{1,0:T(8,128)(2,1)S(1)} %get-tuple-element.27), channel_id=1, source_target_pairs={{0,24},{4,28},{8,16},{12,20},{16,8},{20,12},{24,0},{28,4},{1,25},{... | collective-permute-start | bytes 497672 | tf_op jit(solution)/shard_map/ppermute | solution.py:37
  22.8 1.4 %collective-permute-start.11 = (bf16[48,1152]{1,0:T(8,128)(2,1)S(1)}, bf16[48,1152]{1,0:T(8,128)(2,1)S(1)}, u32[]{:S(2)}, u32[]{:S(2)}) collective-permute-start(bf16[48,1152]{1,0:T(8,128)(2,1)S(1)} %get-tuple-element.33), channel_id=1, source_target_pairs={{0,4},{4,0},{8,12},{12,8},{16,20},{20,16},{24,28},{28,24},{1,5},{5... | collective-permute-start | bytes 331784 | tf_op jit(solution)/shard_map/ppermute | solution.py:37
  24.3 6.7 %collective-permute-start.12 = (bf16[24,1152]{1,0:T(8,128)(2,1)S(1)}, bf16[24,1152]{1,0:T(8,128)(2,1)S(1)}, u32[]{:S(2)}, u32[]{:S(2)}) collective-permute-start(bf16[24,1152]{1,0:T(8,128)(2,1)S(1)} %get-tuple-element.35), channel_id=1, source_target_pairs={{0,8},{4,12},{8,0},{12,4},{16,24},{20,28},{24,16},{28,20},{1,9},{5... | collective-permute-start | bytes 165896 | tf_op jit(solution)/shard_map/ppermute | solution.py:37
  25.4 5.6 %collective-permute-start.13 = (bf16[24,1152]{1,0:T(8,128)(2,1)S(1)}, bf16[24,1152]{1,0:T(8,128)(2,1)S(1)}, u32[]{:S(2)}, u32[]{:S(2)}) collective-permute-start(bf16[24,1152]{1,0:T(8,128)(2,1)S(1)} %get-tuple-element.36), channel_id=1, source_target_pairs={{0,16},{4,20},{8,24},{12,28},{16,0},{20,4},{24,8},{28,12},{1,17},{... | collective-permute-start | bytes 165896 | tf_op jit(solution)/shard_map/ppermute | solution.py:37
  26.9 5.1 %collective-permute-start.14 = (bf16[24,1152]{1,0:T(8,128)(2,1)S(1)}, bf16[24,1152]{1,0:T(8,128)(2,1)S(1)}, u32[]{:S(2)}, u32[]{:S(2)}) collective-permute-start(bf16[24,1152]{1,0:T(8,128)(2,1)S(1)} %get-tuple-element.37), channel_id=1, source_target_pairs={{0,24},{4,28},{8,16},{12,20},{16,8},{20,12},{24,0},{28,4},{1,25},{... | collective-permute-start | bytes 165896 | tf_op jit(solution)/shard_map/ppermute | solution.py:37

commit v6 on v5

--- a/solution.py
+++ b/solution.py
@@ -61,28 +61,54 @@
     ids = column(jnp.where(i == j, ids_line, 0.0))
     cot = column(jnp.where(i == j, cot_line, 0.0))
     rank = column(jnp.where((j < i) & (ids_line == ids), 1.0, 0.0))
-    lane = iota((rows, LANES), 1)
-    tags = jnp.where(lane == 0, cot, jnp.where(lane == 1, ids, jnp.where(lane == 2, rank, 0.0)))
-    out_ref[:, :width] = rows_ref[...]
-    out_ref[:, width:] = tags.astype(BF16)
+    for k in range(width // LANES):
+        out_ref[k * rows:(k + 1) * rows, :] = rows_ref[:, k * LANES:(k + 1) * LANES]
+    lane, groups = iota((8, LANES), 1), rows // 8
+    tags = jnp.zeros((8, LANES), F32)
+    for field, values in enumerate((cot, ids, rank)):
+        for k in range(groups):
+            tags = jnp.where(lane == field * groups + k, values[8 * k:8 * (k + 1), :], tags)
+    out_ref[width // LANES * rows:, :] = tags.astype(BF16)
 
 
 def stack_blocks(*refs):
     blocks, out_ref = refs[:-1], refs[-1]
-    rows = blocks[0].shape[0]
+    size = blocks[0].shape[0] - 8
     for k, block in enumerate(blocks):
-        out_ref[k * rows:(k + 1) * rows, :] = block[...]
+        out_ref[k * size:(k + 1) * size, :] = block[:size, :]
+    tags = jnp.concatenate([block[size:, :].astype(F32) for block in blocks], axis=0)
+    out_ref[len(blocks) * size:, :] = tags.astype(BF16)
+
+
+def unstack_blocks(rows, stacks, xs):
+    width = xs.shape[1] - LANES
+    tiles, groups = width // LANES, rows // 8
+    tags, at = [], 0
+    for stack in stacks:
+        blocks = stack.shape[0] // (tiles * rows + 8)
+        for b in range(blocks):
+            for k in range(tiles):
+                first = (b * tiles + k) * rows
+                xs[at:at + rows, k * LANES:(k + 1) * LANES] = stack[first:first + rows, :]
+            at += rows
+        tags.append(stack[blocks * tiles * rows:, :].astype(F32))
+    total = xs.shape[0]
+    tags = jnp.concatenate([
+        part[8 * b:8 * (b + 1), :] for part in tags for b in range(part.shape[0] // 8) for _ in range(groups)
+    ], axis=0)
+    lane, row = iota((total, LANES), 1), iota((total, LANES), 0)
+    group = (row >> 3) & (groups - 1)
+
+    def column(field):
+        return jnp.sum(jnp.where(lane == field * groups + group, tags, 0.0), axis=1, keepdims=True)
+
+    xs[:, width:] = jnp.where(lane == 0, column(0), 0.0).astype(BF16)
+    return column(1).astype(jnp.int32), column(2).astype(jnp.int32)
 
 
 def gate(preact):
     sig = 0.5 * jnp.tanh(0.5 * preact) + 0.5
     return sig, preact * sig
-
-
-def ids_and_ranks(*refs):
-    tags = [ref[:, ref.shape[1] - LANES:].astype(F32)[:, 1:3] for ref in refs]
-    tags = (tags[0] if len(tags) == 1 else jnp.concatenate(tags, axis=0)).astype(jnp.int32)
-    return tags[:, 0:1], tags[:, 1:2]
 
 
 def first_slot(total, rows):
@@ -101,12 +127,10 @@
     band = band_ref.shape[1]
     half = chips * rows
     kept = 2 * chips * CAP
-    ids, ranks = ids_and_ranks(near_ref, other_ref)
+    ids, ranks = unstack_blocks(rows, (near_ref, other_ref), xs)
     slot = jnp.where(ids == where_ref[0], first_slot(2 * half, rows) + ranks, -1)
     apart = ids[:rows] ^ where_ref[0]
     spread_ref[...] = one_hot((apart >> 1) * (2 * CAP) + (apart & 1) * CAP + ranks[:rows], kept)
-    xs[:half, :] = near_ref[...]
-    xs[half:, :] = other_ref[...]
     kept_ref[...] = dot(one_hot(slot, kept), xs[...], ((0,), (0,))).astype(BF16)
     cot = kept_ref[:, width:].astype(F32)[:, 0:1]
     energy = jnp.zeros((kept, 1), F32)
@@ -135,13 +159,10 @@
 
 def pick_slots(rows, where_ref, far_ref, other_ref, *refs):
     outs, xs = refs[:-1], refs[-1]
-    half = far_ref.shape[0]
     size = outs[0].shape[0]
-    ids, ranks = ids_and_ranks(far_ref, other_ref)
+    ids, ranks = unstack_blocks(rows, (far_ref, other_ref), xs)
     apart = ids ^ where_ref[0]
-    slot = jnp.where(apart & 1 == 0, (apart >> 1) * size + first_slot(2 * half, rows) + ranks, -1)
-    xs[:half, :] = far_ref[...]
-    xs[half:, :] = other_ref[...]
+    slot = jnp.where(apart & 1 == 0, (apart >> 1) * size + first_slot(xs.shape[0], rows) + ranks, -1)
     picked = dot(one_hot(slot, len(outs) * size), xs[...], ((0,), (0,)))
     for k, out_ref in enumerate(outs):
         out_ref[...] = picked[k * size:(k + 1) * size, :].astype(BF16)
@@ -207,23 +228,24 @@
         return [blocks[0]] + [swap(blocks[k], "expert", 2 * k) for k in range(1, chips)]
 
     begun = call(begin, shape(1, LANES, dtype=F32), (where,), flops=WAIT, scalars=1)
+    length = width // LANES * rows + 8
     own = call(
-        label_rows, shape(rows, wide),
+        label_rows, shape(length, LANES),
         (descriptors, expert_ids.reshape(1, rows), cotangent.reshape(1, rows), begun),
     )
     readout = w2
     weight = w1[0]
     far = [swap(own, "rep", k) for k in range(1, replicas)]
-    far = call(stack_blocks, shape(len(far) * rows, wide), tuple(far), flops=WAIT)
+    far = call(stack_blocks, shape(len(far) * length, LANES), tuple(far), flops=WAIT)
     far_other = swap(far, "expert", 1)
     near = to_chips([own] * chips)
-    near = call(stack_blocks, shape(chips * rows, wide), tuple(near), flops=WAIT)
+    near = call(stack_blocks, shape(chips * length, LANES), tuple(near), flops=WAIT)
     near_other = swap(near, "expert", 1)
 
     size = 2 * (replicas - 1) * CAP
     chosen = call(
         functools.partial(pick_slots, rows), [shape(size, wide)] * chips, (where, far, far_other),
-        (pltpu.VMEM((2 * far.shape[0], wide), BF16),),
+        (pltpu.VMEM((2 * (replicas - 1) * rows, wide), BF16),),
         flops=WAIT, scalars=1,
     )
     slots = to_chips(chosen)

time: 33.4 us -> 33 us (0.988)
  transfers between devices with their start and end apart: 15 -> 15, of which waited for: 5 -> 6; matrix products, arithmetic and copies ran while one was open for 0% -> 0% of each run, Pallas kernels for 22% -> 23%
where the time goes in v6:
time: 33 us; the launch traced here: 32.9 us
  starting transfers between devices  16.8 us (51%)
  Pallas kernels  9.43 us (29%)
  waiting for transfers between devices  5.47 us (17%)
  between operations  0.76 us (2%)
    ppermute x15, starting transfers between devices, swap(): lax.ppermute(x, axis, [(i, i ^ k) for i in range(lax.axis_size(axis))])  16.8 us
    pallas_call x9, Pallas kernels, call(): pl.pallas_call(kernel, out_shape=out_shape, in_specs=[SMEM] * scalars + [...  9.43 us
    ppermute x15, waiting for transfers between devices, swap(): lax.ppermute(x, axis, [(i, i ^ k) for i in range(lax.axis_size(axis))])  5.47 us
  transfers between devices with their start and end apart: 15, of which 6 were waited for; matrix products, arithmetic and copies ran while one was open for 0% of the time, Pallas kernels for 23%

profile of v6, /device:TPU:0, one launch (start us, length us, event | category | flops | bytes accessed | tf_op | source)
XLA Modules:
  0.0 32.9 jit_solution(2570983873957890810)
XLA Ops:
  0.6 0.1 pad_add_fusion.where_ref
  0.7 0.0 copy-start.1
  0.7 0.0 copy-start.3
  0.7 0.0 copy-start.4
  0.7 0.5 %shard_map.84.after_ref = f32[1,128]{1,0:T(1,128)S(1)} custom-call(s32[2]{0:T(128)S(1)} %pad_add_fusion.where_ref), custom_call_target="tpu_custom_call" | custom-call | flops 5000000000 | bytes 520 | tf_op jit(solution)/shard_map/pallas_call | solution.py:25
  1.3 0.3 copy-done.1
  1.6 0.0 copy-done.3
  1.6 0.0 copy-done.4
  1.6 0.2 shard_map.85.refs_0_
  1.7 5.0 %collective-permute-start.6 = (bf16[264,128]{1,0:T(8,128)(2,1)S(1)}, bf16[264,128]{1,0:T(8,128)(2,1)S(1)}, u32[]{:S(2)}, u32[]{:S(2)}) collective-permute-start(bf16[264,128]{1,0:T(8,128)(2,1)S(1)} %shard_map.85.refs_0_), channel_id=1, source_target_pairs={{0,3},{1,2},{2,1},{3,0},{4,7},{5,6},{6,5},{7,4},{8,11},{9,10},{10,... | collective-permute-start | bytes 202760 | tf_op jit(solution)/shard_map/ppermute | solution.py:37
  6.8 0.0 collective-permute-start.5
  6.8 0.6 %collective-permute-start.4 = (bf16[264,128]{1,0:T(8,128)(2,1)S(1)}, bf16[264,128]{1,0:T(8,128)(2,1)S(1)}, u32[]{:S(2)}, u32[]{:S(2)}) collective-permute-start(bf16[264,128]{1,0:T(8,128)(2,1)S(1)} %shard_map.85.refs_0_), channel_id=1, source_target_pairs={{0,1},{1,0},{2,3},{3,2},{4,5},{5,4},{6,7},{7,6},{8,9},{9,8},{10,11... | collective-permute-start | bytes 202760 | tf_op jit(solution)/shard_map/ppermute | solution.py:37
  7.4 2.6 %collective-permute-start.2 = (bf16[264,128]{1,0:T(8,128)(2,1)S(1)}, bf16[264,128]{1,0:T(8,128)(2,1)S(1)}, u32[]{:S(2)}, u32[]{:S(2)}) collective-permute-start(bf16[264,128]{1,0:T(8,128)(2,1)S(1)} %shard_map.85.refs_0_), channel_id=1, source_target_pairs={{0,24},{4,28},{8,16},{12,20},{16,8},{20,12},{24,0},{28,4},{1,25},{... | collective-permute-start | bytes 202760 | tf_op jit(solution)/shard_map/ppermute | solution.py:37
  10.0 0.5 %collective-permute-start.1 = (bf16[264,128]{1,0:T(8,128)(2,1)S(1)}, bf16[264,128]{1,0:T(8,128)(2,1)S(1)}, u32[]{:S(2)}, u32[]{:S(2)}) collective-permute-start(bf16[264,128]{1,0:T(8,128)(2,1)S(1)} %shard_map.85.refs_0_), channel_id=1, source_target_pairs={{0,16},{4,20},{8,24},{12,28},{16,0},{20,4},{24,8},{28,12},{1,17},{... | collective-permute-start | bytes 202760 | tf_op jit(solution)/shard_map/ppermute | solution.py:37
  10.5 0.0 collective-permute-done.6.refs_2_
  10.5 0.7 %collective-permute-start = (bf16[264,128]{1,0:T(8,128)(2,1)S(1)}, bf16[264,128]{1,0:T(8,128)(2,1)S(1)}, u32[]{:S(2)}, u32[]{:S(2)}) collective-permute-start(bf16[264,128]{1,0:T(8,128)(2,1)S(1)} %shard_map.85.refs_0_), channel_id=1, source_target_pairs={{0,8},{4,12},{8,0},{12,4},{16,24},{20,28},{24,16},{28,20},{1,9},{5... | collective-permute-start | bytes 202760 | tf_op jit(solution)/shard_map/ppermute | solution.py:37
  11.2 1.3 %collective-permute-done.5.refs_1_ = bf16[264,128]{1,0:T(8,128)(2,1)S(1)} collective-permute-done((bf16[264,128]{1,0:T(8,128)(2,1)S(1)}, bf16[264,128]{1,0:T(8,128)(2,1)S(1)}, u32[]{:S(2)}, u32[]{:S(2)}) %collective-permute-start.5) | collective-permute-done | bytes 67616 | tf_op jit(solution)/shard_map/ppermute | solution.py:37
  12.5 0.0 collective-permute-done.4.refs_0_
  12.5 0.1 collective-permute-start.7
  12.6 0.1 collective-permute-done.2.refs_3_
  12.7 1.6 %collective-permute-done.1.refs_2_ = bf16[264,128]{1,0:T(8,128)(2,1)S(1)} collective-permute-done((bf16[264,128]{1,0:T(8,128)(2,1)S(1)}, bf16[264,128]{1,0:T(8,128)(2,1)S(1)}, u32[]{:S(2)}, u32[]{:S(2)}) %collective-permute-start.1) | collective-permute-done | bytes 67616 | tf_op jit(solution)/shard_map/ppermute | solution.py:37
  14.3 0.5 %collective-permute-done.refs_1_ = bf16[264,128]{1,0:T(8,128)(2,1)S(1)} collective-permute-done((bf16[264,128]{1,0:T(8,128)(2,1)S(1)}, bf16[264,128]{1,0:T(8,128)(2,1)S(1)}, u32[]{:S(2)}, u32[]{:S(2)}) %collective-permute-start) | collective-permute-done | bytes 67616 | tf_op jit(solution)/shard_map/ppermute | solution.py:37
  14.8 0.0 copy-start
  14.8 0.0 copy-start.2
  14.8 0.1 collective-permute-start.3
  14.9 0.0 collective-permute-done.7.other_ref
  14.9 1.1 %shard_map.88 = (bf16[72,1152]{1,0:T(8,128)(2,1)S(1)}, bf16[72,1152]{1,0:T(8,128)(2,1)S(1)}, bf16[72,1152]{1,0:T(8,128)(2,1)S(1)}, bf16[72,1152]{1,0:T(8,128)(2,1)S(1)}) custom-call(s32[2]{0:T(128)S(1)} %pad_add_fusion.where_ref, bf16[792,128]{1,0:T(8,128)(2,1)S(1)} %shard_map.87.far_ref, bf16[792,128]{1,0:T(8,128)(2,1)S(1)} %collective-permute-done.7.other_ref), custom_call_target="tpu_custom_call" | custom-call | flops 5000000000 | bytes 1069064 | tf_op jit(solution)/shard_map/pallas_call | solution.py:25
  16.0 0.8 %collective-permute-start.8 = (bf16[72,1152]{1,0:T(8,128)(2,1)S(1)}, bf16[72,1152]{1,0:T(8,128)(2,1)S(1)}, u32[]{:S(2)}, u32[]{:S(2)}) collective-permute-start(bf16[72,1152]{1,0:T(8,128)(2,1)S(1)} %get-tuple-element.25), channel_id=1, source_target_pairs={{0,8},{4,12},{8,0},{12,4},{16,24},{20,28},{24,16},{28,20},{1,9},{5... | collective-permute-start | bytes 497672 | tf_op jit(solution)/shard_map/ppermute | solution.py:37
  16.8 1.5 %collective-permute-start.9 = (bf16[72,1152]{1,0:T(8,128)(2,1)S(1)}, bf16[72,1152]{1,0:T(8,128)(2,1)S(1)}, u32[]{:S(2)}, u32[]{:S(2)}) collective-permute-start(bf16[72,1152]{1,0:T(8,128)(2,1)S(1)} %get-tuple-element.26), channel_id=1, source_target_pairs={{0,16},{4,20},{8,24},{12,28},{16,0},{20,4},{24,8},{28,12},{1,17},{... | collective-permute-start | bytes 497672 | tf_op jit(solution)/shard_map/ppermute | solution.py:37
  18.3 1.2 %collective-permute-start.10 = (bf16[72,1152]{1,0:T(8,128)(2,1)S(1)}, bf16[72,1152]{1,0:T(8,128)(2,1)S(1)}, u32[]{:S(2)}, u32[]{:S(2)}) collective-permute-start(bf16[72,1152]{1,0:T(8,128)(2,1)S(1)} %get-tuple-element.27), channel_id=1, source_target_pairs={{0,24},{4,28},{8,16},{12,20},{16,8},{20,12},{24,0},{28,4},{1,25},{... | collective-permute-start | bytes 497672 | tf_op jit(solution)/shard_map/ppermute | solution.py:37
  19.6 0.0 collective-permute-done.3.other_ref
  19.6 0.0 copy-done
  19.6 0.0 copy-done.2
  19.6 3.2 %shard_map.89 = (bf16[48,1152]{1,0:T(8,128)(2,1)S(1)}, bf16[48,1152]{1,0:T(8,128)(2,1)S(1)}, bf16[96,512]{1,0:T(8,128)(2,1)S(1)}, bf16[96,1152]{1,0:T(8,128)(2,1...) custom-call(s32[2]{0:T(128)S(1)} %pad_add_fusion.where_ref, bf16[1056,128]{1,0:T(8,128)(2,1)S(1)} %shard_map.86.near_ref, ...), custom_call_target="tpu_custom_call" | custom-call | flops 805306368 | bytes 5459976 | tf_op jit(solution)/shard_map/pallas_call | solution.py:25
  22.8 0.1 collective-permute-start.11
  22.9 1.3 %collective-permute-done.11.got_ref = bf16[48,1152]{1,0:T(8,128)(2,1)S(1)} collective-permute-done((bf16[48,1152]{1,0:T(8,128)(2,1)S(1)}, bf16[48,1152]{1,0:T(8,128)(2,1)S(1)}, u32[]{:S(2)}, u32[]{:S(2)}) %collective-permute-start.11) | collective-permute-done | bytes 110624 | tf_op jit(solution)/shard_map/ppermute | solution.py:37
  24.2 0.8 %collective-permute-start.12 = (bf16[24,1152]{1,0:T(8,128)(2,1)S(1)}, bf16[24,1152]{1,0:T(8,128)(2,1)S(1)}, u32[]{:S(2)}, u32[]{:S(2)}) collective-permute-start(bf16[24,1152]{1,0:T(8,128)(2,1)S(1)} %get-tuple-element.35), channel_id=1, source_target_pairs={{0,8},{4,12},{8,0},{12,4},{16,24},{20,28},{24,16},{28,20},{1,9},{5... | collective-permute-start | bytes 165896 | tf_op jit(solution)/shard_map/ppermute | solution.py:37
  25.0 1.5 %collective-permute-start.13 = (bf16[24,1152]{1,0:T(8,128)(2,1)S(1)}, bf16[24,1152]{1,0:T(8,128)(2,1)S(1)}, u32[]{:S(2)}, u32[]{:S(2)}) collective-permute-start(bf16[24,1152]{1,0:T(8,128)(2,1)S(1)} %get-tuple-element.36), channel_id=1, source_target_pairs={{0,16},{4,20},{8,24},{12,28},{16,0},{20,4},{24,8},{28,12},{1,17},{... | collective-permute-start | bytes 165896 | tf_op jit(solution)/shard_map/ppermute | solution.py:37
  26.6 0.0 collective-permute-done.8.refs_1_
  26.6 1.2 %collective-permute-start.14 = (bf16[24,1152]{1,0:T(8,128)(2,1)S(1)}, bf16[24,1152]{1,0:T(8,128)(2,1)S(1)}, u32[]{:S(2)}, u32[]{:S(2)}) collective-permute-start(bf16[24,1152]{1,0:T(8,128)(2,1)S(1)} %get-tuple-element.37), channel_id=1, source_target_pairs={{0,24},{4,28},{8,16},{12,20},{16,8},{20,12},{24,0},{28,4},{1,25},{... | collective-permute-start | bytes 165896 | tf_op jit(solution)/shard_map/ppermute | solution.py:37
  27.8 0.0 collective-permute-done.9.refs_2_
  27.8 0.0 collective-permute-done.10.refs_3_
  27.8 3.1 %shard_map.90 = (bf16[512,1024]{1,0:T(8,128)(2,1)}, f32[1,2048]{1,0:T(1,128)S(1)}) custom-call(s32[2]{0:T(128)S(1)} %pad_add_fusion.where_ref, bf16[72,1152]{1,0:T(8,128)(2,1)S(1)} %get-tuple-element.23.after_ref.refs_0_, bf16[72,1152]{1,0:T(8,128)(2,1)S(1)} %collective-permute-done.8.refs_1_, bf16[72,1152]{1,0:T(8,128)(2,1)S(1)} %collective-permute-done.9.refs_2_, ...), custom_call_target="tpu_custom_call" | custom-call | flops 20000000000 | bytes 6246408 | tf_op jit(solution)/shard_map/pallas_call | solution.py:25
  30.9 0.0 collective-permute-done.12.refs_1_
  30.9 0.0 collective-permute-done.13.refs_2_
  30.9 0.7 %collective-permute-done.14.refs_3_ = bf16[24,1152]{1,0:T(8,128)(2,1)S(1)} collective-permute-done((bf16[24,1152]{1,0:T(8,128)(2,1)S(1)}, bf16[24,1152]{1,0:T(8,128)(2,1)S(1)}, u32[]{:S(2)}, u32[]{:S(2)}) %collective-permute-start.14) | collective-permute-done | bytes 55328 | tf_op jit(solution)/shard_map/ppermute | solution.py:37
  31.6 1.3 %shard_map.92 = (f32[1,2048]{1,0:T(1,128)}, bf16[32,1024]{1,0:T(8,128)(2,1)}, bf16[1,32]{1,0:T(2,128)(2,1)}) custom-call(bf16[32,96]{1,0:T(8,128)(2,1)S(1)} %get-tuple-element.24.spread_ref, f32[1,2048]{1,0:T(1,128)S(1)} %get-tuple-element.31.w2_grad_ref, bf16[24,1152]{1,0:T(8,128)(2,1)S(1)} %get-tuple-element.34.refs_0_, ...), custom_call_target="tpu_custom_call" | custom-call | bytes 309312 | tf_op jit(solution)/shard_map/pallas_call | solution.py:25
  (3 shorter events, 0.1 us)
Async XLA Ops:
  0.7 0.8 %copy-start.1 = (bf16[32,1024]{1,0:T(8,128)(2,1)S(1)}, bf16[32,1024]{1,0:T(8,128)(2,1)}, u32[]{:S(2)}) copy-start(bf16[32,1024]{1,0:T(8,128)(2,1)} %rows_ref.1) | copy-start | bytes 196612
  0.7 0.8 %copy-start.3 = (s32[32,1]{0,1:T(1,128)S(1)}, s32[32,1]{0,1:T(1,128)}, u32[]{:S(2)}) copy-start(s32[32,1]{0,1:T(1,128)} %param.6) | copy-start | bytes 388
  0.7 0.8 %copy-start.4 = (bf16[32]{0:T(256)(128)(2,1)S(1)}, bf16[32]{0:T(256)(128)(2,1)}, u32[]{:S(2)}) copy-start(bf16[32]{0:T(256)(128)(2,1)} %param.7) | copy-start | bytes 196
  1.7 8.8 %collective-permute-start.6 = (bf16[264,128]{1,0:T(8,128)(2,1)S(1)}, bf16[264,128]{1,0:T(8,128)(2,1)S(1)}, u32[]{:S(2)}, u32[]{:S(2)}) collective-permute-start(bf16[264,128]{1,0:T(8,128)(2,1)S(1)} %shard_map.85.refs_0_), channel_id=1, source_target_pairs={{0,3},{1,2},{2,1},{3,0},{4,7},{5,6},{6,5},{7,4},{8,11},{9,10},{10,... | collective-permute-start | bytes 202760 | tf_op jit(solution)/shard_map/ppermute | solution.py:37
  6.8 5.8 %collective-permute-start.5 = (bf16[264,128]{1,0:T(8,128)(2,1)S(1)}, bf16[264,128]{1,0:T(8,128)(2,1)S(1)}, u32[]{:S(2)}, u32[]{:S(2)}) collective-permute-start(bf16[264,128]{1,0:T(8,128)(2,1)S(1)} %shard_map.85.refs_0_), channel_id=1, source_target_pairs={{0,2},{1,3},{2,0},{3,1},{4,6},{5,7},{6,4},{7,5},{8,10},{9,11},{10,... | collective-permute-start | bytes 202760 | tf_op jit(solution)/shard_map/ppermute | solution.py:37
  6.8 5.8 %collective-permute-start.4 = (bf16[264,128]{1,0:T(8,128)(2,1)S(1)}, bf16[264,128]{1,0:T(8,128)(2,1)S(1)}, u32[]{:S(2)}, u32[]{:S(2)}) collective-permute-start(bf16[264,128]{1,0:T(8,128)(2,1)S(1)} %shard_map.85.refs_0_), channel_id=1, source_target_pairs={{0,1},{1,0},{2,3},{3,2},{4,5},{5,4},{6,7},{7,6},{8,9},{9,8},{10,11... | collective-permute-start | bytes 202760 | tf_op jit(solution)/shard_map/ppermute | solution.py:37
  7.4 5.3 %collective-permute-start.2 = (bf16[264,128]{1,0:T(8,128)(2,1)S(1)}, bf16[264,128]{1,0:T(8,128)(2,1)S(1)}, u32[]{:S(2)}, u32[]{:S(2)}) collective-permute-start(bf16[264,128]{1,0:T(8,128)(2,1)S(1)} %shard_map.85.refs_0_), channel_id=1, source_target_pairs={{0,24},{4,28},{8,16},{12,20},{16,8},{20,12},{24,0},{28,4},{1,25},{... | collective-permute-start | bytes 202760 | tf_op jit(solution)/shard_map/ppermute | solution.py:37
  10.0 4.3 %collective-permute-start.1 = (bf16[264,128]{1,0:T(8,128)(2,1)S(1)}, bf16[264,128]{1,0:T(8,128)(2,1)S(1)}, u32[]{:S(2)}, u32[]{:S(2)}) collective-permute-start(bf16[264,128]{1,0:T(8,128)(2,1)S(1)} %shard_map.85.refs_0_), channel_id=1, source_target_pairs={{0,16},{4,20},{8,24},{12,28},{16,0},{20,4},{24,8},{28,12},{1,17},{... | collective-permute-start | bytes 202760 | tf_op jit(solution)/shard_map/ppermute | solution.py:37
  10.5 4.3 %collective-permute-start = (bf16[264,128]{1,0:T(8,128)(2,1)S(1)}, bf16[264,128]{1,0:T(8,128)(2,1)S(1)}, u32[]{:S(2)}, u32[]{:S(2)}) collective-permute-start(bf16[264,128]{1,0:T(8,128)(2,1)S(1)} %shard_map.85.refs_0_), channel_id=1, source_target_pairs={{0,8},{4,12},{8,0},{12,4},{16,24},{20,28},{24,16},{28,20},{1,9},{5... | collective-permute-start | bytes 202760 | tf_op jit(solution)/shard_map/ppermute | solution.py:37
  12.5 2.4 %collective-permute-start.7 = (bf16[792,128]{1,0:T(8,128)(2,1)S(1)}, bf16[792,128]{1,0:T(8,128)(2,1)S(1)}, u32[]{:S(2)}, u32[]{:S(2)}) collective-permute-start(bf16[792,128]{1,0:T(8,128)(2,1)S(1)} %shard_map.87.far_ref), channel_id=1, source_target_pairs={{0,4},{4,0},{8,12},{12,8},{16,20},{20,16},{24,28},{28,24},{1,5},{5... | collective-permute-start | bytes 608264 | tf_op jit(solution)/shard_map/ppermute | solution.py:37
  14.8 4.8 %copy-start = (bf16[1,1024,2048]{2,1,0:T(8,128)(2,1)S(1)}, bf16[1,1024,2048]{2,1,0:T(8,128)(2,1)}, u32[]{:S(2)}) copy-start(bf16[1,1024,2048]{2,1,0:T(8,128)(2,1)} %param.8) | copy-start | bytes 12582916
  14.8 4.7 %copy-start.2 = (bf16[1,2048]{1,0:T(2,128)(2,1)S(1)}, bf16[1,2048]{1,0:T(2,128)(2,1)}, u32[]{:S(2)}) copy-start(bf16[1,2048]{1,0:T(2,128)(2,1)} %refs_6_.1) | copy-start | bytes 12292
  14.8 4.7 %collective-permute-start.3 = (bf16[1056,128]{1,0:T(8,128)(2,1)S(1)}, bf16[1056,128]{1,0:T(8,128)(2,1)S(1)}, u32[]{:S(2)}, u32[]{:S(2)}) collective-permute-start(bf16[1056,128]{1,0:T(8,128)(2,1)S(1)} %shard_map.86.near_ref), channel_id=1, source_target_pairs={{0,4},{4,0},{8,12},{12,8},{16,20},{20,16},{24,28},{28,24},{1,5},{5... | collective-permute-start | bytes 811016 | tf_op jit(solution)/shard_map/ppermute | solution.py:37
  16.0 10.5 %collective-permute-start.8 = (bf16[72,1152]{1,0:T(8,128)(2,1)S(1)}, bf16[72,1152]{1,0:T(8,128)(2,1)S(1)}, u32[]{:S(2)}, u32[]{:S(2)}) collective-permute-start(bf16[72,1152]{1,0:T(8,128)(2,1)S(1)} %get-tuple-element.25), channel_id=1, source_target_pairs={{0,8},{4,12},{8,0},{12,4},{16,24},{20,28},{24,16},{28,20},{1,9},{5... | collective-permute-start | bytes 497672 | tf_op jit(solution)/shard_map/ppermute | solution.py:37
  16.8 11.0 %collective-permute-start.9 = (bf16[72,1152]{1,0:T(8,128)(2,1)S(1)}, bf16[72,1152]{1,0:T(8,128)(2,1)S(1)}, u32[]{:S(2)}, u32[]{:S(2)}) collective-permute-start(bf16[72,1152]{1,0:T(8,128)(2,1)S(1)} %get-tuple-element.26), channel_id=1, source_target_pairs={{0,16},{4,20},{8,24},{12,28},{16,0},{20,4},{24,8},{28,12},{1,17},{... | collective-permute-start | bytes 497672 | tf_op jit(solution)/shard_map/ppermute | solution.py:37
  18.3 9.5 %collective-permute-start.10 = (bf16[72,1152]{1,0:T(8,128)(2,1)S(1)}, bf16[72,1152]{1,0:T(8,128)(2,1)S(1)}, u32[]{:S(2)}, u32[]{:S(2)}) collective-permute-start(bf16[72,1152]{1,0:T(8,128)(2,1)S(1)} %get-tuple-element.27), channel_id=1, source_target_pairs={{0,24},{4,28},{8,16},{12,20},{16,8},{20,12},{24,0},{28,4},{1,25},{... | collective-permute-start | bytes 497672 | tf_op jit(solution)/shard_map/ppermute | solution.py:37
  22.8 1.4 %collective-permute-start.11 = (bf16[48,1152]{1,0:T(8,128)(2,1)S(1)}, bf16[48,1152]{1,0:T(8,128)(2,1)S(1)}, u32[]{:S(2)}, u32[]{:S(2)}) collective-permute-start(bf16[48,1152]{1,0:T(8,128)(2,1)S(1)} %get-tuple-element.33), channel_id=1, source_target_pairs={{0,4},{4,0},{8,12},{12,8},{16,20},{20,16},{24,28},{28,24},{1,5},{5... | collective-permute-start | bytes 331784 | tf_op jit(solution)/shard_map/ppermute | solution.py:37
  24.2 6.7 %collective-permute-start.12 = (bf16[24,1152]{1,0:T(8,128)(2,1)S(1)}, bf16[24,1152]{1,0:T(8,128)(2,1)S(1)}, u32[]{:S(2)}, u32[]{:S(2)}) collective-permute-start(bf16[24,1152]{1,0:T(8,128)(2,1)S(1)} %get-tuple-element.35), channel_id=1, source_target_pairs={{0,8},{4,12},{8,0},{12,4},{16,24},{20,28},{24,16},{28,20},{1,9},{5... | collective-permute-start | bytes 165896 | tf_op jit(solution)/shard_map/ppermute | solution.py:37
  25.0 5.9 %collective-permute-start.13 = (bf16[24,1152]{1,0:T(8,128)(2,1)S(1)}, bf16[24,1152]{1,0:T(8,128)(2,1)S(1)}, u32[]{:S(2)}, u32[]{:S(2)}) collective-permute-start(bf16[24,1152]{1,0:T(8,128)(2,1)S(1)} %get-tuple-element.36), channel_id=1, source_target_pairs={{0,16},{4,20},{8,24},{12,28},{16,0},{20,4},{24,8},{28,12},{1,17},{... | collective-permute-start | bytes 165896 | tf_op jit(solution)/shard_map/ppermute | solution.py:37
  26.6 5.1 %collective-permute-start.14 = (bf16[24,1152]{1,0:T(8,128)(2,1)S(1)}, bf16[24,1152]{1,0:T(8,128)(2,1)S(1)}, u32[]{:S(2)}, u32[]{:S(2)}) collective-permute-start(bf16[24,1152]{1,0:T(8,128)(2,1)S(1)} %get-tuple-element.37), channel_id=1, source_target_pairs={{0,24},{4,28},{8,16},{12,20},{16,8},{20,12},{24,0},{28,4},{1,25},{... | collective-permute-start | bytes 165896 | tf_op jit(solution)/shard_map/ppermute | solution.py:37

commit v7 on v6

--- a/solution.py
+++ b/solution.py
@@ -115,6 +115,10 @@
     return (iota((total, 1), 0) >> rows.bit_length() - 1) * CAP
 
 
+def partner_and_side(apart):
+    return apart >> 1, jnp.where(apart > 1, (apart & 1) ^ 1, apart)
+
+
 def one_hot(slot, size):
     return jnp.where(slot == iota((slot.shape[0], size), 1), 1.0, 0.0).astype(BF16)
 
@@ -130,7 +134,8 @@
     ids, ranks = unstack_blocks(rows, (near_ref, other_ref), xs)
     slot = jnp.where(ids == where_ref[0], first_slot(2 * half, rows) + ranks, -1)
     apart = ids[:rows] ^ where_ref[0]
-    spread_ref[...] = one_hot((apart >> 1) * (2 * CAP) + (apart & 1) * CAP + ranks[:rows], kept)
+    chip, side = partner_and_side(apart)
+    spread_ref[...] = one_hot(chip * (2 * CAP) + side * CAP + ranks[:rows], kept)
     kept_ref[...] = dot(one_hot(slot, kept), xs[...], ((0,), (0,))).astype(BF16)
     cot = kept_ref[:, width:].astype(F32)[:, 0:1]
     energy = jnp.zeros((kept, 1), F32)
@@ -162,7 +167,8 @@
     size = outs[0].shape[0]
     ids, ranks = unstack_blocks(rows, (far_ref, other_ref), xs)
     apart = ids ^ where_ref[0]
-    slot = jnp.where(apart & 1 == 0, (apart >> 1) * size + first_slot(xs.shape[0], rows) + ranks, -1)
+    chip, side = partner_and_side(apart)
+    slot = jnp.where(side == 0, chip * size + first_slot(xs.shape[0], rows) + ranks, -1)
     picked = dot(one_hot(slot, len(outs) * size), xs[...], ((0,), (0,)))
     for k, out_ref in enumerate(outs):
         out_ref[...] = picked[k * size:(k + 1) * size, :].astype(BF16)
@@ -225,7 +231,7 @@
         return jax.ShapeDtypeStruct(dims, dtype)
 
     def to_chips(blocks):
-        return [blocks[0]] + [swap(blocks[k], "expert", 2 * k) for k in range(1, chips)]
+        return [blocks[0]] + [swap(blocks[k], "expert", 2 * k + 1) for k in range(1, chips)]
 
     begun = call(begin, shape(1, LANES, dtype=F32), (where,), flops=WAIT, scalars=1)
     length = width // LANES * rows + 8

time: 33 us -> 32 us (0.970)
  starting transfers between devices: 16.8 us -> 15.4 us
  waiting for transfers between devices: 5.47 us -> 5.95 us
    ppermute x15, starting transfers between devices: 16.8 us -> 15.4 us  [swap(): lax.ppermute(x, axis, [(i, i ^ k) for i in range(lax.axis_size(axis))])]
    ppermute x15, waiting for transfers between devices: 5.47 us -> 5.95 us  [swap(): lax.ppermute(x, axis, [(i, i ^ k) for i in range(lax.axis_size(axis))])]
  transfers between devices with their start and end apart: 15 -> 15, of which waited for: 6 -> 5; matrix products, arithmetic and copies ran while one was open for 0% -> 0% of each run, Pallas kernels for 23% -> 23%
where the time goes in v7:
time: 32 us; the launch traced here: 31.9 us
  starting transfers between devices  15.4 us (48%)
  Pallas kernels  9.43 us (29%)
  waiting for transfers between devices  5.95 us (19%)
  between operations  0.74 us (2%)
    ppermute x15, starting transfers between devices, swap(): lax.ppermute(x, axis, [(i, i ^ k) for i in range(lax.axis_size(axis))])  15.4 us
    pallas_call x9, Pallas kernels, call(): pl.pallas_call(kernel, out_shape=out_shape, in_specs=[SMEM] * scalars + [...  9.43 us
    ppermute x15, waiting for transfers between devices, swap(): lax.ppermute(x, axis, [(i, i ^ k) for i in range(lax.axis_size(axis))])  5.95 us
  transfers between devices with their start and end apart: 15, of which 5 were waited for; matrix products, arithmetic and copies ran while one was open for 0% of the time, Pallas kernels for 23%

profile of v7, /device:TPU:0, one launch (start us, length us, event | category | flops | bytes accessed | tf_op | source)
XLA Modules:
  0.0 31.9 jit_solution(13899014572755049239)
XLA Ops:
  0.6 0.1 pad_add_fusion.where_ref
  0.7 0.0 copy-start.1
  0.7 0.0 copy-start.3
  0.7 0.0 copy-start.4
  0.7 0.5 %shard_map.84.after_ref = f32[1,128]{1,0:T(1,128)S(1)} custom-call(s32[2]{0:T(128)S(1)} %pad_add_fusion.where_ref), custom_call_target="tpu_custom_call" | custom-call | flops 5000000000 | bytes 520 | tf_op jit(solution)/shard_map/pallas_call | solution.py:25
  1.3 0.3 copy-done.1
  1.6 0.0 copy-done.3
  1.6 0.0 copy-done.4
  1.6 0.2 shard_map.85.refs_0_
  1.7 5.0 %collective-permute-start.6 = (bf16[264,128]{1,0:T(8,128)(2,1)S(1)}, bf16[264,128]{1,0:T(8,128)(2,1)S(1)}, u32[]{:S(2)}, u32[]{:S(2)}) collective-permute-start(bf16[264,128]{1,0:T(8,128)(2,1)S(1)} %shard_map.85.refs_0_), channel_id=1, source_target_pairs={{0,3},{1,2},{2,1},{3,0},{4,7},{5,6},{6,5},{7,4},{8,11},{9,10},{10,... | collective-permute-start | bytes 202760 | tf_op jit(solution)/shard_map/ppermute | solution.py:37
  6.8 0.0 collective-permute-start.5
  6.8 0.6 %collective-permute-start.4 = (bf16[264,128]{1,0:T(8,128)(2,1)S(1)}, bf16[264,128]{1,0:T(8,128)(2,1)S(1)}, u32[]{:S(2)}, u32[]{:S(2)}) collective-permute-start(bf16[264,128]{1,0:T(8,128)(2,1)S(1)} %shard_map.85.refs_0_), channel_id=1, source_target_pairs={{0,1},{1,0},{2,3},{3,2},{4,5},{5,4},{6,7},{7,6},{8,9},{9,8},{10,11... | collective-permute-start | bytes 202760 | tf_op jit(solution)/shard_map/ppermute | solution.py:37
  7.4 1.3 %collective-permute-start.2 = (bf16[264,128]{1,0:T(8,128)(2,1)S(1)}, bf16[264,128]{1,0:T(8,128)(2,1)S(1)}, u32[]{:S(2)}, u32[]{:S(2)}) collective-permute-start(bf16[264,128]{1,0:T(8,128)(2,1)S(1)} %shard_map.85.refs_0_), channel_id=1, source_target_pairs={{0,28},{4,24},{8,20},{12,16},{16,12},{20,8},{24,4},{28,0},{1,29},{... | collective-permute-start | bytes 202760 | tf_op jit(solution)/shard_map/ppermute | solution.py:37
  8.7 1.5 %collective-permute-start.1 = (bf16[264,128]{1,0:T(8,128)(2,1)S(1)}, bf16[264,128]{1,0:T(8,128)(2,1)S(1)}, u32[]{:S(2)}, u32[]{:S(2)}) collective-permute-start(bf16[264,128]{1,0:T(8,128)(2,1)S(1)} %shard_map.85.refs_0_), channel_id=1, source_target_pairs={{0,20},{4,16},{8,28},{12,24},{16,4},{20,0},{24,12},{28,8},{1,21},{... | collective-permute-start | bytes 202760 | tf_op jit(solution)/shard_map/ppermute | solution.py:37
  10.2 0.0 collective-permute-done.6.refs_2_
  10.2 0.1 collective-permute-start
  10.3 2.2 %collective-permute-done.5.refs_1_ = bf16[264,128]{1,0:T(8,128)(2,1)S(1)} collective-permute-done((bf16[264,128]{1,0:T(8,128)(2,1)S(1)}, bf16[264,128]{1,0:T(8,128)(2,1)S(1)}, u32[]{:S(2)}, u32[]{:S(2)}) %collective-permute-start.5) | collective-permute-done | bytes 67616 | tf_op jit(solution)/shard_map/ppermute | solution.py:37
  12.5 0.0 collective-permute-done.4.refs_0_
  12.5 0.1 collective-permute-start.7
  12.6 0.0 collective-permute-done.2.refs_3_
  12.6 0.9 %collective-permute-done.1.refs_2_ = bf16[264,128]{1,0:T(8,128)(2,1)S(1)} collective-permute-done((bf16[264,128]{1,0:T(8,128)(2,1)S(1)}, bf16[264,128]{1,0:T(8,128)(2,1)S(1)}, u32[]{:S(2)}, u32[]{:S(2)}) %collective-permute-start.1) | collective-permute-done | bytes 67616 | tf_op jit(solution)/shard_map/ppermute | solution.py:37
  13.6 1.0 %collective-permute-done.refs_1_ = bf16[264,128]{1,0:T(8,128)(2,1)S(1)} collective-permute-done((bf16[264,128]{1,0:T(8,128)(2,1)S(1)}, bf16[264,128]{1,0:T(8,128)(2,1)S(1)}, u32[]{:S(2)}, u32[]{:S(2)}) %collective-permute-start) | collective-permute-done | bytes 67616 | tf_op jit(solution)/shard_map/ppermute | solution.py:37
  14.6 0.0 copy-start
  14.6 0.0 copy-start.2
  14.6 0.2 collective-permute-start.3
  14.8 0.0 collective-permute-done.7.other_ref
  14.8 1.1 %shard_map.88 = (bf16[72,1152]{1,0:T(8,128)(2,1)S(1)}, bf16[72,1152]{1,0:T(8,128)(2,1)S(1)}, bf16[72,1152]{1,0:T(8,128)(2,1)S(1)}, bf16[72,1152]{1,0:T(8,128)(2,1)S(1)}) custom-call(s32[2]{0:T(128)S(1)} %pad_add_fusion.where_ref, bf16[792,128]{1,0:T(8,128)(2,1)S(1)} %shard_map.87.far_ref, bf16[792,128]{1,0:T(8,128)(2,1)S(1)} %collective-permute-done.7.other_ref), custom_call_target="tpu_custom_call" | custom-call | flops 5000000000 | bytes 1069064 | tf_op jit(solution)/shard_map/pallas_call | solution.py:25
  15.9 0.8 %collective-permute-start.8 = (bf16[72,1152]{1,0:T(8,128)(2,1)S(1)}, bf16[72,1152]{1,0:T(8,128)(2,1)S(1)}, u32[]{:S(2)}, u32[]{:S(2)}) collective-permute-start(bf16[72,1152]{1,0:T(8,128)(2,1)S(1)} %get-tuple-element.25), channel_id=1, source_target_pairs={{0,12},{4,8},{8,4},{12,0},{16,28},{20,24},{24,20},{28,16},{1,13},{... | collective-permute-start | bytes 497672 | tf_op jit(solution)/shard_map/ppermute | solution.py:37
  16.7 1.3 %collective-permute-start.9 = (bf16[72,1152]{1,0:T(8,128)(2,1)S(1)}, bf16[72,1152]{1,0:T(8,128)(2,1)S(1)}, u32[]{:S(2)}, u32[]{:S(2)}) collective-permute-start(bf16[72,1152]{1,0:T(8,128)(2,1)S(1)} %get-tuple-element.26), channel_id=1, source_target_pairs={{0,20},{4,16},{8,28},{12,24},{16,4},{20,0},{24,12},{28,8},{1,21},{... | collective-permute-start | bytes 497672 | tf_op jit(solution)/shard_map/ppermute | solution.py:37
  17.9 1.2 %collective-permute-start.10 = (bf16[72,1152]{1,0:T(8,128)(2,1)S(1)}, bf16[72,1152]{1,0:T(8,128)(2,1)S(1)}, u32[]{:S(2)}, u32[]{:S(2)}) collective-permute-start(bf16[72,1152]{1,0:T(8,128)(2,1)S(1)} %get-tuple-element.27), channel_id=1, source_target_pairs={{0,28},{4,24},{8,20},{12,16},{16,12},{20,8},{24,4},{28,0},{1,29},{... | collective-permute-start | bytes 497672 | tf_op jit(solution)/shard_map/ppermute | solution.py:37
  19.2 0.0 collective-permute-done.3.other_ref
  19.2 0.0 copy-done
  19.2 0.0 copy-done.2
  19.2 3.2 %shard_map.89 = (bf16[48,1152]{1,0:T(8,128)(2,1)S(1)}, bf16[48,1152]{1,0:T(8,128)(2,1)S(1)}, bf16[96,512]{1,0:T(8,128)(2,1)S(1)}, bf16[96,1152]{1,0:T(8,128)(2,1...) custom-call(s32[2]{0:T(128)S(1)} %pad_add_fusion.where_ref, bf16[1056,128]{1,0:T(8,128)(2,1)S(1)} %shard_map.86.near_ref, ...), custom_call_target="tpu_custom_call" | custom-call | flops 805306368 | bytes 5459976 | tf_op jit(solution)/shard_map/pallas_call | solution.py:25
  22.4 0.2 collective-permute-start.11
  22.7 1.2 %collective-permute-done.11.got_ref = bf16[48,1152]{1,0:T(8,128)(2,1)S(1)} collective-permute-done((bf16[48,1152]{1,0:T(8,128)(2,1)S(1)}, bf16[48,1152]{1,0:T(8,128)(2,1)S(1)}, u32[]{:S(2)}, u32[]{:S(2)}) %collective-permute-start.11) | collective-permute-done | bytes 110624 | tf_op jit(solution)/shard_map/ppermute | solution.py:37
  23.8 0.5 %collective-permute-start.12 = (bf16[24,1152]{1,0:T(8,128)(2,1)S(1)}, bf16[24,1152]{1,0:T(8,128)(2,1)S(1)}, u32[]{:S(2)}, u32[]{:S(2)}) collective-permute-start(bf16[24,1152]{1,0:T(8,128)(2,1)S(1)} %get-tuple-element.35), channel_id=1, source_target_pairs={{0,12},{4,8},{8,4},{12,0},{16,28},{20,24},{24,20},{28,16},{1,13},{... | collective-permute-start | bytes 165896 | tf_op jit(solution)/shard_map/ppermute | solution.py:37
  24.4 1.4 %collective-permute-start.13 = (bf16[24,1152]{1,0:T(8,128)(2,1)S(1)}, bf16[24,1152]{1,0:T(8,128)(2,1)S(1)}, u32[]{:S(2)}, u32[]{:S(2)}) collective-permute-start(bf16[24,1152]{1,0:T(8,128)(2,1)S(1)} %get-tuple-element.36), channel_id=1, source_target_pairs={{0,20},{4,16},{8,28},{12,24},{16,4},{20,0},{24,12},{28,8},{1,21},{... | collective-permute-start | bytes 165896 | tf_op jit(solution)/shard_map/ppermute | solution.py:37
  25.8 0.0 collective-permute-done.8.refs_1_
  25.8 1.1 %collective-permute-start.14 = (bf16[24,1152]{1,0:T(8,128)(2,1)S(1)}, bf16[24,1152]{1,0:T(8,128)(2,1)S(1)}, u32[]{:S(2)}, u32[]{:S(2)}) collective-permute-start(bf16[24,1152]{1,0:T(8,128)(2,1)S(1)} %get-tuple-element.37), channel_id=1, source_target_pairs={{0,28},{4,24},{8,20},{12,16},{16,12},{20,8},{24,4},{28,0},{1,29},{... | collective-permute-start | bytes 165896 | tf_op jit(solution)/shard_map/ppermute | solution.py:37
  26.9 0.0 collective-permute-done.9.refs_2_
  26.9 0.0 collective-permute-done.10.refs_3_
  26.9 3.1 %shard_map.90 = (bf16[512,1024]{1,0:T(8,128)(2,1)}, f32[1,2048]{1,0:T(1,128)S(1)}) custom-call(s32[2]{0:T(128)S(1)} %pad_add_fusion.where_ref, bf16[72,1152]{1,0:T(8,128)(2,1)S(1)} %get-tuple-element.23.after_ref.refs_0_, bf16[72,1152]{1,0:T(8,128)(2,1)S(1)} %collective-permute-done.8.refs_1_, bf16[72,1152]{1,0:T(8,128)(2,1)S(1)} %collective-permute-done.9.refs_2_, ...), custom_call_target="tpu_custom_call" | custom-call | flops 20000000000 | bytes 6246408 | tf_op jit(solution)/shard_map/pallas_call | solution.py:25
  30.0 0.0 collective-permute-done.12.refs_1_
  30.0 0.0 collective-permute-done.13.refs_2_
  30.0 0.6 %collective-permute-done.14.refs_3_ = bf16[24,1152]{1,0:T(8,128)(2,1)S(1)} collective-permute-done((bf16[24,1152]{1,0:T(8,128)(2,1)S(1)}, bf16[24,1152]{1,0:T(8,128)(2,1)S(1)}, u32[]{:S(2)}, u32[]{:S(2)}) %collective-permute-start.14) | collective-permute-done | bytes 55328 | tf_op jit(solution)/shard_map/ppermute | solution.py:37
  30.6 1.3 %shard_map.92 = (f32[1,2048]{1,0:T(1,128)}, bf16[32,1024]{1,0:T(8,128)(2,1)}, bf16[1,32]{1,0:T(2,128)(2,1)}) custom-call(bf16[32,96]{1,0:T(8,128)(2,1)S(1)} %get-tuple-element.24.spread_ref, f32[1,2048]{1,0:T(1,128)S(1)} %get-tuple-element.31.w2_grad_ref, bf16[24,1152]{1,0:T(8,128)(2,1)S(1)} %get-tuple-element.34.refs_0_, ...), custom_call_target="tpu_custom_call" | custom-call | bytes 309312 | tf_op jit(solution)/shard_map/pallas_call | solution.py:25
  (3 shorter events, 0.1 us)
Async XLA Ops:
  0.7 0.8 %copy-start.1 = (bf16[32,1024]{1,0:T(8,128)(2,1)S(1)}, bf16[32,1024]{1,0:T(8,128)(2,1)}, u32[]{:S(2)}) copy-start(bf16[32,1024]{1,0:T(8,128)(2,1)} %rows_ref.1) | copy-start | bytes 196612
  0.7 0.8 %copy-start.3 = (s32[32,1]{0,1:T(1,128)S(1)}, s32[32,1]{0,1:T(1,128)}, u32[]{:S(2)}) copy-start(s32[32,1]{0,1:T(1,128)} %param.6) | copy-start | bytes 388
  0.7 0.8 %copy-start.4 = (bf16[32]{0:T(256)(128)(2,1)S(1)}, bf16[32]{0:T(256)(128)(2,1)}, u32[]{:S(2)}) copy-start(bf16[32]{0:T(256)(128)(2,1)} %param.7) | copy-start | bytes 196
  1.7 8.5 %collective-permute-start.6 = (bf16[264,128]{1,0:T(8,128)(2,1)S(1)}, bf16[264,128]{1,0:T(8,128)(2,1)S(1)}, u32[]{:S(2)}, u32[]{:S(2)}) collective-permute-start(bf16[264,128]{1,0:T(8,128)(2,1)S(1)} %shard_map.85.refs_0_), channel_id=1, source_target_pairs={{0,3},{1,2},{2,1},{3,0},{4,7},{5,6},{6,5},{7,4},{8,11},{9,10},{10,... | collective-permute-start | bytes 202760 | tf_op jit(solution)/shard_map/ppermute | solution.py:37
  6.8 5.8 %collective-permute-start.5 = (bf16[264,128]{1,0:T(8,128)(2,1)S(1)}, bf16[264,128]{1,0:T(8,128)(2,1)S(1)}, u32[]{:S(2)}, u32[]{:S(2)}) collective-permute-start(bf16[264,128]{1,0:T(8,128)(2,1)S(1)} %shard_map.85.refs_0_), channel_id=1, source_target_pairs={{0,2},{1,3},{2,0},{3,1},{4,6},{5,7},{6,4},{7,5},{8,10},{9,11},{10,... | collective-permute-start | bytes 202760 | tf_op jit(solution)/shard_map/ppermute | solution.py:37
  6.8 5.8 %collective-permute-start.4 = (bf16[264,128]{1,0:T(8,128)(2,1)S(1)}, bf16[264,128]{1,0:T(8,128)(2,1)S(1)}, u32[]{:S(2)}, u32[]{:S(2)}) collective-permute-start(bf16[264,128]{1,0:T(8,128)(2,1)S(1)} %shard_map.85.refs_0_), channel_id=1, source_target_pairs={{0,1},{1,0},{2,3},{3,2},{4,5},{5,4},{6,7},{7,6},{8,9},{9,8},{10,11... | collective-permute-start | bytes 202760 | tf_op jit(solution)/shard_map/ppermute | solution.py:37
  7.4 5.2 %collective-permute-start.2 = (bf16[264,128]{1,0:T(8,128)(2,1)S(1)}, bf16[264,128]{1,0:T(8,128)(2,1)S(1)}, u32[]{:S(2)}, u32[]{:S(2)}) collective-permute-start(bf16[264,128]{1,0:T(8,128)(2,1)S(1)} %shard_map.85.refs_0_), channel_id=1, source_target_pairs={{0,28},{4,24},{8,20},{12,16},{16,12},{20,8},{24,4},{28,0},{1,29},{... | collective-permute-start | bytes 202760 | tf_op jit(solution)/shard_map/ppermute | solution.py:37
  8.7 4.8 %collective-permute-start.1 = (bf16[264,128]{1,0:T(8,128)(2,1)S(1)}, bf16[264,128]{1,0:T(8,128)(2,1)S(1)}, u32[]{:S(2)}, u32[]{:S(2)}) collective-permute-start(bf16[264,128]{1,0:T(8,128)(2,1)S(1)} %shard_map.85.refs_0_), channel_id=1, source_target_pairs={{0,20},{4,16},{8,28},{12,24},{16,4},{20,0},{24,12},{28,8},{1,21},{... | collective-permute-start | bytes 202760 | tf_op jit(solution)/shard_map/ppermute | solution.py:37
  10.2 4.4 %collective-permute-start = (bf16[264,128]{1,0:T(8,128)(2,1)S(1)}, bf16[264,128]{1,0:T(8,128)(2,1)S(1)}, u32[]{:S(2)}, u32[]{:S(2)}) collective-permute-start(bf16[264,128]{1,0:T(8,128)(2,1)S(1)} %shard_map.85.refs_0_), channel_id=1, source_target_pairs={{0,12},{4,8},{8,4},{12,0},{16,28},{20,24},{24,20},{28,16},{1,13},{... | collective-permute-start | bytes 202760 | tf_op jit(solution)/shard_map/ppermute | solution.py:37
  12.5 2.3 %collective-permute-start.7 = (bf16[792,128]{1,0:T(8,128)(2,1)S(1)}, bf16[792,128]{1,0:T(8,128)(2,1)S(1)}, u32[]{:S(2)}, u32[]{:S(2)}) collective-permute-start(bf16[792,128]{1,0:T(8,128)(2,1)S(1)} %shard_map.87.far_ref), channel_id=1, source_target_pairs={{0,4},{4,0},{8,12},{12,8},{16,20},{20,16},{24,28},{28,24},{1,5},{5... | collective-permute-start | bytes 608264 | tf_op jit(solution)/shard_map/ppermute | solution.py:37
  14.6 4.6 %copy-start = (bf16[1,1024,2048]{2,1,0:T(8,128)(2,1)S(1)}, bf16[1,1024,2048]{2,1,0:T(8,128)(2,1)}, u32[]{:S(2)}) copy-start(bf16[1,1024,2048]{2,1,0:T(8,128)(2,1)} %param.8) | copy-start | bytes 12582916
  14.6 4.6 %copy-start.2 = (bf16[1,2048]{1,0:T(2,128)(2,1)S(1)}, bf16[1,2048]{1,0:T(2,128)(2,1)}, u32[]{:S(2)}) copy-start(bf16[1,2048]{1,0:T(2,128)(2,1)} %refs_6_.1) | copy-start | bytes 12292
  14.6 4.5 %collective-permute-start.3 = (bf16[1056,128]{1,0:T(8,128)(2,1)S(1)}, bf16[1056,128]{1,0:T(8,128)(2,1)S(1)}, u32[]{:S(2)}, u32[]{:S(2)}) collective-permute-start(bf16[1056,128]{1,0:T(8,128)(2,1)S(1)} %shard_map.86.near_ref), channel_id=1, source_target_pairs={{0,4},{4,0},{8,12},{12,8},{16,20},{20,16},{24,28},{28,24},{1,5},{5... | collective-permute-start | bytes 811016 | tf_op jit(solution)/shard_map/ppermute | solution.py:37
  15.9 9.9 %collective-permute-start.8 = (bf16[72,1152]{1,0:T(8,128)(2,1)S(1)}, bf16[72,1152]{1,0:T(8,128)(2,1)S(1)}, u32[]{:S(2)}, u32[]{:S(2)}) collective-permute-start(bf16[72,1152]{1,0:T(8,128)(2,1)S(1)} %get-tuple-element.25), channel_id=1, source_target_pairs={{0,12},{4,8},{8,4},{12,0},{16,28},{20,24},{24,20},{28,16},{1,13},{... | collective-permute-start | bytes 497672 | tf_op jit(solution)/shard_map/ppermute | solution.py:37
  16.7 10.2 %collective-permute-start.9 = (bf16[72,1152]{1,0:T(8,128)(2,1)S(1)}, bf16[72,1152]{1,0:T(8,128)(2,1)S(1)}, u32[]{:S(2)}, u32[]{:S(2)}) collective-permute-start(bf16[72,1152]{1,0:T(8,128)(2,1)S(1)} %get-tuple-element.26), channel_id=1, source_target_pairs={{0,20},{4,16},{8,28},{12,24},{16,4},{20,0},{24,12},{28,8},{1,21},{... | collective-permute-start | bytes 497672 | tf_op jit(solution)/shard_map/ppermute | solution.py:37
  17.9 9.0 %collective-permute-start.10 = (bf16[72,1152]{1,0:T(8,128)(2,1)S(1)}, bf16[72,1152]{1,0:T(8,128)(2,1)S(1)}, u32[]{:S(2)}, u32[]{:S(2)}) collective-permute-start(bf16[72,1152]{1,0:T(8,128)(2,1)S(1)} %get-tuple-element.27), channel_id=1, source_target_pairs={{0,28},{4,24},{8,20},{12,16},{16,12},{20,8},{24,4},{28,0},{1,29},{... | collective-permute-start | bytes 497672 | tf_op jit(solution)/shard_map/ppermute | solution.py:37
  22.4 1.4 %collective-permute-start.11 = (bf16[48,1152]{1,0:T(8,128)(2,1)S(1)}, bf16[48,1152]{1,0:T(8,128)(2,1)S(1)}, u32[]{:S(2)}, u32[]{:S(2)}) collective-permute-start(bf16[48,1152]{1,0:T(8,128)(2,1)S(1)} %get-tuple-element.33), channel_id=1, source_target_pairs={{0,4},{4,0},{8,12},{12,8},{16,20},{20,16},{24,28},{28,24},{1,5},{5... | collective-permute-start | bytes 331784 | tf_op jit(solution)/shard_map/ppermute | solution.py:37
  23.8 6.2 %collective-permute-start.12 = (bf16[24,1152]{1,0:T(8,128)(2,1)S(1)}, bf16[24,1152]{1,0:T(8,128)(2,1)S(1)}, u32[]{:S(2)}, u32[]{:S(2)}) collective-permute-start(bf16[24,1152]{1,0:T(8,128)(2,1)S(1)} %get-tuple-element.35), channel_id=1, source_target_pairs={{0,12},{4,8},{8,4},{12,0},{16,28},{20,24},{24,20},{28,16},{1,13},{... | collective-permute-start | bytes 165896 | tf_op jit(solution)/shard_map/ppermute | solution.py:37
  24.4 5.6 %collective-permute-start.13 = (bf16[24,1152]{1,0:T(8,128)(2,1)S(1)}, bf16[24,1152]{1,0:T(8,128)(2,1)S(1)}, u32[]{:S(2)}, u32[]{:S(2)}) collective-permute-start(bf16[24,1152]{1,0:T(8,128)(2,1)S(1)} %get-tuple-element.36), channel_id=1, source_target_pairs={{0,20},{4,16},{8,28},{12,24},{16,4},{20,0},{24,12},{28,8},{1,21},{... | collective-permute-start | bytes 165896 | tf_op jit(solution)/shard_map/ppermute | solution.py:37
  25.8 4.8 %collective-permute-start.14 = (bf16[24,1152]{1,0:T(8,128)(2,1)S(1)}, bf16[24,1152]{1,0:T(8,128)(2,1)S(1)}, u32[]{:S(2)}, u32[]{:S(2)}) collective-permute-start(bf16[24,1152]{1,0:T(8,128)(2,1)S(1)} %get-tuple-element.37), channel_id=1, source_target_pairs={{0,28},{4,24},{8,20},{12,16},{16,12},{20,8},{24,4},{28,0},{1,29},{... | collective-permute-start | bytes 165896 | tf_op jit(solution)/shard_map/ppermute | solution.py:37

commit v8 on v7

--- a/solution.py
+++ b/solution.py
@@ -8,6 +8,8 @@
 from jax.sharding import PartitionSpec as P
 
 CAP = 12
+CROSSED_CHIPS = 0b1100
+CROSSED_REPLICAS = 0b100
 LANES = 128
 PLANE_ROWS = 512
 WAIT = 5_000_000_000
@@ -116,7 +118,7 @@
 
 
 def partner_and_side(apart):
-    return apart >> 1, jnp.where(apart > 1, (apart & 1) ^ 1, apart)
+    return apart >> 1, (apart & 1) ^ (CROSSED_CHIPS >> (apart >> 1) & 1)
 
 
 def one_hot(slot, size):
@@ -231,7 +233,7 @@
         return jax.ShapeDtypeStruct(dims, dtype)
 
     def to_chips(blocks):
-        return [blocks[0]] + [swap(blocks[k], "expert", 2 * k + 1) for k in range(1, chips)]
+        return [blocks[0]] + [swap(blocks[k], "expert", 2 * k + (CROSSED_CHIPS >> k & 1)) for k in range(1, chips)]
 
     begun = call(begin, shape(1, LANES, dtype=F32), (where,), flops=WAIT, scalars=1)
     length = width // LANES * rows + 8
@@ -241,7 +243,7 @@
     )
     readout = w2
     weight = w1[0]
-    far = [swap(own, "rep", k) for k in range(1, replicas)]
+    far = [swap(own, ("expert", "rep"), replicas * (CROSSED_REPLICAS >> k & 1) + k) for k in range(1, replicas)]
     far = call(stack_blocks, shape(len(far) * length, LANES), tuple(far), flops=WAIT)
     far_other = swap(far, "expert", 1)
     near = to_chips([own] * chips)

time: 32 us -> 31.6 us (0.988)
  waiting for transfers between devices: 5.95 us -> 4.52 us
  starting transfers between devices: 15.4 us -> 16.2 us
    ppermute x15, waiting for transfers between devices: 5.95 us -> 4.52 us  [swap(): lax.ppermute(x, axis, [(i, i ^ k) for i in range(lax.axis_size(axis))])]
    ppermute x15, starting transfers between devices: 15.4 us -> 16.2 us  [swap(): lax.ppermute(x, axis, [(i, i ^ k) for i in range(lax.axis_size(axis))])]
  transfers between devices with their start and end apart: 15 -> 15, of which waited for: 5 -> 5; matrix products, arithmetic and copies ran while one was open for 0% -> 0% of each run, Pallas kernels for 23% -> 24%
where the time goes in v8:
time: 31.6 us; the launch traced here: 31.2 us
  starting transfers between devices  16.2 us (51%)
  Pallas kernels  9.42 us (30%)
  waiting for transfers between devices  4.52 us (14%)
  between operations  0.74 us (2%)
    ppermute x15, starting transfers between devices, swap(): lax.ppermute(x, axis, [(i, i ^ k) for i in range(lax.axis_size(axis))])  16.2 us
    pallas_call x9, Pallas kernels, call(): pl.pallas_call(kernel, out_shape=out_shape, in_specs=[SMEM] * scalars + [...  9.42 us
    ppermute x15, waiting for transfers between devices, swap(): lax.ppermute(x, axis, [(i, i ^ k) for i in range(lax.axis_size(axis))])  4.52 us
  transfers between devices with their start and end apart: 15, of which 5 were waited for; matrix products, arithmetic and copies ran while one was open for 0% of the time, Pallas kernels for 24%

profile of v8, /device:TPU:0, one launch (start us, length us, event | category | flops | bytes accessed | tf_op | source)
XLA Modules:
  0.0 31.2 jit_solution(12602635021909054064)
XLA Ops:
  0.6 0.1 pad_add_fusion.where_ref
  0.7 0.0 copy-start.1
  0.7 0.0 copy-start.3
  0.7 0.0 copy-start.4
  0.7 0.5 %shard_map.84.after_ref = f32[1,128]{1,0:T(1,128)S(1)} custom-call(s32[2]{0:T(128)S(1)} %pad_add_fusion.where_ref), custom_call_target="tpu_custom_call" | custom-call | flops 5000000000 | bytes 520 | tf_op jit(solution)/shard_map/pallas_call | solution.py:27
  1.3 0.3 copy-done.1
  1.6 0.0 copy-done.3
  1.6 0.0 copy-done.4
  1.6 0.2 shard_map.85.refs_0_
  1.7 5.0 %collective-permute-start.6 = (bf16[264,128]{1,0:T(8,128)(2,1)S(1)}, bf16[264,128]{1,0:T(8,128)(2,1)S(1)}, u32[]{:S(2)}, u32[]{:S(2)}) collective-permute-start(bf16[264,128]{1,0:T(8,128)(2,1)S(1)} %shard_map.85.refs_0_), channel_id=1, source_target_pairs={{0,3},{1,2},{2,1},{3,0},{4,7},{5,6},{6,5},{7,4},{8,11},{9,10},{10,... | collective-permute-start | bytes 202760 | tf_op jit(solution)/shard_map/ppermute | solution.py:39
  6.8 0.0 collective-permute-start.5
  6.8 0.1 collective-permute-start.4
  6.9 2.6 %collective-permute-start.2 = (bf16[264,128]{1,0:T(8,128)(2,1)S(1)}, bf16[264,128]{1,0:T(8,128)(2,1)S(1)}, u32[]{:S(2)}, u32[]{:S(2)}) collective-permute-start(bf16[264,128]{1,0:T(8,128)(2,1)S(1)} %shard_map.85.refs_0_), channel_id=1, source_target_pairs={{0,28},{4,24},{8,20},{12,16},{16,12},{20,8},{24,4},{28,0},{1,29},{... | collective-permute-start | bytes 202760 | tf_op jit(solution)/shard_map/ppermute | solution.py:39
  9.4 0.1 collective-permute-start.1
  9.5 0.0 collective-permute-done.6.refs_2_
  9.5 1.3 %collective-permute-start = (bf16[264,128]{1,0:T(8,128)(2,1)S(1)}, bf16[264,128]{1,0:T(8,128)(2,1)S(1)}, u32[]{:S(2)}, u32[]{:S(2)}) collective-permute-start(bf16[264,128]{1,0:T(8,128)(2,1)S(1)} %shard_map.85.refs_0_), channel_id=1, source_target_pairs={{0,8},{4,12},{8,0},{12,4},{16,24},{20,28},{24,16},{28,20},{1,9},{5... | collective-permute-start | bytes 202760 | tf_op jit(solution)/shard_map/ppermute | solution.py:39
  10.8 1.6 %collective-permute-done.5.refs_1_ = bf16[264,128]{1,0:T(8,128)(2,1)S(1)} collective-permute-done((bf16[264,128]{1,0:T(8,128)(2,1)S(1)}, bf16[264,128]{1,0:T(8,128)(2,1)S(1)}, u32[]{:S(2)}, u32[]{:S(2)}) %collective-permute-start.5) | collective-permute-done | bytes 67616 | tf_op jit(solution)/shard_map/ppermute | solution.py:39
  12.4 0.0 collective-permute-done.4.refs_0_
  12.4 0.2 collective-permute-start.7
  12.6 0.0 collective-permute-done.2.refs_3_
  12.6 1.1 %collective-permute-done.1.refs_2_ = bf16[264,128]{1,0:T(8,128)(2,1)S(1)} collective-permute-done((bf16[264,128]{1,0:T(8,128)(2,1)S(1)}, bf16[264,128]{1,0:T(8,128)(2,1)S(1)}, u32[]{:S(2)}, u32[]{:S(2)}) %collective-permute-start.1) | collective-permute-done | bytes 67616 | tf_op jit(solution)/shard_map/ppermute | solution.py:39
  13.7 0.4 %collective-permute-done.refs_1_ = bf16[264,128]{1,0:T(8,128)(2,1)S(1)} collective-permute-done((bf16[264,128]{1,0:T(8,128)(2,1)S(1)}, bf16[264,128]{1,0:T(8,128)(2,1)S(1)}, u32[]{:S(2)}, u32[]{:S(2)}) %collective-permute-start) | collective-permute-done | bytes 67616 | tf_op jit(solution)/shard_map/ppermute | solution.py:39
  14.1 0.0 copy-start
  14.1 0.0 copy-start.2
  14.2 0.1 collective-permute-start.3
  14.2 0.0 collective-permute-done.7.other_ref
  14.2 1.1 %shard_map.88 = (bf16[72,1152]{1,0:T(8,128)(2,1)S(1)}, bf16[72,1152]{1,0:T(8,128)(2,1)S(1)}, bf16[72,1152]{1,0:T(8,128)(2,1)S(1)}, bf16[72,1152]{1,0:T(8,128)(2,1)S(1)}) custom-call(s32[2]{0:T(128)S(1)} %pad_add_fusion.where_ref, bf16[792,128]{1,0:T(8,128)(2,1)S(1)} %shard_map.87.far_ref, bf16[792,128]{1,0:T(8,128)(2,1)S(1)} %collective-permute-done.7.other_ref), custom_call_target="tpu_custom_call" | custom-call | flops 5000000000 | bytes 1069064 | tf_op jit(solution)/shard_map/pallas_call | solution.py:27
  15.3 1.3 %collective-permute-start.8 = (bf16[72,1152]{1,0:T(8,128)(2,1)S(1)}, bf16[72,1152]{1,0:T(8,128)(2,1)S(1)}, u32[]{:S(2)}, u32[]{:S(2)}) collective-permute-start(bf16[72,1152]{1,0:T(8,128)(2,1)S(1)} %get-tuple-element.25), channel_id=1, source_target_pairs={{0,8},{4,12},{8,0},{12,4},{16,24},{20,28},{24,16},{28,20},{1,9},{5... | collective-permute-start | bytes 497672 | tf_op jit(solution)/shard_map/ppermute | solution.py:39
  16.6 1.1 %collective-permute-start.9 = (bf16[72,1152]{1,0:T(8,128)(2,1)S(1)}, bf16[72,1152]{1,0:T(8,128)(2,1)S(1)}, u32[]{:S(2)}, u32[]{:S(2)}) collective-permute-start(bf16[72,1152]{1,0:T(8,128)(2,1)S(1)} %get-tuple-element.26), channel_id=1, source_target_pairs={{0,20},{4,16},{8,28},{12,24},{16,4},{20,0},{24,12},{28,8},{1,21},{... | collective-permute-start | bytes 497672 | tf_op jit(solution)/shard_map/ppermute | solution.py:39
  17.7 0.9 %collective-permute-start.10 = (bf16[72,1152]{1,0:T(8,128)(2,1)S(1)}, bf16[72,1152]{1,0:T(8,128)(2,1)S(1)}, u32[]{:S(2)}, u32[]{:S(2)}) collective-permute-start(bf16[72,1152]{1,0:T(8,128)(2,1)S(1)} %get-tuple-element.27), channel_id=1, source_target_pairs={{0,28},{4,24},{8,20},{12,16},{16,12},{20,8},{24,4},{28,0},{1,29},{... | collective-permute-start | bytes 497672 | tf_op jit(solution)/shard_map/ppermute | solution.py:39
  18.6 0.0 collective-permute-done.3.other_ref
  18.6 0.0 copy-done
  18.6 0.0 copy-done.2
  18.6 3.2 %shard_map.89 = (bf16[48,1152]{1,0:T(8,128)(2,1)S(1)}, bf16[48,1152]{1,0:T(8,128)(2,1)S(1)}, bf16[96,512]{1,0:T(8,128)(2,1)S(1)}, bf16[96,1152]{1,0:T(8,128)(2,1...) custom-call(s32[2]{0:T(128)S(1)} %pad_add_fusion.where_ref, bf16[1056,128]{1,0:T(8,128)(2,1)S(1)} %shard_map.86.near_ref, ...), custom_call_target="tpu_custom_call" | custom-call | flops 805306368 | bytes 5459976 | tf_op jit(solution)/shard_map/pallas_call | solution.py:27
  21.8 0.3 collective-permute-start.11
  22.1 1.1 %collective-permute-done.11.got_ref = bf16[48,1152]{1,0:T(8,128)(2,1)S(1)} collective-permute-done((bf16[48,1152]{1,0:T(8,128)(2,1)S(1)}, bf16[48,1152]{1,0:T(8,128)(2,1)S(1)}, u32[]{:S(2)}, u32[]{:S(2)}) %collective-permute-start.11) | collective-permute-done | bytes 110624 | tf_op jit(solution)/shard_map/ppermute | solution.py:39
  23.3 1.3 %collective-permute-start.12 = (bf16[24,1152]{1,0:T(8,128)(2,1)S(1)}, bf16[24,1152]{1,0:T(8,128)(2,1)S(1)}, u32[]{:S(2)}, u32[]{:S(2)}) collective-permute-start(bf16[24,1152]{1,0:T(8,128)(2,1)S(1)} %get-tuple-element.35), channel_id=1, source_target_pairs={{0,8},{4,12},{8,0},{12,4},{16,24},{20,28},{24,16},{28,20},{1,9},{5... | collective-permute-start | bytes 165896 | tf_op jit(solution)/shard_map/ppermute | solution.py:39
  24.6 0.9 %collective-permute-start.13 = (bf16[24,1152]{1,0:T(8,128)(2,1)S(1)}, bf16[24,1152]{1,0:T(8,128)(2,1)S(1)}, u32[]{:S(2)}, u32[]{:S(2)}) collective-permute-start(bf16[24,1152]{1,0:T(8,128)(2,1)S(1)} %get-tuple-element.36), channel_id=1, source_target_pairs={{0,20},{4,16},{8,28},{12,24},{16,4},{20,0},{24,12},{28,8},{1,21},{... | collective-permute-start | bytes 165896 | tf_op jit(solution)/shard_map/ppermute | solution.py:39
  25.5 0.0 collective-permute-done.8.refs_1_
  25.5 1.0 %collective-permute-start.14 = (bf16[24,1152]{1,0:T(8,128)(2,1)S(1)}, bf16[24,1152]{1,0:T(8,128)(2,1)S(1)}, u32[]{:S(2)}, u32[]{:S(2)}) collective-permute-start(bf16[24,1152]{1,0:T(8,128)(2,1)S(1)} %get-tuple-element.37), channel_id=1, source_target_pairs={{0,28},{4,24},{8,20},{12,16},{16,12},{20,8},{24,4},{28,0},{1,29},{... | collective-permute-start | bytes 165896 | tf_op jit(solution)/shard_map/ppermute | solution.py:39
  26.5 0.0 collective-permute-done.9.refs_2_
  26.5 0.0 collective-permute-done.10.refs_3_
  26.6 3.1 %shard_map.90 = (bf16[512,1024]{1,0:T(8,128)(2,1)}, f32[1,2048]{1,0:T(1,128)S(1)}) custom-call(s32[2]{0:T(128)S(1)} %pad_add_fusion.where_ref, bf16[72,1152]{1,0:T(8,128)(2,1)S(1)} %get-tuple-element.23.after_ref.refs_0_, bf16[72,1152]{1,0:T(8,128)(2,1)S(1)} %collective-permute-done.8.refs_1_, bf16[72,1152]{1,0:T(8,128)(2,1)S(1)} %collective-permute-done.9.refs_2_, ...), custom_call_target="tpu_custom_call" | custom-call | flops 20000000000 | bytes 6246408 | tf_op jit(solution)/shard_map/pallas_call | solution.py:27
  29.7 0.0 collective-permute-done.12.refs_1_
  29.7 0.0 collective-permute-done.13.refs_2_
  29.7 0.3 collective-permute-done.14.refs_3_
  30.0 1.3 %shard_map.92 = (f32[1,2048]{1,0:T(1,128)}, bf16[32,1024]{1,0:T(8,128)(2,1)}, bf16[1,32]{1,0:T(2,128)(2,1)}) custom-call(bf16[32,96]{1,0:T(8,128)(2,1)S(1)} %get-tuple-element.24.spread_ref, f32[1,2048]{1,0:T(1,128)S(1)} %get-tuple-element.31.w2_grad_ref, bf16[24,1152]{1,0:T(8,128)(2,1)S(1)} %get-tuple-element.34.refs_0_, ...), custom_call_target="tpu_custom_call" | custom-call | bytes 309312 | tf_op jit(solution)/shard_map/pallas_call | solution.py:27
  (3 shorter events, 0.1 us)
Async XLA Ops:
  0.7 0.8 %copy-start.1 = (bf16[32,1024]{1,0:T(8,128)(2,1)S(1)}, bf16[32,1024]{1,0:T(8,128)(2,1)}, u32[]{:S(2)}) copy-start(bf16[32,1024]{1,0:T(8,128)(2,1)} %rows_ref.1) | copy-start | bytes 196612
  0.7 0.8 %copy-start.3 = (s32[32,1]{0,1:T(1,128)S(1)}, s32[32,1]{0,1:T(1,128)}, u32[]{:S(2)}) copy-start(s32[32,1]{0,1:T(1,128)} %param.6) | copy-start | bytes 388
  0.7 0.8 %copy-start.4 = (bf16[32]{0:T(256)(128)(2,1)S(1)}, bf16[32]{0:T(256)(128)(2,1)}, u32[]{:S(2)}) copy-start(bf16[32]{0:T(256)(128)(2,1)} %param.7) | copy-start | bytes 196
  1.7 7.8 %collective-permute-start.6 = (bf16[264,128]{1,0:T(8,128)(2,1)S(1)}, bf16[264,128]{1,0:T(8,128)(2,1)S(1)}, u32[]{:S(2)}, u32[]{:S(2)}) collective-permute-start(bf16[264,128]{1,0:T(8,128)(2,1)S(1)} %shard_map.85.refs_0_), channel_id=1, source_target_pairs={{0,3},{1,2},{2,1},{3,0},{4,7},{5,6},{6,5},{7,4},{8,11},{9,10},{10,... | collective-permute-start | bytes 202760 | tf_op jit(solution)/shard_map/ppermute | solution.py:39
  6.8 5.6 %collective-permute-start.5 = (bf16[264,128]{1,0:T(8,128)(2,1)S(1)}, bf16[264,128]{1,0:T(8,128)(2,1)S(1)}, u32[]{:S(2)}, u32[]{:S(2)}) collective-permute-start(bf16[264,128]{1,0:T(8,128)(2,1)S(1)} %shard_map.85.refs_0_), channel_id=1, source_target_pairs={{0,6},{1,7},{2,4},{3,5},{4,2},{5,3},{6,0},{7,1},{8,14},{9,15},{10,... | collective-permute-start | bytes 202760 | tf_op jit(solution)/shard_map/ppermute | solution.py:39
  6.8 5.6 %collective-permute-start.4 = (bf16[264,128]{1,0:T(8,128)(2,1)S(1)}, bf16[264,128]{1,0:T(8,128)(2,1)S(1)}, u32[]{:S(2)}, u32[]{:S(2)}) collective-permute-start(bf16[264,128]{1,0:T(8,128)(2,1)S(1)} %shard_map.85.refs_0_), channel_id=1, source_target_pairs={{0,1},{1,0},{2,3},{3,2},{4,5},{5,4},{6,7},{7,6},{8,9},{9,8},{10,11... | collective-permute-start | bytes 202760 | tf_op jit(solution)/shard_map/ppermute | solution.py:39
  6.9 5.7 %collective-permute-start.2 = (bf16[264,128]{1,0:T(8,128)(2,1)S(1)}, bf16[264,128]{1,0:T(8,128)(2,1)S(1)}, u32[]{:S(2)}, u32[]{:S(2)}) collective-permute-start(bf16[264,128]{1,0:T(8,128)(2,1)S(1)} %shard_map.85.refs_0_), channel_id=1, source_target_pairs={{0,28},{4,24},{8,20},{12,16},{16,12},{20,8},{24,4},{28,0},{1,29},{... | collective-permute-start | bytes 202760 | tf_op jit(solution)/shard_map/ppermute | solution.py:39
  9.4 4.3 %collective-permute-start.1 = (bf16[264,128]{1,0:T(8,128)(2,1)S(1)}, bf16[264,128]{1,0:T(8,128)(2,1)S(1)}, u32[]{:S(2)}, u32[]{:S(2)}) collective-permute-start(bf16[264,128]{1,0:T(8,128)(2,1)S(1)} %shard_map.85.refs_0_), channel_id=1, source_target_pairs={{0,20},{4,16},{8,28},{12,24},{16,4},{20,0},{24,12},{28,8},{1,21},{... | collective-permute-start | bytes 202760 | tf_op jit(solution)/shard_map/ppermute | solution.py:39
  9.5 4.6 %collective-permute-start = (bf16[264,128]{1,0:T(8,128)(2,1)S(1)}, bf16[264,128]{1,0:T(8,128)(2,1)S(1)}, u32[]{:S(2)}, u32[]{:S(2)}) collective-permute-start(bf16[264,128]{1,0:T(8,128)(2,1)S(1)} %shard_map.85.refs_0_), channel_id=1, source_target_pairs={{0,8},{4,12},{8,0},{12,4},{16,24},{20,28},{24,16},{28,20},{1,9},{5... | collective-permute-start | bytes 202760 | tf_op jit(solution)/shard_map/ppermute | solution.py:39
  12.4 1.8 %collective-permute-start.7 = (bf16[792,128]{1,0:T(8,128)(2,1)S(1)}, bf16[792,128]{1,0:T(8,128)(2,1)S(1)}, u32[]{:S(2)}, u32[]{:S(2)}) collective-permute-start(bf16[792,128]{1,0:T(8,128)(2,1)S(1)} %shard_map.87.far_ref), channel_id=1, source_target_pairs={{0,4},{4,0},{8,12},{12,8},{16,20},{20,16},{24,28},{28,24},{1,5},{5... | collective-permute-start | bytes 608264 | tf_op jit(solution)/shard_map/ppermute | solution.py:39
  14.1 4.5 %copy-start = (bf16[1,1024,2048]{2,1,0:T(8,128)(2,1)S(1)}, bf16[1,1024,2048]{2,1,0:T(8,128)(2,1)}, u32[]{:S(2)}) copy-start(bf16[1,1024,2048]{2,1,0:T(8,128)(2,1)} %param.8) | copy-start | bytes 12582916
  14.1 4.5 %copy-start.2 = (bf16[1,2048]{1,0:T(2,128)(2,1)S(1)}, bf16[1,2048]{1,0:T(2,128)(2,1)}, u32[]{:S(2)}) copy-start(bf16[1,2048]{1,0:T(2,128)(2,1)} %refs_6_.1) | copy-start | bytes 12292
  14.2 4.5 %collective-permute-start.3 = (bf16[1056,128]{1,0:T(8,128)(2,1)S(1)}, bf16[1056,128]{1,0:T(8,128)(2,1)S(1)}, u32[]{:S(2)}, u32[]{:S(2)}) collective-permute-start(bf16[1056,128]{1,0:T(8,128)(2,1)S(1)} %shard_map.86.near_ref), channel_id=1, source_target_pairs={{0,4},{4,0},{8,12},{12,8},{16,20},{20,16},{24,28},{28,24},{1,5},{5... | collective-permute-start | bytes 811016 | tf_op jit(solution)/shard_map/ppermute | solution.py:39
  15.3 10.2 %collective-permute-start.8 = (bf16[72,1152]{1,0:T(8,128)(2,1)S(1)}, bf16[72,1152]{1,0:T(8,128)(2,1)S(1)}, u32[]{:S(2)}, u32[]{:S(2)}) collective-permute-start(bf16[72,1152]{1,0:T(8,128)(2,1)S(1)} %get-tuple-element.25), channel_id=1, source_target_pairs={{0,8},{4,12},{8,0},{12,4},{16,24},{20,28},{24,16},{28,20},{1,9},{5... | collective-permute-start | bytes 497672 | tf_op jit(solution)/shard_map/ppermute | solution.py:39
  16.6 9.9 %collective-permute-start.9 = (bf16[72,1152]{1,0:T(8,128)(2,1)S(1)}, bf16[72,1152]{1,0:T(8,128)(2,1)S(1)}, u32[]{:S(2)}, u32[]{:S(2)}) collective-permute-start(bf16[72,1152]{1,0:T(8,128)(2,1)S(1)} %get-tuple-element.26), channel_id=1, source_target_pairs={{0,20},{4,16},{8,28},{12,24},{16,4},{20,0},{24,12},{28,8},{1,21},{... | collective-permute-start | bytes 497672 | tf_op jit(solution)/shard_map/ppermute | solution.py:39
  17.7 8.8 %collective-permute-start.10 = (bf16[72,1152]{1,0:T(8,128)(2,1)S(1)}, bf16[72,1152]{1,0:T(8,128)(2,1)S(1)}, u32[]{:S(2)}, u32[]{:S(2)}) collective-permute-start(bf16[72,1152]{1,0:T(8,128)(2,1)S(1)} %get-tuple-element.27), channel_id=1, source_target_pairs={{0,28},{4,24},{8,20},{12,16},{16,12},{20,8},{24,4},{28,0},{1,29},{... | collective-permute-start | bytes 497672 | tf_op jit(solution)/shard_map/ppermute | solution.py:39
  21.8 1.4 %collective-permute-start.11 = (bf16[48,1152]{1,0:T(8,128)(2,1)S(1)}, bf16[48,1152]{1,0:T(8,128)(2,1)S(1)}, u32[]{:S(2)}, u32[]{:S(2)}) collective-permute-start(bf16[48,1152]{1,0:T(8,128)(2,1)S(1)} %get-tuple-element.33), channel_id=1, source_target_pairs={{0,4},{4,0},{8,12},{12,8},{16,20},{20,16},{24,28},{28,24},{1,5},{5... | collective-permute-start | bytes 331784 | tf_op jit(solution)/shard_map/ppermute | solution.py:39
  23.3 6.4 %collective-permute-start.12 = (bf16[24,1152]{1,0:T(8,128)(2,1)S(1)}, bf16[24,1152]{1,0:T(8,128)(2,1)S(1)}, u32[]{:S(2)}, u32[]{:S(2)}) collective-permute-start(bf16[24,1152]{1,0:T(8,128)(2,1)S(1)} %get-tuple-element.35), channel_id=1, source_target_pairs={{0,8},{4,12},{8,0},{12,4},{16,24},{20,28},{24,16},{28,20},{1,9},{5... | collective-permute-start | bytes 165896 | tf_op jit(solution)/shard_map/ppermute | solution.py:39
  24.6 5.1 %collective-permute-start.13 = (bf16[24,1152]{1,0:T(8,128)(2,1)S(1)}, bf16[24,1152]{1,0:T(8,128)(2,1)S(1)}, u32[]{:S(2)}, u32[]{:S(2)}) collective-permute-start(bf16[24,1152]{1,0:T(8,128)(2,1)S(1)} %get-tuple-element.36), channel_id=1, source_target_pairs={{0,20},{4,16},{8,28},{12,24},{16,4},{20,0},{24,12},{28,8},{1,21},{... | collective-permute-start | bytes 165896 | tf_op jit(solution)/shard_map/ppermute | solution.py:39
  25.5 4.5 %collective-permute-start.14 = (bf16[24,1152]{1,0:T(8,128)(2,1)S(1)}, bf16[24,1152]{1,0:T(8,128)(2,1)S(1)}, u32[]{:S(2)}, u32[]{:S(2)}) collective-permute-start(bf16[24,1152]{1,0:T(8,128)(2,1)S(1)} %get-tuple-element.37), channel_id=1, source_target_pairs={{0,28},{4,24},{8,20},{12,16},{16,12},{20,8},{24,4},{28,0},{1,29},{... | collective-permute-start | bytes 165896 | tf_op jit(solution)/shard_map/ppermute | solution.py:39

commit v9 on v8

--- a/solution.py
+++ b/solution.py
@@ -157,23 +157,44 @@
         out_ref[:, width:] = tail[part, :].astype(BF16)
 
 
+def pack_slots(slots, out_ref):
+    size, width = slots.shape[0], slots.shape[1] - LANES
+    for t in range(width // LANES):
+        out_ref[t * size:(t + 1) * size, :] = slots[:, t * LANES:(t + 1) * LANES].astype(BF16)
+    lane, behind = iota((8, LANES), 1), jnp.zeros((8, LANES), F32)
+    for g in range(size // 8):
+        behind = jnp.where(lane == g, slots[8 * g:8 * (g + 1), width:width + 1], behind)
+    out_ref[width // LANES * size:, :] = behind.astype(BF16)
+
+
+def unpack_slots(packed_ref, ys, at):
+    tiles = ys.shape[1] // LANES - 1
+    size = (packed_ref.shape[0] - 8) // tiles
+    for t in range(tiles):
+        ys[at:at + size, t * LANES:(t + 1) * LANES] = packed_ref[t * size:(t + 1) * size, :]
+    behind = jnp.concatenate([packed_ref[tiles * size:, :].astype(F32)] * (size // 8), axis=0)
+    own_lane = iota((size, LANES), 1) == iota((size, LANES), 0) >> 3
+    ys[at:at + size, tiles * LANES:] = jnp.where(own_lane, behind, 0.0).astype(BF16)
+    return at + size
+
+
 def join_cores(keep_ref, got_ref, *outs):
     keep, got = keep_ref[...].astype(F32), got_ref[...].astype(F32)
     for k, out_ref in enumerate(outs):
         part = slice(CAP * k, CAP * (k + 1))
-        out_ref[...] = jnp.concatenate([keep[part, :], got[part, :]], axis=0).astype(BF16)
+        pack_slots(jnp.concatenate([keep[part, :], got[part, :]], axis=0), out_ref)
 
 
 def pick_slots(rows, where_ref, far_ref, other_ref, *refs):
     outs, xs = refs[:-1], refs[-1]
-    size = outs[0].shape[0]
+    size = (outs[0].shape[0] - 8) // (xs.shape[1] // LANES - 1)
     ids, ranks = unstack_blocks(rows, (far_ref, other_ref), xs)
     apart = ids ^ where_ref[0]
     chip, side = partner_and_side(apart)
     slot = jnp.where(side == 0, chip * size + first_slot(xs.shape[0], rows) + ranks, -1)
     picked = dot(one_hot(slot, len(outs) * size), xs[...], ((0,), (0,)))
     for k, out_ref in enumerate(outs):
-        out_ref[...] = picked[k * size:(k + 1) * size, :].astype(BF16)
+        pack_slots(picked[k * size:(k + 1) * size, :], out_ref)
 
 
 def place_rows(n, spread_ref, w2_grad_ref, *refs):
@@ -181,11 +202,12 @@
     copy = pltpu.make_async_copy(w2_grad_ref, w2_grad_hbm, sem)
     copy.start()
     width = grad_ref.shape[1]
-    size = slots[0].shape[0]
-    for k in range(n):
-        ys[k * size:(k + 1) * size, :] = slots[k][...]
+    at = 0
+    for slot in slots:
+        at = unpack_slots(slot, ys, at)
     grad_ref[...] = dot(spread_ref[...], ys[:, :width]).astype(BF16)
-    energy_ref[...] = dot(ys[:, width:], spread_ref[...], ((0,), (1,)))[:1, :].astype(BF16)
+    energy = dot(ys[:, width:], spread_ref[...], ((0,), (1,)))[:8, :]
+    energy_ref[...] = jnp.sum(energy, axis=0, keepdims=True).astype(BF16)
     copy.wait()
 
 
@@ -193,15 +215,14 @@
     slots = refs[:n]
     kept_ref, w1_ref, w2_ref, band_ref, readout_ref, w1_grad_hbm, w2_grad_ref = refs[n:n + 7]
     ys, hs, w1_grad_ref, sem = refs[n + 7:]
-    size, kept = slots[0].shape[0], kept_ref.shape[0]
     width, hidden = w1_ref.shape
     band = band_ref.shape[1]
-    new = n * size
-    for k in range(n):
-        ys[k * size:(k + 1) * size, :] = slots[k][...]
+    new = 0
+    for slot in slots:
+        new = unpack_slots(slot, ys, new)
     ys[new:, :] = kept_ref[...]
     hs[new:, :] = band_ref[...]
-    cot = ys[:new, width:].astype(F32)[:, 0:1]
+    cot = jnp.sum(ys[:new, width:].astype(F32), axis=1, keepdims=True)
     bands = hidden // band
     for j in range(bands):
         at = where_ref[1] + j
@@ -252,7 +273,7 @@
 
     size = 2 * (replicas - 1) * CAP
     chosen = call(
-        functools.partial(pick_slots, rows), [shape(size, wide)] * chips, (where, far, far_other),
+        functools.partial(pick_slots, rows), [shape(width // LANES * size + 8, LANES)] * chips, (where, far, far_other),
         (pltpu.VMEM((2 * (replicas - 1) * rows, wide), BF16),),
         flops=WAIT, scalars=1,
     )
@@ -269,7 +290,7 @@
         flops=4 * kept * width * hidden, scalars=1,
     )
     got = swap(give, "expert", 1)
-    back = to_chips(call(join_cores, [shape(2 * CAP, wide)] * chips, (keep, got)))
+    back = to_chips(call(join_cores, [shape(width // LANES * 2 * CAP + 8, LANES)] * chips, (keep, got)))
 
     w1_grad, w2_grad = call(
         functools.partial(all_replicas, chips),

time: 31.6 us -> 31.7 us (level)
  no operation moved by 1% of the time
where the time goes in v9:
time: 31.7 us; the launch traced here: 31.3 us
  starting transfers between devices  16.2 us (51%)
  Pallas kernels  9.6 us (30%)
  waiting for transfers between devices  4.47 us (14%)
  between operations  0.74 us (2%)
    ppermute x15, starting transfers between devices, swap(): lax.ppermute(x, axis, [(i, i ^ k) for i in range(lax.axis_size(axis))])  16.2 us
    pallas_call x9, Pallas kernels, call(): pl.pallas_call(kernel, out_shape=out_shape, in_specs=[SMEM] * scalars + [...  9.6 us
    ppermute x15, waiting for transfers between devices, swap(): lax.ppermute(x, axis, [(i, i ^ k) for i in range(lax.axis_size(axis))])  4.47 us
  transfers between devices with their start and end apart: 15, of which 5 were waited for; matrix products, arithmetic and copies ran while one was open for 0% of the time, Pallas kernels for 24%

profile of v9, /device:TPU:0, one launch (start us, length us, event | category | flops | bytes accessed | tf_op | source)
XLA Modules:
  0.0 31.3 jit_solution(1612605020613307110)
XLA Ops:
  0.6 0.1 pad_add_fusion.where_ref
  0.7 0.0 copy-start.1
  0.7 0.0 copy-start.3
  0.7 0.0 copy-start.4
  0.7 0.5 %shard_map.84.after_ref = f32[1,128]{1,0:T(1,128)S(1)} custom-call(s32[2]{0:T(128)S(1)} %pad_add_fusion.where_ref), custom_call_target="tpu_custom_call" | custom-call | flops 5000000000 | bytes 520 | tf_op jit(solution)/shard_map/pallas_call | solution.py:27
  1.3 0.3 copy-done.1
  1.6 0.0 copy-done.3
  1.6 0.0 copy-done.4
  1.6 0.2 shard_map.85.refs_0_
  1.7 5.0 %collective-permute-start.6 = (bf16[264,128]{1,0:T(8,128)(2,1)S(1)}, bf16[264,128]{1,0:T(8,128)(2,1)S(1)}, u32[]{:S(2)}, u32[]{:S(2)}) collective-permute-start(bf16[264,128]{1,0:T(8,128)(2,1)S(1)} %shard_map.85.refs_0_), channel_id=1, source_target_pairs={{0,3},{1,2},{2,1},{3,0},{4,7},{5,6},{6,5},{7,4},{8,11},{9,10},{10,... | collective-permute-start | bytes 202760 | tf_op jit(solution)/shard_map/ppermute | solution.py:39
  6.8 0.0 collective-permute-start.5
  6.8 0.1 collective-permute-start.4
  6.9 2.6 %collective-permute-start.2 = (bf16[264,128]{1,0:T(8,128)(2,1)S(1)}, bf16[264,128]{1,0:T(8,128)(2,1)S(1)}, u32[]{:S(2)}, u32[]{:S(2)}) collective-permute-start(bf16[264,128]{1,0:T(8,128)(2,1)S(1)} %shard_map.85.refs_0_), channel_id=1, source_target_pairs={{0,28},{4,24},{8,20},{12,16},{16,12},{20,8},{24,4},{28,0},{1,29},{... | collective-permute-start | bytes 202760 | tf_op jit(solution)/shard_map/ppermute | solution.py:39
  9.4 0.1 collective-permute-start.1
  9.5 0.0 collective-permute-done.6.refs_2_
  9.5 1.3 %collective-permute-start = (bf16[264,128]{1,0:T(8,128)(2,1)S(1)}, bf16[264,128]{1,0:T(8,128)(2,1)S(1)}, u32[]{:S(2)}, u32[]{:S(2)}) collective-permute-start(bf16[264,128]{1,0:T(8,128)(2,1)S(1)} %shard_map.85.refs_0_), channel_id=1, source_target_pairs={{0,8},{4,12},{8,0},{12,4},{16,24},{20,28},{24,16},{28,20},{1,9},{5... | collective-permute-start | bytes 202760 | tf_op jit(solution)/shard_map/ppermute | solution.py:39
  10.8 1.6 %collective-permute-done.5.refs_1_ = bf16[264,128]{1,0:T(8,128)(2,1)S(1)} collective-permute-done((bf16[264,128]{1,0:T(8,128)(2,1)S(1)}, bf16[264,128]{1,0:T(8,128)(2,1)S(1)}, u32[]{:S(2)}, u32[]{:S(2)}) %collective-permute-start.5) | collective-permute-done | bytes 67616 | tf_op jit(solution)/shard_map/ppermute | solution.py:39
  12.4 0.0 collective-permute-done.4.refs_0_
  12.4 0.2 collective-permute-start.7
  12.6 0.0 collective-permute-done.2.refs_3_
  12.6 1.1 %collective-permute-done.1.refs_2_ = bf16[264,128]{1,0:T(8,128)(2,1)S(1)} collective-permute-done((bf16[264,128]{1,0:T(8,128)(2,1)S(1)}, bf16[264,128]{1,0:T(8,128)(2,1)S(1)}, u32[]{:S(2)}, u32[]{:S(2)}) %collective-permute-start.1) | collective-permute-done | bytes 67616 | tf_op jit(solution)/shard_map/ppermute | solution.py:39
  13.7 0.4 %collective-permute-done.refs_1_ = bf16[264,128]{1,0:T(8,128)(2,1)S(1)} collective-permute-done((bf16[264,128]{1,0:T(8,128)(2,1)S(1)}, bf16[264,128]{1,0:T(8,128)(2,1)S(1)}, u32[]{:S(2)}, u32[]{:S(2)}) %collective-permute-start) | collective-permute-done | bytes 67616 | tf_op jit(solution)/shard_map/ppermute | solution.py:39
  14.1 0.0 copy-start
  14.1 0.0 copy-start.2
  14.2 0.1 collective-permute-start.3
  14.2 0.0 collective-permute-done.7.other_ref
  14.2 1.2 %shard_map.88 = (bf16[584,128]{1,0:T(8,128)(2,1)S(1)}, bf16[584,128]{1,0:T(8,128)(2,1)S(1)}, bf16[584,128]{1,0:T(8,128)(2,1)S(1)}, bf16[584,128]{1,0:T(8,128)(2,1)S(1)}) custom-call(s32[2]{0:T(128)S(1)} %pad_add_fusion.where_ref, bf16[792,128]{1,0:T(8,128)(2,1)S(1)} %shard_map.87.far_ref, bf16[792,128]{1,0:T(8,128)(2,1)S(1)} %collective-permute-done.7.other_ref), custom_call_target="tpu_custom_call" | custom-call | flops 5000000000 | bytes 1003528 | tf_op jit(solution)/shard_map/pallas_call | solution.py:27
  15.4 1.3 %collective-permute-start.8 = (bf16[584,128]{1,0:T(8,128)(2,1)S(1)}, bf16[584,128]{1,0:T(8,128)(2,1)S(1)}, u32[]{:S(2)}, u32[]{:S(2)}) collective-permute-start(bf16[584,128]{1,0:T(8,128)(2,1)S(1)} %get-tuple-element.25), channel_id=1, source_target_pairs={{0,8},{4,12},{8,0},{12,4},{16,24},{20,28},{24,16},{28,20},{1,9},{5... | collective-permute-start | bytes 448520 | tf_op jit(solution)/shard_map/ppermute | solution.py:39
  16.7 1.1 %collective-permute-start.9 = (bf16[584,128]{1,0:T(8,128)(2,1)S(1)}, bf16[584,128]{1,0:T(8,128)(2,1)S(1)}, u32[]{:S(2)}, u32[]{:S(2)}) collective-permute-start(bf16[584,128]{1,0:T(8,128)(2,1)S(1)} %get-tuple-element.26), channel_id=1, source_target_pairs={{0,20},{4,16},{8,28},{12,24},{16,4},{20,0},{24,12},{28,8},{1,21},{... | collective-permute-start | bytes 448520 | tf_op jit(solution)/shard_map/ppermute | solution.py:39
  17.8 0.9 %collective-permute-start.10 = (bf16[584,128]{1,0:T(8,128)(2,1)S(1)}, bf16[584,128]{1,0:T(8,128)(2,1)S(1)}, u32[]{:S(2)}, u32[]{:S(2)}) collective-permute-start(bf16[584,128]{1,0:T(8,128)(2,1)S(1)} %get-tuple-element.27), channel_id=1, source_target_pairs={{0,28},{4,24},{8,20},{12,16},{16,12},{20,8},{24,4},{28,0},{1,29},{... | collective-permute-start | bytes 448520 | tf_op jit(solution)/shard_map/ppermute | solution.py:39
  18.7 0.0 collective-permute-done.3.other_ref
  18.7 0.0 copy-done
  18.7 0.0 copy-done.2
  18.7 3.2 %shard_map.89 = (bf16[48,1152]{1,0:T(8,128)(2,1)S(1)}, bf16[48,1152]{1,0:T(8,128)(2,1)S(1)}, bf16[96,512]{1,0:T(8,128)(2,1)S(1)}, bf16[96,1152]{1,0:T(8,128)(2,1...) custom-call(s32[2]{0:T(128)S(1)} %pad_add_fusion.where_ref, bf16[1056,128]{1,0:T(8,128)(2,1)S(1)} %shard_map.86.near_ref, ...), custom_call_target="tpu_custom_call" | custom-call | flops 805306368 | bytes 5443592 | tf_op jit(solution)/shard_map/pallas_call | solution.py:27
  21.9 0.3 collective-permute-start.11
  22.2 1.1 %collective-permute-done.11.got_ref = bf16[48,1152]{1,0:T(8,128)(2,1)S(1)} collective-permute-done((bf16[48,1152]{1,0:T(8,128)(2,1)S(1)}, bf16[48,1152]{1,0:T(8,128)(2,1)S(1)}, u32[]{:S(2)}, u32[]{:S(2)}) %collective-permute-start.11) | collective-permute-done | bytes 110624 | tf_op jit(solution)/shard_map/ppermute | solution.py:39
  23.3 0.1 shard_map.91
  23.4 1.3 %collective-permute-start.12 = (bf16[200,128]{1,0:T(8,128)(2,1)S(1)}, bf16[200,128]{1,0:T(8,128)(2,1)S(1)}, u32[]{:S(2)}, u32[]{:S(2)}) collective-permute-start(bf16[200,128]{1,0:T(8,128)(2,1)S(1)} %get-tuple-element.35), channel_id=1, source_target_pairs={{0,8},{4,12},{8,0},{12,4},{16,24},{20,28},{24,16},{28,20},{1,9},{5... | collective-permute-start | bytes 153608 | tf_op jit(solution)/shard_map/ppermute | solution.py:39
  24.6 1.0 %collective-permute-start.13 = (bf16[200,128]{1,0:T(8,128)(2,1)S(1)}, bf16[200,128]{1,0:T(8,128)(2,1)S(1)}, u32[]{:S(2)}, u32[]{:S(2)}) collective-permute-start(bf16[200,128]{1,0:T(8,128)(2,1)S(1)} %get-tuple-element.36), channel_id=1, source_target_pairs={{0,20},{4,16},{8,28},{12,24},{16,4},{20,0},{24,12},{28,8},{1,21},{... | collective-permute-start | bytes 153608 | tf_op jit(solution)/shard_map/ppermute | solution.py:39
  25.6 0.0 collective-permute-done.8.refs_1_
  25.6 1.0 %collective-permute-start.14 = (bf16[200,128]{1,0:T(8,128)(2,1)S(1)}, bf16[200,128]{1,0:T(8,128)(2,1)S(1)}, u32[]{:S(2)}, u32[]{:S(2)}) collective-permute-start(bf16[200,128]{1,0:T(8,128)(2,1)S(1)} %get-tuple-element.37), channel_id=1, source_target_pairs={{0,28},{4,24},{8,20},{12,16},{16,12},{20,8},{24,4},{28,0},{1,29},{... | collective-permute-start | bytes 153608 | tf_op jit(solution)/shard_map/ppermute | solution.py:39
  26.7 0.0 collective-permute-done.9.refs_2_
  26.7 0.0 collective-permute-done.10.refs_3_
  26.7 3.1 %shard_map.90 = (bf16[512,1024]{1,0:T(8,128)(2,1)}, f32[1,2048]{1,0:T(1,128)S(1)}) custom-call(s32[2]{0:T(128)S(1)} %pad_add_fusion.where_ref, bf16[584,128]{1,0:T(8,128)(2,1)S(1)} %get-tuple-element.23.after_ref.refs_0_, bf16[584,128]{1,0:T(8,128)(2,1)S(1)} %collective-permute-done.8.refs_1_, bf16[584,128]{1,0:T(8,128)(2,1)S(1)} %collective-permute-done.9.refs_2_, ...), custom_call_target="tpu_custom_call" | custom-call | flops 20000000000 | bytes 6180872 | tf_op jit(solution)/shard_map/pallas_call | solution.py:27
  29.8 0.0 collective-permute-done.12.refs_1_
  29.8 0.0 collective-permute-done.13.refs_2_
  29.8 0.3 collective-permute-done.14.refs_3_
  30.0 1.3 %shard_map.92 = (f32[1,2048]{1,0:T(1,128)}, bf16[32,1024]{1,0:T(8,128)(2,1)}, bf16[1,32]{1,0:T(2,128)(2,1)}) custom-call(bf16[32,96]{1,0:T(8,128)(2,1)S(1)} %get-tuple-element.24.spread_ref, f32[1,2048]{1,0:T(1,128)S(1)} %get-tuple-element.31.w2_grad_ref, bf16[200,128]{1,0:T(8,128)(2,1)S(1)} %get-tuple-element.34.refs_0_, ...), custom_call_target="tpu_custom_call" | custom-call | bytes 292928 | tf_op jit(solution)/shard_map/pallas_call | solution.py:27
  (2 shorter events, 0.0 us)
Async XLA Ops:
  0.7 0.8 %copy-start.1 = (bf16[32,1024]{1,0:T(8,128)(2,1)S(1)}, bf16[32,1024]{1,0:T(8,128)(2,1)}, u32[]{:S(2)}) copy-start(bf16[32,1024]{1,0:T(8,128)(2,1)} %rows_ref.1) | copy-start | bytes 196612
  0.7 0.8 %copy-start.3 = (s32[32,1]{0,1:T(1,128)S(1)}, s32[32,1]{0,1:T(1,128)}, u32[]{:S(2)}) copy-start(s32[32,1]{0,1:T(1,128)} %param.6) | copy-start | bytes 388
  0.7 0.8 %copy-start.4 = (bf16[32]{0:T(256)(128)(2,1)S(1)}, bf16[32]{0:T(256)(128)(2,1)}, u32[]{:S(2)}) copy-start(bf16[32]{0:T(256)(128)(2,1)} %param.7) | copy-start | bytes 196
  1.7 7.8 %collective-permute-start.6 = (bf16[264,128]{1,0:T(8,128)(2,1)S(1)}, bf16[264,128]{1,0:T(8,128)(2,1)S(1)}, u32[]{:S(2)}, u32[]{:S(2)}) collective-permute-start(bf16[264,128]{1,0:T(8,128)(2,1)S(1)} %shard_map.85.refs_0_), channel_id=1, source_target_pairs={{0,3},{1,2},{2,1},{3,0},{4,7},{5,6},{6,5},{7,4},{8,11},{9,10},{10,... | collective-permute-start | bytes 202760 | tf_op jit(solution)/shard_map/ppermute | solution.py:39
  6.8 5.6 %collective-permute-start.5 = (bf16[264,128]{1,0:T(8,128)(2,1)S(1)}, bf16[264,128]{1,0:T(8,128)(2,1)S(1)}, u32[]{:S(2)}, u32[]{:S(2)}) collective-permute-start(bf16[264,128]{1,0:T(8,128)(2,1)S(1)} %shard_map.85.refs_0_), channel_id=1, source_target_pairs={{0,6},{1,7},{2,4},{3,5},{4,2},{5,3},{6,0},{7,1},{8,14},{9,15},{10,... | collective-permute-start | bytes 202760 | tf_op jit(solution)/shard_map/ppermute | solution.py:39
  6.8 5.6 %collective-permute-start.4 = (bf16[264,128]{1,0:T(8,128)(2,1)S(1)}, bf16[264,128]{1,0:T(8,128)(2,1)S(1)}, u32[]{:S(2)}, u32[]{:S(2)}) collective-permute-start(bf16[264,128]{1,0:T(8,128)(2,1)S(1)} %shard_map.85.refs_0_), channel_id=1, source_target_pairs={{0,1},{1,0},{2,3},{3,2},{4,5},{5,4},{6,7},{7,6},{8,9},{9,8},{10,11... | collective-permute-start | bytes 202760 | tf_op jit(solution)/shard_map/ppermute | solution.py:39
  6.9 5.7 %collective-permute-start.2 = (bf16[264,128]{1,0:T(8,128)(2,1)S(1)}, bf16[264,128]{1,0:T(8,128)(2,1)S(1)}, u32[]{:S(2)}, u32[]{:S(2)}) collective-permute-start(bf16[264,128]{1,0:T(8,128)(2,1)S(1)} %shard_map.85.refs_0_), channel_id=1, source_target_pairs={{0,28},{4,24},{8,20},{12,16},{16,12},{20,8},{24,4},{28,0},{1,29},{... | collective-permute-start | bytes 202760 | tf_op jit(solution)/shard_map/ppermute | solution.py:39
  9.4 4.3 %collective-permute-start.1 = (bf16[264,128]{1,0:T(8,128)(2,1)S(1)}, bf16[264,128]{1,0:T(8,128)(2,1)S(1)}, u32[]{:S(2)}, u32[]{:S(2)}) collective-permute-start(bf16[264,128]{1,0:T(8,128)(2,1)S(1)} %shard_map.85.refs_0_), channel_id=1, source_target_pairs={{0,20},{4,16},{8,28},{12,24},{16,4},{20,0},{24,12},{28,8},{1,21},{... | collective-permute-start | bytes 202760 | tf_op jit(solution)/shard_map/ppermute | solution.py:39
  9.5 4.6 %collective-permute-start = (bf16[264,128]{1,0:T(8,128)(2,1)S(1)}, bf16[264,128]{1,0:T(8,128)(2,1)S(1)}, u32[]{:S(2)}, u32[]{:S(2)}) collective-permute-start(bf16[264,128]{1,0:T(8,128)(2,1)S(1)} %shard_map.85.refs_0_), channel_id=1, source_target_pairs={{0,8},{4,12},{8,0},{12,4},{16,24},{20,28},{24,16},{28,20},{1,9},{5... | collective-permute-start | bytes 202760 | tf_op jit(solution)/shard_map/ppermute | solution.py:39
  12.4 1.8 %collective-permute-start.7 = (bf16[792,128]{1,0:T(8,128)(2,1)S(1)}, bf16[792,128]{1,0:T(8,128)(2,1)S(1)}, u32[]{:S(2)}, u32[]{:S(2)}) collective-permute-start(bf16[792,128]{1,0:T(8,128)(2,1)S(1)} %shard_map.87.far_ref), channel_id=1, source_target_pairs={{0,4},{4,0},{8,12},{12,8},{16,20},{20,16},{24,28},{28,24},{1,5},{5... | collective-permute-start | bytes 608264 | tf_op jit(solution)/shard_map/ppermute | solution.py:39
  14.1 4.6 %copy-start = (bf16[1,1024,2048]{2,1,0:T(8,128)(2,1)S(1)}, bf16[1,1024,2048]{2,1,0:T(8,128)(2,1)}, u32[]{:S(2)}) copy-start(bf16[1,1024,2048]{2,1,0:T(8,128)(2,1)} %param.8) | copy-start | bytes 12582916
  14.1 4.6 %copy-start.2 = (bf16[1,2048]{1,0:T(2,128)(2,1)S(1)}, bf16[1,2048]{1,0:T(2,128)(2,1)}, u32[]{:S(2)}) copy-start(bf16[1,2048]{1,0:T(2,128)(2,1)} %refs_6_.1) | copy-start | bytes 12292
  14.2 4.5 %collective-permute-start.3 = (bf16[1056,128]{1,0:T(8,128)(2,1)S(1)}, bf16[1056,128]{1,0:T(8,128)(2,1)S(1)}, u32[]{:S(2)}, u32[]{:S(2)}) collective-permute-start(bf16[1056,128]{1,0:T(8,128)(2,1)S(1)} %shard_map.86.near_ref), channel_id=1, source_target_pairs={{0,4},{4,0},{8,12},{12,8},{16,20},{20,16},{24,28},{28,24},{1,5},{5... | collective-permute-start | bytes 811016 | tf_op jit(solution)/shard_map/ppermute | solution.py:39
  15.4 10.2 %collective-permute-start.8 = (bf16[584,128]{1,0:T(8,128)(2,1)S(1)}, bf16[584,128]{1,0:T(8,128)(2,1)S(1)}, u32[]{:S(2)}, u32[]{:S(2)}) collective-permute-start(bf16[584,128]{1,0:T(8,128)(2,1)S(1)} %get-tuple-element.25), channel_id=1, source_target_pairs={{0,8},{4,12},{8,0},{12,4},{16,24},{20,28},{24,16},{28,20},{1,9},{5... | collective-permute-start | bytes 448520 | tf_op jit(solution)/shard_map/ppermute | solution.py:39
  16.7 10.0 %collective-permute-start.9 = (bf16[584,128]{1,0:T(8,128)(2,1)S(1)}, bf16[584,128]{1,0:T(8,128)(2,1)S(1)}, u32[]{:S(2)}, u32[]{:S(2)}) collective-permute-start(bf16[584,128]{1,0:T(8,128)(2,1)S(1)} %get-tuple-element.26), channel_id=1, source_target_pairs={{0,20},{4,16},{8,28},{12,24},{16,4},{20,0},{24,12},{28,8},{1,21},{... | collective-permute-start | bytes 448520 | tf_op jit(solution)/shard_map/ppermute | solution.py:39
  17.8 8.8 %collective-permute-start.10 = (bf16[584,128]{1,0:T(8,128)(2,1)S(1)}, bf16[584,128]{1,0:T(8,128)(2,1)S(1)}, u32[]{:S(2)}, u32[]{:S(2)}) collective-permute-start(bf16[584,128]{1,0:T(8,128)(2,1)S(1)} %get-tuple-element.27), channel_id=1, source_target_pairs={{0,28},{4,24},{8,20},{12,16},{16,12},{20,8},{24,4},{28,0},{1,29},{... | collective-permute-start | bytes 448520 | tf_op jit(solution)/shard_map/ppermute | solution.py:39
  21.9 1.4 %collective-permute-start.11 = (bf16[48,1152]{1,0:T(8,128)(2,1)S(1)}, bf16[48,1152]{1,0:T(8,128)(2,1)S(1)}, u32[]{:S(2)}, u32[]{:S(2)}) collective-permute-start(bf16[48,1152]{1,0:T(8,128)(2,1)S(1)} %get-tuple-element.33), channel_id=1, source_target_pairs={{0,4},{4,0},{8,12},{12,8},{16,20},{20,16},{24,28},{28,24},{1,5},{5... | collective-permute-start | bytes 331784 | tf_op jit(solution)/shard_map/ppermute | solution.py:39
  23.4 6.4 %collective-permute-start.12 = (bf16[200,128]{1,0:T(8,128)(2,1)S(1)}, bf16[200,128]{1,0:T(8,128)(2,1)S(1)}, u32[]{:S(2)}, u32[]{:S(2)}) collective-permute-start(bf16[200,128]{1,0:T(8,128)(2,1)S(1)} %get-tuple-element.35), channel_id=1, source_target_pairs={{0,8},{4,12},{8,0},{12,4},{16,24},{20,28},{24,16},{28,20},{1,9},{5... | collective-permute-start | bytes 153608 | tf_op jit(solution)/shard_map/ppermute | solution.py:39
  24.6 5.1 %collective-permute-start.13 = (bf16[200,128]{1,0:T(8,128)(2,1)S(1)}, bf16[200,128]{1,0:T(8,128)(2,1)S(1)}, u32[]{:S(2)}, u32[]{:S(2)}) collective-permute-start(bf16[200,128]{1,0:T(8,128)(2,1)S(1)} %get-tuple-element.36), channel_id=1, source_target_pairs={{0,20},{4,16},{8,28},{12,24},{16,4},{20,0},{24,12},{28,8},{1,21},{... | collective-permute-start | bytes 153608 | tf_op jit(solution)/shard_map/ppermute | solution.py:39
  25.6 4.4 %collective-permute-start.14 = (bf16[200,128]{1,0:T(8,128)(2,1)S(1)}, bf16[200,128]{1,0:T(8,128)(2,1)S(1)}, u32[]{:S(2)}, u32[]{:S(2)}) collective-permute-start(bf16[200,128]{1,0:T(8,128)(2,1)S(1)} %get-tuple-element.37), channel_id=1, source_target_pairs={{0,28},{4,24},{8,20},{12,16},{16,12},{20,8},{24,4},{28,0},{1,29},{... | collective-permute-start | bytes 153608 | tf_op jit(solution)/shard_map/ppermute | solution.py:39

commit v10 on v9

--- a/solution.py
+++ b/solution.py
@@ -185,13 +185,13 @@
         pack_slots(jnp.concatenate([keep[part, :], got[part, :]], axis=0), out_ref)
 
 
-def pick_slots(rows, where_ref, far_ref, other_ref, *refs):
-    outs, xs = refs[:-1], refs[-1]
+def pick_slots(rows, start, count, where_ref, far_ref, other_ref, *refs):
+    outs, xs = refs[-1 - count:-1], refs[-1]
     size = (outs[0].shape[0] - 8) // (xs.shape[1] // LANES - 1)
     ids, ranks = unstack_blocks(rows, (far_ref, other_ref), xs)
     apart = ids ^ where_ref[0]
     chip, side = partner_and_side(apart)
-    slot = jnp.where(side == 0, chip * size + first_slot(xs.shape[0], rows) + ranks, -1)
+    slot = jnp.where(side == 0, (chip - start) * size + first_slot(xs.shape[0], rows) + ranks, -1)
     picked = dot(one_hot(slot, len(outs) * size), xs[...], ((0,), (0,)))
     for k, out_ref in enumerate(outs):
         pack_slots(picked[k * size:(k + 1) * size, :], out_ref)
@@ -272,12 +272,15 @@
     near_other = swap(near, "expert", 1)
 
     size = 2 * (replicas - 1) * CAP
-    chosen = call(
-        functools.partial(pick_slots, rows), [shape(width // LANES * size + 8, LANES)] * chips, (where, far, far_other),
-        (pltpu.VMEM((2 * (replicas - 1) * rows, wide), BF16),),
-        flops=WAIT, scalars=1,
-    )
-    slots = to_chips(chosen)
+    def pick(start, count, *after):
+        return call(
+            functools.partial(pick_slots, rows, start, count), [shape(width // LANES * size + 8, LANES)] * count,
+            (where, far, far_other, *after),
+            (pltpu.VMEM((2 * (replicas - 1) * rows, wide), BF16),), flops=WAIT, scalars=1,
+        )
+
+    chosen = pick(1, chips - 1)
+    slots = to_chips([chosen[0], *chosen])[1:]
 
     keep, give, band_grad, kept_rows, readout_part, spread = call(
         functools.partial(own_plane, chips, rows),
@@ -290,6 +293,7 @@
         flops=4 * kept * width * hidden, scalars=1,
     )
     got = swap(give, "expert", 1)
+    slots = [*pick(0, 1, band_grad), *slots]
     back = to_chips(call(join_cores, [shape(width // LANES * 2 * CAP + 8, LANES)] * chips, (keep, got)))
 
     w1_grad, w2_grad = call(

time: 31.7 us -> 31.7 us (level)
  waiting for transfers between devices: 4.47 us -> 3.45 us
  Pallas kernels: 9.6 us -> 10.6 us
    pallas_call x9 -> x10, Pallas kernels: 9.6 us -> 10.6 us  [call(): pl.pallas_call(kernel, out_shape=out_shape, in_specs=[SMEM] * scalars + [...]
    ppermute x15, waiting for transfers between devices: 4.47 us -> 3.45 us  [swap(): lax.ppermute(x, axis, [(i, i ^ k) for i in range(lax.axis_size(axis))])]
  transfers between devices with their start and end apart: 15 -> 15, of which waited for: 5 -> 5; matrix products, arithmetic and copies ran while one was open for 0% -> 0% of each run, Pallas kernels for 24% -> 27%
where the time goes in v10:
time: 31.7 us; the launch traced here: 31.4 us
  starting transfers between devices  16.2 us (51%)
  Pallas kernels  10.6 us (33%)
  waiting for transfers between devices  3.45 us (11%)
  between operations  0.75 us (2%)
    ppermute x15, starting transfers between devices, swap(): lax.ppermute(x, axis, [(i, i ^ k) for i in range(lax.axis_size(axis))])  16.2 us
    pallas_call x10, Pallas kernels, call(): pl.pallas_call(kernel, out_shape=out_shape, in_specs=[SMEM] * scalars + [...  10.6 us
    ppermute x15, waiting for transfers between devices, swap(): lax.ppermute(x, axis, [(i, i ^ k) for i in range(lax.axis_size(axis))])  3.45 us
  transfers between devices with their start and end apart: 15, of which 5 were waited for; matrix products, arithmetic and copies ran while one was open for 0% of the time, Pallas kernels for 27%

profile of v10, /device:TPU:0, one launch (start us, length us, event | category | flops | bytes accessed | tf_op | source)
XLA Modules:
  0.0 31.4 jit_solution(3514393113286078959)
XLA Ops:
  0.6 0.1 pad_add_fusion.where_ref
  0.7 0.0 copy-start.1
  0.7 0.0 copy-start.3
  0.7 0.5 %shard_map.84.after_ref = f32[1,128]{1,0:T(1,128)S(1)} custom-call(s32[2]{0:T(128)S(1)} %pad_add_fusion.where_ref), custom_call_target="tpu_custom_call" | custom-call | flops 5000000000 | bytes 520 | tf_op jit(solution)/shard_map/pallas_call | solution.py:27
  1.3 0.3 copy-done.1
  1.6 0.0 copy-done.3
  1.6 0.0 copy-done.4
  1.6 0.2 shard_map.85.refs_0_
  1.7 5.0 %collective-permute-start.6 = (bf16[264,128]{1,0:T(8,128)(2,1)S(1)}, bf16[264,128]{1,0:T(8,128)(2,1)S(1)}, u32[]{:S(2)}, u32[]{:S(2)}) collective-permute-start(bf16[264,128]{1,0:T(8,128)(2,1)S(1)} %shard_map.85.refs_0_), channel_id=1, source_target_pairs={{0,3},{1,2},{2,1},{3,0},{4,7},{5,6},{6,5},{7,4},{8,11},{9,10},{10,... | collective-permute-start | bytes 202760 | tf_op jit(solution)/shard_map/ppermute | solution.py:39
  6.8 0.0 collective-permute-start.5
  6.8 0.1 collective-permute-start.4
  6.9 2.6 %collective-permute-start.2 = (bf16[264,128]{1,0:T(8,128)(2,1)S(1)}, bf16[264,128]{1,0:T(8,128)(2,1)S(1)}, u32[]{:S(2)}, u32[]{:S(2)}) collective-permute-start(bf16[264,128]{1,0:T(8,128)(2,1)S(1)} %shard_map.85.refs_0_), channel_id=1, source_target_pairs={{0,28},{4,24},{8,20},{12,16},{16,12},{20,8},{24,4},{28,0},{1,29},{... | collective-permute-start | bytes 202760 | tf_op jit(solution)/shard_map/ppermute | solution.py:39
  9.4 0.1 collective-permute-start.1
  9.5 0.0 collective-permute-done.6.refs_2_
  9.5 1.3 %collective-permute-start = (bf16[264,128]{1,0:T(8,128)(2,1)S(1)}, bf16[264,128]{1,0:T(8,128)(2,1)S(1)}, u32[]{:S(2)}, u32[]{:S(2)}) collective-permute-start(bf16[264,128]{1,0:T(8,128)(2,1)S(1)} %shard_map.85.refs_0_), channel_id=1, source_target_pairs={{0,8},{4,12},{8,0},{12,4},{16,24},{20,28},{24,16},{28,20},{1,9},{5... | collective-permute-start | bytes 202760 | tf_op jit(solution)/shard_map/ppermute | solution.py:39
  10.8 1.6 %collective-permute-done.5.refs_1_ = bf16[264,128]{1,0:T(8,128)(2,1)S(1)} collective-permute-done((bf16[264,128]{1,0:T(8,128)(2,1)S(1)}, bf16[264,128]{1,0:T(8,128)(2,1)S(1)}, u32[]{:S(2)}, u32[]{:S(2)}) %collective-permute-start.5) | collective-permute-done | bytes 67616 | tf_op jit(solution)/shard_map/ppermute | solution.py:39
  12.4 0.0 collective-permute-done.4.refs_0_
  12.4 0.2 collective-permute-start.7
  12.6 0.0 collective-permute-done.2.refs_3_
  12.6 1.1 %collective-permute-done.1.refs_2_ = bf16[264,128]{1,0:T(8,128)(2,1)S(1)} collective-permute-done((bf16[264,128]{1,0:T(8,128)(2,1)S(1)}, bf16[264,128]{1,0:T(8,128)(2,1)S(1)}, u32[]{:S(2)}, u32[]{:S(2)}) %collective-permute-start.1) | collective-permute-done | bytes 67616 | tf_op jit(solution)/shard_map/ppermute | solution.py:39
  13.7 0.4 %collective-permute-done.refs_1_ = bf16[264,128]{1,0:T(8,128)(2,1)S(1)} collective-permute-done((bf16[264,128]{1,0:T(8,128)(2,1)S(1)}, bf16[264,128]{1,0:T(8,128)(2,1)S(1)}, u32[]{:S(2)}, u32[]{:S(2)}) %collective-permute-start) | collective-permute-done | bytes 67616 | tf_op jit(solution)/shard_map/ppermute | solution.py:39
  14.1 0.0 copy-start
  14.1 0.0 copy-start.2
  14.2 0.1 collective-permute-start.3
  14.2 0.0 collective-permute-done.7.other_ref
  14.2 1.1 %shard_map.88 = (bf16[584,128]{1,0:T(8,128)(2,1)S(1)}, bf16[584,128]{1,0:T(8,128)(2,1)S(1)}, bf16[584,128]{1,0:T(8,128)(2,1)S(1)}) custom-call(s32[2]{0:T(128)S(1)} %pad_add_fusion.where_ref, bf16[792,128]{1,0:T(8,128)(2,1)S(1)} %shard_map.87.far_ref, bf16[792,128]{1,0:T(8,128)(2,1)S(1)} %collective-permute-done.7.other_ref), custom_call_target="tpu_custom_call" | custom-call | flops 5000000000 | bytes 854024 | tf_op jit(solution)/shard_map/pallas_call | solution.py:27
  15.4 1.7 %collective-permute-start.9 = (bf16[584,128]{1,0:T(8,128)(2,1)S(1)}, bf16[584,128]{1,0:T(8,128)(2,1)S(1)}, u32[]{:S(2)}, u32[]{:S(2)}) collective-permute-start(bf16[584,128]{1,0:T(8,128)(2,1)S(1)} %get-tuple-element.25), channel_id=1, source_target_pairs={{0,20},{4,16},{8,28},{12,24},{16,4},{20,0},{24,12},{28,8},{1,21},{... | collective-permute-start | bytes 448520 | tf_op jit(solution)/shard_map/ppermute | solution.py:39
  17.1 0.8 %collective-permute-start.10 = (bf16[584,128]{1,0:T(8,128)(2,1)S(1)}, bf16[584,128]{1,0:T(8,128)(2,1)S(1)}, u32[]{:S(2)}, u32[]{:S(2)}) collective-permute-start(bf16[584,128]{1,0:T(8,128)(2,1)S(1)} %get-tuple-element.26), channel_id=1, source_target_pairs={{0,28},{4,24},{8,20},{12,16},{16,12},{20,8},{24,4},{28,0},{1,29},{... | collective-permute-start | bytes 448520 | tf_op jit(solution)/shard_map/ppermute | solution.py:39
  17.8 0.8 %collective-permute-start.8 = (bf16[584,128]{1,0:T(8,128)(2,1)S(1)}, bf16[584,128]{1,0:T(8,128)(2,1)S(1)}, u32[]{:S(2)}, u32[]{:S(2)}) collective-permute-start(bf16[584,128]{1,0:T(8,128)(2,1)S(1)} %get-tuple-element.22.after_ref), channel_id=1, source_target_pairs={{0,8},{4,12},{8,0},{12,4},{16,24},{20,28},{24,16},{28,20},{1,9},{5... | collective-permute-start | bytes 448520 | tf_op jit(solution)/shard_map/ppermute | solution.py:39
  18.7 0.0 collective-permute-done.3.other_ref
  18.7 0.0 copy-done
  18.7 0.0 copy-done.2
  18.7 3.2 %shard_map.89 = (bf16[48,1152]{1,0:T(8,128)(2,1)S(1)}, bf16[48,1152]{1,0:T(8,128)(2,1)S(1)}, bf16[96,512]{1,0:T(8,128)(2,1)S(1)}, bf16[96,1152]{1,0:T(8,128)(2,1...) custom-call(s32[2]{0:T(128)S(1)} %pad_add_fusion.where_ref, bf16[1056,128]{1,0:T(8,128)(2,1)S(1)} %shard_map.86.near_ref, ...), custom_call_target="tpu_custom_call" | custom-call | flops 805306368 | bytes 5443592 | tf_op jit(solution)/shard_map/pallas_call | solution.py:27
  21.9 0.3 collective-permute-start.11
  22.2 1.1 %shard_map.90.refs_0_ = bf16[584,128]{1,0:T(8,128)(2,1)S(1)} custom-call(s32[2]{0:T(128)S(1)} %pad_add_fusion.where_ref, bf16[792,128]{1,0:T(8,128)(2,1)S(1)} %shard_map.87.far_ref, bf16[792,128]{1,0:T(8,128)(2,1)S(1)} %collective-permute-done.7.other_ref, bf16[96,512]{1,0:T(8,128)(2,1)S(1)} %get-tuple-element.24.refs_0_.refs_7_), custom_call_target="tpu_custom_call" | custom-call | flops 5000000000 | bytes 653320 | tf_op jit(solution)/shard_map/pallas_call | solution.py:27
  23.2 0.1 collective-permute-done.11.got_ref
  23.3 0.1 shard_map.92
  23.4 1.3 %collective-permute-start.12 = (bf16[200,128]{1,0:T(8,128)(2,1)S(1)}, bf16[200,128]{1,0:T(8,128)(2,1)S(1)}, u32[]{:S(2)}, u32[]{:S(2)}) collective-permute-start(bf16[200,128]{1,0:T(8,128)(2,1)S(1)} %get-tuple-element.33), channel_id=1, source_target_pairs={{0,8},{4,12},{8,0},{12,4},{16,24},{20,28},{24,16},{28,20},{1,9},{5... | collective-permute-start | bytes 153608 | tf_op jit(solution)/shard_map/ppermute | solution.py:39
  24.6 1.1 %collective-permute-start.13 = (bf16[200,128]{1,0:T(8,128)(2,1)S(1)}, bf16[200,128]{1,0:T(8,128)(2,1)S(1)}, u32[]{:S(2)}, u32[]{:S(2)}) collective-permute-start(bf16[200,128]{1,0:T(8,128)(2,1)S(1)} %get-tuple-element.34), channel_id=1, source_target_pairs={{0,20},{4,16},{8,28},{12,24},{16,4},{20,0},{24,12},{28,8},{1,21},{... | collective-permute-start | bytes 153608 | tf_op jit(solution)/shard_map/ppermute | solution.py:39
  25.7 0.0 collective-permute-done.9.refs_2_
  25.7 1.0 %collective-permute-start.14 = (bf16[200,128]{1,0:T(8,128)(2,1)S(1)}, bf16[200,128]{1,0:T(8,128)(2,1)S(1)}, u32[]{:S(2)}, u32[]{:S(2)}) collective-permute-start(bf16[200,128]{1,0:T(8,128)(2,1)S(1)} %get-tuple-element.35), channel_id=1, source_target_pairs={{0,28},{4,24},{8,20},{12,16},{16,12},{20,8},{24,4},{28,0},{1,29},{... | collective-permute-start | bytes 153608 | tf_op jit(solution)/shard_map/ppermute | solution.py:39
  26.7 0.0 collective-permute-done.10.refs_3_
  26.7 0.0 collective-permute-done.8.refs_1_
  26.7 3.1 %shard_map.91 = (bf16[512,1024]{1,0:T(8,128)(2,1)}, f32[1,2048]{1,0:T(1,128)S(1)}) custom-call(s32[2]{0:T(128)S(1)} %pad_add_fusion.where_ref, bf16[584,128]{1,0:T(8,128)(2,1)S(1)} %shard_map.90.refs_0_, bf16[584,128]{1,0:T(8,128)(2,1)S(1)} %collective-permute-done.8.refs_1_, bf16[584,128]{1,0:T(8,128)(2,1)S(1)} %collective-permute-done.9.refs_2_, ...), custom_call_target="tpu_custom_call" | custom-call | flops 20000000000 | bytes 6180872 | tf_op jit(solution)/shard_map/pallas_call | solution.py:27
  29.8 0.0 collective-permute-done.12.refs_1_
  29.8 0.0 collective-permute-done.13.refs_2_
  29.8 0.3 collective-permute-done.14.refs_3_
  30.1 1.3 %shard_map.93 = (f32[1,2048]{1,0:T(1,128)}, bf16[32,1024]{1,0:T(8,128)(2,1)}, bf16[1,32]{1,0:T(2,128)(2,1)}) custom-call(bf16[32,96]{1,0:T(8,128)(2,1)S(1)} %get-tuple-element.23.spread_ref, f32[1,2048]{1,0:T(1,128)S(1)} %get-tuple-element.29.w2_grad_ref, bf16[200,128]{1,0:T(8,128)(2,1)S(1)} %get-tuple-element.32.refs_0_, ...), custom_call_target="tpu_custom_call" | custom-call | bytes 292928 | tf_op jit(solution)/shard_map/pallas_call | solution.py:27
  (3 shorter events, 0.0 us)
Async XLA Ops:
  0.7 0.8 %copy-start.1 = (bf16[32,1024]{1,0:T(8,128)(2,1)S(1)}, bf16[32,1024]{1,0:T(8,128)(2,1)}, u32[]{:S(2)}) copy-start(bf16[32,1024]{1,0:T(8,128)(2,1)} %rows_ref.1) | copy-start | bytes 196612
  0.7 0.8 %copy-start.3 = (s32[32,1]{0,1:T(1,128)S(1)}, s32[32,1]{0,1:T(1,128)}, u32[]{:S(2)}) copy-start(s32[32,1]{0,1:T(1,128)} %param.6) | copy-start | bytes 388
  0.7 0.8 %copy-start.4 = (bf16[32]{0:T(256)(128)(2,1)S(1)}, bf16[32]{0:T(256)(128)(2,1)}, u32[]{:S(2)}) copy-start(bf16[32]{0:T(256)(128)(2,1)} %param.7) | copy-start | bytes 196
  1.7 7.8 %collective-permute-start.6 = (bf16[264,128]{1,0:T(8,128)(2,1)S(1)}, bf16[264,128]{1,0:T(8,128)(2,1)S(1)}, u32[]{:S(2)}, u32[]{:S(2)}) collective-permute-start(bf16[264,128]{1,0:T(8,128)(2,1)S(1)} %shard_map.85.refs_0_), channel_id=1, source_target_pairs={{0,3},{1,2},{2,1},{3,0},{4,7},{5,6},{6,5},{7,4},{8,11},{9,10},{10,... | collective-permute-start | bytes 202760 | tf_op jit(solution)/shard_map/ppermute | solution.py:39
  6.8 5.6 %collective-permute-start.5 = (bf16[264,128]{1,0:T(8,128)(2,1)S(1)}, bf16[264,128]{1,0:T(8,128)(2,1)S(1)}, u32[]{:S(2)}, u32[]{:S(2)}) collective-permute-start(bf16[264,128]{1,0:T(8,128)(2,1)S(1)} %shard_map.85.refs_0_), channel_id=1, source_target_pairs={{0,6},{1,7},{2,4},{3,5},{4,2},{5,3},{6,0},{7,1},{8,14},{9,15},{10,... | collective-permute-start | bytes 202760 | tf_op jit(solution)/shard_map/ppermute | solution.py:39
  6.8 5.6 %collective-permute-start.4 = (bf16[264,128]{1,0:T(8,128)(2,1)S(1)}, bf16[264,128]{1,0:T(8,128)(2,1)S(1)}, u32[]{:S(2)}, u32[]{:S(2)}) collective-permute-start(bf16[264,128]{1,0:T(8,128)(2,1)S(1)} %shard_map.85.refs_0_), channel_id=1, source_target_pairs={{0,1},{1,0},{2,3},{3,2},{4,5},{5,4},{6,7},{7,6},{8,9},{9,8},{10,11... | collective-permute-start | bytes 202760 | tf_op jit(solution)/shard_map/ppermute | solution.py:39
  6.9 5.7 %collective-permute-start.2 = (bf16[264,128]{1,0:T(8,128)(2,1)S(1)}, bf16[264,128]{1,0:T(8,128)(2,1)S(1)}, u32[]{:S(2)}, u32[]{:S(2)}) collective-permute-start(bf16[264,128]{1,0:T(8,128)(2,1)S(1)} %shard_map.85.refs_0_), channel_id=1, source_target_pairs={{0,28},{4,24},{8,20},{12,16},{16,12},{20,8},{24,4},{28,0},{1,29},{... | collective-permute-start | bytes 202760 | tf_op jit(solution)/shard_map/ppermute | solution.py:39
  9.4 4.3 %collective-permute-start.1 = (bf16[264,128]{1,0:T(8,128)(2,1)S(1)}, bf16[264,128]{1,0:T(8,128)(2,1)S(1)}, u32[]{:S(2)}, u32[]{:S(2)}) collective-permute-start(bf16[264,128]{1,0:T(8,128)(2,1)S(1)} %shard_map.85.refs_0_), channel_id=1, source_target_pairs={{0,20},{4,16},{8,28},{12,24},{16,4},{20,0},{24,12},{28,8},{1,21},{... | collective-permute-start | bytes 202760 | tf_op jit(solution)/shard_map/ppermute | solution.py:39
  9.5 4.6 %collective-permute-start = (bf16[264,128]{1,0:T(8,128)(2,1)S(1)}, bf16[264,128]{1,0:T(8,128)(2,1)S(1)}, u32[]{:S(2)}, u32[]{:S(2)}) collective-permute-start(bf16[264,128]{1,0:T(8,128)(2,1)S(1)} %shard_map.85.refs_0_), channel_id=1, source_target_pairs={{0,8},{4,12},{8,0},{12,4},{16,24},{20,28},{24,16},{28,20},{1,9},{5... | collective-permute-start | bytes 202760 | tf_op jit(solution)/shard_map/ppermute | solution.py:39
  12.4 1.8 %collective-permute-start.7 = (bf16[792,128]{1,0:T(8,128)(2,1)S(1)}, bf16[792,128]{1,0:T(8,128)(2,1)S(1)}, u32[]{:S(2)}, u32[]{:S(2)}) collective-permute-start(bf16[792,128]{1,0:T(8,128)(2,1)S(1)} %shard_map.87.far_ref), channel_id=1, source_target_pairs={{0,4},{4,0},{8,12},{12,8},{16,20},{20,16},{24,28},{28,24},{1,5},{5... | collective-permute-start | bytes 608264 | tf_op jit(solution)/shard_map/ppermute | solution.py:39
  14.1 4.5 %copy-start = (bf16[1,1024,2048]{2,1,0:T(8,128)(2,1)S(1)}, bf16[1,1024,2048]{2,1,0:T(8,128)(2,1)}, u32[]{:S(2)}) copy-start(bf16[1,1024,2048]{2,1,0:T(8,128)(2,1)} %param.8) | copy-start | bytes 12582916
  14.1 4.5 %copy-start.2 = (bf16[1,2048]{1,0:T(2,128)(2,1)S(1)}, bf16[1,2048]{1,0:T(2,128)(2,1)}, u32[]{:S(2)}) copy-start(bf16[1,2048]{1,0:T(2,128)(2,1)} %refs_6_.1) | copy-start | bytes 12292
  14.2 4.5 %collective-permute-start.3 = (bf16[1056,128]{1,0:T(8,128)(2,1)S(1)}, bf16[1056,128]{1,0:T(8,128)(2,1)S(1)}, u32[]{:S(2)}, u32[]{:S(2)}) collective-permute-start(bf16[1056,128]{1,0:T(8,128)(2,1)S(1)} %shard_map.86.near_ref), channel_id=1, source_target_pairs={{0,4},{4,0},{8,12},{12,8},{16,20},{20,16},{24,28},{28,24},{1,5},{5... | collective-permute-start | bytes 811016 | tf_op jit(solution)/shard_map/ppermute | solution.py:39
  15.4 10.3 %collective-permute-start.9 = (bf16[584,128]{1,0:T(8,128)(2,1)S(1)}, bf16[584,128]{1,0:T(8,128)(2,1)S(1)}, u32[]{:S(2)}, u32[]{:S(2)}) collective-permute-start(bf16[584,128]{1,0:T(8,128)(2,1)S(1)} %get-tuple-element.25), channel_id=1, source_target_pairs={{0,20},{4,16},{8,28},{12,24},{16,4},{20,0},{24,12},{28,8},{1,21},{... | collective-permute-start | bytes 448520 | tf_op jit(solution)/shard_map/ppermute | solution.py:39
  17.1 9.6 %collective-permute-start.10 = (bf16[584,128]{1,0:T(8,128)(2,1)S(1)}, bf16[584,128]{1,0:T(8,128)(2,1)S(1)}, u32[]{:S(2)}, u32[]{:S(2)}) collective-permute-start(bf16[584,128]{1,0:T(8,128)(2,1)S(1)} %get-tuple-element.26), channel_id=1, source_target_pairs={{0,28},{4,24},{8,20},{12,16},{16,12},{20,8},{24,4},{28,0},{1,29},{... | collective-permute-start | bytes 448520 | tf_op jit(solution)/shard_map/ppermute | solution.py:39
  17.8 8.9 %collective-permute-start.8 = (bf16[584,128]{1,0:T(8,128)(2,1)S(1)}, bf16[584,128]{1,0:T(8,128)(2,1)S(1)}, u32[]{:S(2)}, u32[]{:S(2)}) collective-permute-start(bf16[584,128]{1,0:T(8,128)(2,1)S(1)} %get-tuple-element.22.after_ref), channel_id=1, source_target_pairs={{0,8},{4,12},{8,0},{12,4},{16,24},{20,28},{24,16},{28,20},{1,9},{5... | collective-permute-start | bytes 448520 | tf_op jit(solution)/shard_map/ppermute | solution.py:39
  21.9 1.4 %collective-permute-start.11 = (bf16[48,1152]{1,0:T(8,128)(2,1)S(1)}, bf16[48,1152]{1,0:T(8,128)(2,1)S(1)}, u32[]{:S(2)}, u32[]{:S(2)}) collective-permute-start(bf16[48,1152]{1,0:T(8,128)(2,1)S(1)} %get-tuple-element.31), channel_id=1, source_target_pairs={{0,4},{4,0},{8,12},{12,8},{16,20},{20,16},{24,28},{28,24},{1,5},{5... | collective-permute-start | bytes 331784 | tf_op jit(solution)/shard_map/ppermute | solution.py:39
  23.4 6.5 %collective-permute-start.12 = (bf16[200,128]{1,0:T(8,128)(2,1)S(1)}, bf16[200,128]{1,0:T(8,128)(2,1)S(1)}, u32[]{:S(2)}, u32[]{:S(2)}) collective-permute-start(bf16[200,128]{1,0:T(8,128)(2,1)S(1)} %get-tuple-element.33), channel_id=1, source_target_pairs={{0,8},{4,12},{8,0},{12,4},{16,24},{20,28},{24,16},{28,20},{1,9},{5... | collective-permute-start | bytes 153608 | tf_op jit(solution)/shard_map/ppermute | solution.py:39
  24.6 5.2 %collective-permute-start.13 = (bf16[200,128]{1,0:T(8,128)(2,1)S(1)}, bf16[200,128]{1,0:T(8,128)(2,1)S(1)}, u32[]{:S(2)}, u32[]{:S(2)}) collective-permute-start(bf16[200,128]{1,0:T(8,128)(2,1)S(1)} %get-tuple-element.34), channel_id=1, source_target_pairs={{0,20},{4,16},{8,28},{12,24},{16,4},{20,0},{24,12},{28,8},{1,21},{... | collective-permute-start | bytes 153608 | tf_op jit(solution)/shard_map/ppermute | solution.py:39
  25.7 4.4 %collective-permute-start.14 = (bf16[200,128]{1,0:T(8,128)(2,1)S(1)}, bf16[200,128]{1,0:T(8,128)(2,1)S(1)}, u32[]{:S(2)}, u32[]{:S(2)}) collective-permute-start(bf16[200,128]{1,0:T(8,128)(2,1)S(1)} %get-tuple-element.35), channel_id=1, source_target_pairs={{0,28},{4,24},{8,20},{12,16},{16,12},{20,8},{24,4},{28,0},{1,29},{... | collective-permute-start | bytes 153608 | tf_op jit(solution)/shard_map/ppermute | solution.py:39
